TPU v7x, 32 devices: a whole 2x2x4 slice. The times are simulated.
32 devices in a mesh: group: 2 (over y), latent: 16 (over z, x, core).
Axes of the slice: x: 2, y: 2, z: 4, core: 2. Of those that a mesh axis runs over, the one named last changes fastest.
Arguments:
- activations: bfloat16 [16, 256, 7168], P('group', 'latent'), parts along dimension 0, may hold values from -6 to 6
- enc_weight: bfloat16 [32, 7168, 128], P(('group', 'latent')), parts along dimension 0, may hold values from -0.0625 to 0.0625
- enc_bias: float32 [32, 128], P(('group', 'latent')), parts along dimension 0, may hold values from -3 to 3
- dec_weight: bfloat16 [32, 128, 7168], P(('group', 'latent')), parts along dimension 0, may hold values from -0.5 to 0.5
- dec_bias: float32 [14336], P('group'), parts along dimension 0, may hold values from -3 to 3
- active: int32 [16, 3], P('group'), parts along dimension 0, may hold values from 0 to 15, all different within a row; in each aligned block of 8 rows (0 to 7, 8 to 15, ...) at most 2 rows name the same one
Outputs:
- enc_grad: float32 [32, 7168, 128], P(('group', 'latent')), parts along dimension 0
- enc_bias_grad: float32 [32, 128], P(('group', 'latent')), parts along dimension 0
- dec_grad: float32 [32, 128, 7168], P(('group', 'latent')), parts along dimension 0
- dec_bias_grad: float32 [14336], P('group'), parts along dimension 0
There are 2 independent parts, one for each index of `group`. A program takes and returns all parts, laid end to end along the dimension named above; each array names one. Nothing has to cross between parts.
Inputs may be any that keep to these rules, and one draw needn't show every extreme that they name: `active`: each row names 3 different blocks; no block is named by more than 2 rows, and some block by exactly 2.
All inputs are finite; a program needn't handle non-finite values.
Results may differ from a plain program's by a relative error of at most 0.0045.
Values may be sent and summed in bfloat16 or wider, within the bound.
No kernel may reach another device: no remote copies, remote signals or barrier semaphores. Data moves between devices by JAX's collectives and lax.ppermute only.
A program may use at most 128 MiB of HBM per device.

v0:
```python
import jax
import jax.numpy as jnp
from jax import lax
from jax.sharding import PartitionSpec as P

MOST = 2


penalty_weight = 0.1
grad_scale = 0.0625
epsilon = 1e-06


def owner_forward(received, markers, enc_weight, enc_bias, dec_weight):
    feature_width = received.shape[-1]
    row_count = received.shape[0] * received.shape[1] * received.shape[2]
    token_rows = received.reshape(row_count, feature_width)
    live_mask = markers.reshape(row_count, 1).astype(jnp.float32)
    preact = jnp.dot(token_rows, enc_weight[0], preferred_element_type=jnp.float32) + enc_bias[0]
    features = jnp.maximum(preact, 0.0) * live_mask
    contrib = jnp.dot(
        features.astype(jnp.bfloat16), dec_weight[0], preferred_element_type=jnp.float32
    ).astype(jnp.bfloat16)
    return (preact, contrib.reshape(received.shape))


def shards(activations, enc_weight, enc_bias, dec_weight, dec_bias, active):
    peer_count = lax.axis_size("latent")
    span_count, part_rows, feature_width = activations.shape
    half_width = feature_width // 2
    blocks = jnp.arange(peer_count, dtype=jnp.int32)
    member = jnp.any(active[:, :, None] == blocks[None, None, :], axis=1).astype(jnp.int32)
    position = jnp.cumsum(member, axis=0) - member
    slot_index = jnp.arange(MOST, dtype=jnp.int32)
    chosen = member[:, :, None] * (position[:, :, None] == slot_index[None, None, :]).astype(
        jnp.int32
    )
    selector = chosen.reshape(span_count, peer_count * MOST).T.astype(jnp.bfloat16)
    flat_rows = activations.reshape(span_count, part_rows * feature_width)
    outgoing = jnp.dot(selector, flat_rows, preferred_element_type=jnp.float32).astype(jnp.bfloat16)
    outgoing = outgoing.reshape(peer_count, MOST, part_rows, feature_width)
    markers = jnp.broadcast_to(
        jnp.sum(chosen, axis=0).astype(jnp.bfloat16)[:, :, None], (peer_count, MOST, part_rows)
    )
    received, markers_in = (
        lax.all_to_all(outgoing, "latent", split_axis=0, concat_axis=0, tiled=True),
        lax.all_to_all(markers, "latent", split_axis=0, concat_axis=0, tiled=True),
    )
    preact, contrib = owner_forward(received, markers_in, enc_weight, enc_bias, dec_weight)
    returned = lax.all_to_all(contrib, "latent", split_axis=0, concat_axis=0, tiled=True)
    arrived = returned.reshape(peer_count * MOST, part_rows * feature_width)
    summed = jnp.dot(selector.T, arrived, preferred_element_type=jnp.float32)
    residue = (
        summed.reshape(span_count, part_rows, feature_width)
        + dec_bias
        - activations.astype(jnp.float32)
    )
    scaled = residue * grad_scale
    deltas = scaled.astype(jnp.bfloat16)
    bias_part = jnp.sum(scaled, axis=(0, 1))
    delta_out = jnp.dot(
        selector,
        deltas.reshape(span_count, part_rows * feature_width),
        preferred_element_type=jnp.float32,
    ).astype(jnp.bfloat16)
    delta_out = delta_out.reshape(peer_count, MOST, part_rows, feature_width)
    delta_rows = lax.all_to_all(
        delta_out, "latent", split_axis=0, concat_axis=0, tiled=True
    ).reshape(-1, feature_width)
    dec_bias_grad = lax.psum(bias_part, "latent")
    token_rows = received.reshape(-1, feature_width)
    live_mask = markers_in.reshape(-1, 1).astype(jnp.float32)
    features = jnp.maximum(preact, 0.0) * live_mask
    weights = dec_weight[0].astype(jnp.float32)
    base_part = weights[:, :half_width]
    chat_part = weights[:, half_width:]
    base_norm = jnp.sqrt(jnp.sum(base_part * base_part, axis=1) + epsilon)
    chat_norm = jnp.sqrt(jnp.sum(chat_part * chat_part, axis=1) + epsilon)
    directions = jnp.concatenate(
        [base_part / base_norm[:, None], chat_part / chat_norm[:, None]], axis=1
    )
    feature_sum = jnp.sum(features, axis=0)
    dec_grad = (
        jnp.dot(features.astype(jnp.bfloat16).T, delta_rows, preferred_element_type=jnp.float32)
        + penalty_weight * feature_sum[:, None] * directions
    )
    feature_grad = jnp.dot(
        delta_rows, dec_weight[0].T, preferred_element_type=jnp.float32
    ) + penalty_weight * (base_norm + chat_norm)
    preact_grad = jnp.where(preact > 0.0, feature_grad, 0.0) * live_mask
    enc_grad = jnp.dot(
        token_rows.T, preact_grad.astype(jnp.bfloat16), preferred_element_type=jnp.float32
    )
    bias_grad = jnp.sum(preact_grad, axis=0)
    return (enc_grad[None], bias_grad[None], dec_grad[None], dec_bias_grad)


def solution(mesh):
    in_specs = (
        P("group", "latent", None),
        P(("group", "latent"), None, None),
        P(("group", "latent"), None),
        P(("group", "latent"), None, None),
        P("group"),
        P("group", None),
    )
    out_specs = (
        P(("group", "latent"), None, None),
        P(("group", "latent"), None),
        P(("group", "latent"), None, None),
        P("group"),
    )
    return jax.shard_map(shards, mesh=mesh, in_specs=in_specs, out_specs=out_specs, check_vma=False)
```

profile of v0, /device:TPU:15, one launch (start us, length us, event | category | flops | bytes accessed | tf_op | source)
XLA Modules:
  0.0 613.7 jit_solution(7950548419580658526)
XLA Ops:
  0.6 0.0 copy-start
  0.6 0.9 fusion.26
  1.5 0.1 copy.17
  1.7 0.1 copy.16
  1.7 0.3 fusion.25
  2.1 0.7 broadcast_in_dim.9
  2.8 6.6 %all-to-all-start.1 = ((bf16[16,2,16]{2,1,0:T(2,128)(2,1)}), bf16[16,2,16]{2,1,0:T(2,128)(2,1)S(1)}, u32[]{:S(2)}, u32[]{:S(2)}) async-start(bf16[16,2,16]{2,1,0:T(2,128)(2,1)} %broadcast_in_dim.9), calls=%async_computation.1 | async-start | bytes 16384 | tf_op jit(solution)/shard_map/all_to_all | solution.py:47
  9.3 0.1 eq.43
  9.4 2.5 copy.24
  12.0 0.1 select_convert_fusion
  12.0 2.0 convolution_convert_fusion.1
  14.1 7.0 %copy.25 = bf16[4,8,16,7168]{3,2,1,0:T(8,128)(2,1)} copy(bf16[4,8,16,7168]{3,1,2,0:T(8,128)(2,1)S(1)} %bitcast.72) | data formatting | bytes 14680064
  21.1 0.0 all-to-all-done.1
  21.1 0.0 copy-start.8
  21.1 17.5 %all-to-all-start = ((bf16[16,2,16,7168]{3,2,1,0:T(8,128)(2,1)}), bf16[16,2,16,7168]{3,2,1,0:T(8,128)(2,1)}, u32[]{:S(2)}, u32[]{:S(2)}) async-start(bf16[16,2,16,7168]{3,2,1,0:T(8,128)(2,1)} %bitcast.70), calls=%async_computation | async-start | bytes 14680064 | tf_op jit(solution)/shard_map/all_to_all | solution.py:46
  38.6 0.1 reshape.99
  38.7 159.7 %all-to-all-done = bf16[16,2,16,7168]{3,2,1,0:T(8,128)(2,1)} async-done(((bf16[16,2,16,7168]{3,2,1,0:T(8,128)(2,1)}), bf16[16,2,16,7168]{3,2,1,0:T(8,128)(2,1)}, u32[]{:S(2)}, u32[]{:S(2)}) %all-to-all-start) | async-done | bytes 7340064 | tf_op jit(solution)/shard_map/all_to_all | solution.py:46
  198.4 0.0 copy-done
  198.4 0.0 copy-done.8
  198.4 0.0 copy-start.2
  198.4 5.3 fusion.22
  203.7 0.0 copy-done.2
  203.7 2.1 convolution_convert_fusion.2
  205.8 0.0 copy-start.6
  205.8 0.0 copy-start.7
  205.8 164.5 %all_to_all.20 = bf16[16,2,16,7168]{3,2,1,0:T(8,128)(2,1)S(1)} all-to-all(bf16[16,2,16,7168]{3,2,1,0:T(8,128)(2,1)S(1)} %bitcast.73), channel_id=1, replica_groups=mesh['group'=2,'latent'=16] {'latent'}, dimensions={0} | all-to-all | bytes 14680064 | tf_op jit(solution)/shard_map/all_to_all | solution.py:50
  370.3 0.0 copy-done.6
  370.3 0.0 copy-done.7
  370.3 10.2 %fusion.30 = (f32[7168]{0:T(1024)S(1)}, bf16[8,16,7168]{2,0,1:T(8,128)(2,1)S(1)}) fusion(bf16[8,16,7168]{2,1,0:T(8,128)(2,1)S(1)} %copy-done.6, f32[7168]{0:T(1024)S(1)} %copy-done.7, bf16[8,32]{0,1:T(8,128)(2,1)S(1)} %select_convert_fusion, bf16[4,8,16,7168]{3,2,1,0:T(8,128)(2,1)S(1)} %bitcast.74), kind=kOutput, calls=%fused_computation.41 | convolution fusion | flops 64218112 | bytes 11067904 | tf_op jit(solution)/shard_map/dot_general | solution.py:52
  380.5 2.2 convolution_convert_fusion
  382.7 7.0 %copy.27 = bf16[4,8,16,7168]{3,2,1,0:T(8,128)(2,1)} copy(bf16[4,8,16,7168]{3,1,2,0:T(8,128)(2,1)S(1)} %bitcast.71) | data formatting | bytes 14680064
  389.7 0.0 copy-start.3
  389.7 5.8 all-to-all-start.3
  395.4 0.0 copy-done.3
  395.5 0.4 bitcast_convert_fusion
  395.8 0.3 multiply_reduce_fusion
  396.2 2.3 slice_divide_fusion.1
  398.5 194.8 %psum.7 = f32[7168]{0:T(1024)} all-reduce(f32[7168]{0:T(1024)S(1)} %get-tuple-element.6), channel_id=1, replica_groups=mesh['group'=2,'latent'=16] {'latent'}, use_global_device_ids=true, to_apply=%region_8.9 | all-reduce | flops 7168 | bytes 57344 | tf_op jit(solution)/shard_map/psum | solution.py:70
  593.3 0.0 all-to-all-done.3
  593.3 5.7 fusion.31
  599.0 0.0 copy-start.4
  599.0 0.0 copy-start.5
  599.0 7.2 %convolution_bitcast_fusion = f32[1,7168,128]{2,1,0:T(8,128)} fusion(bf16[512,7168]{1,0:T(8,128)(2,1)} %bitcast.2, bf16[512,128]{1,0:T(8,128)(2,1)S(1)} %get-tuple-element.15), kind=kOutput, calls=%fused_computation.5 | convolution fusion | flops 939524096 | bytes 11141120 | tf_op jit(solution)/shard_map/dot_general | solution.py:91
  606.2 0.0 copy-done.4
  606.2 0.0 copy-done.5
  606.2 0.0 copy-start.1
  606.2 7.0 %fusion = f32[1,128,7168]{2,1,0:T(8,128)} fusion(bf16[512,7168]{1,0:T(8,128)(2,1)} %bitcast.10, f32[128,3584]{1,0:T(8,128)S(1)} %copy-done.5, f32[128,3584]{1,0:T(8,128)S(1)} %copy-done.4, f32[128]{0:T(128)S(1)} %broadcast_multiply_fusion, f32[512,128]{1,0:T(8,128)S(1)} %get-tuple-element.17, f32[512]{0:T(512)S(1)} %reshape.99), kind=kOutput, calls=%fused_computation.4 | convolution fusion | flops 942473216 | bytes 14944768 | tf_op jit(solution)/shard_map/dot_general | solution.py:84
  613.2 0.0 copy-done.1
  (9 shorter events, 0.1 us)
Async XLA Ops:
  0.6 197.7 %copy-start = (bf16[1,7168,128]{2,1,0:T(8,128)(2,1)S(1)}, bf16[1,7168,128]{2,1,0:T(8,128)(2,1)}, u32[]{:S(2)}) copy-start(bf16[1,7168,128]{2,1,0:T(8,128)(2,1)} %param.7) | copy-start | bytes 5505028
  2.8 18.4 %all-to-all-start.1 = ((bf16[16,2,16]{2,1,0:T(2,128)(2,1)}), bf16[16,2,16]{2,1,0:T(2,128)(2,1)S(1)}, u32[]{:S(2)}, u32[]{:S(2)}) async-start(bf16[16,2,16]{2,1,0:T(2,128)(2,1)} %broadcast_in_dim.9), calls=%async_computation.1 | async-start | bytes 16384 | tf_op jit(solution)/shard_map/all_to_all | solution.py:47
  21.1 177.2 %copy-start.8 = (f32[1,128]{1,0:T(1,128)S(1)}, f32[1,128]{1,0:T(1,128)}, u32[]{:S(2)}) copy-start(f32[1,128]{1,0:T(1,128)} %param.8) | copy-start | bytes 1540
  21.1 177.2 %all-to-all-start = ((bf16[16,2,16,7168]{3,2,1,0:T(8,128)(2,1)}), bf16[16,2,16,7168]{3,2,1,0:T(8,128)(2,1)}, u32[]{:S(2)}, u32[]{:S(2)}) async-start(bf16[16,2,16,7168]{3,2,1,0:T(8,128)(2,1)} %bitcast.70), calls=%async_computation | async-start | bytes 14680064 | tf_op jit(solution)/shard_map/all_to_all | solution.py:46
  198.4 5.3 copy-start.2
  205.8 164.5 %copy-start.6 = (bf16[8,16,7168]{2,1,0:T(8,128)(2,1)S(1)}, bf16[8,16,7168]{2,1,0:T(8,128)(2,1)}, u32[]{:S(2)}) copy-start(bf16[8,16,7168]{2,1,0:T(8,128)(2,1)} %param.6) | copy-start | bytes 5505028
  205.8 164.5 %copy-start.7 = (f32[7168]{0:T(1024)S(1)}, f32[7168]{0:T(1024)}, u32[]{:S(2)}) copy-start(f32[7168]{0:T(1024)} %param.10) | copy-start | bytes 86020
  389.7 5.8 copy-start.3
  389.7 203.6 %all-to-all-start.3 = ((bf16[16,2,16,7168]{3,2,1,0:T(8,128)(2,1)}), bf16[16,2,16,7168]{3,2,1,0:T(8,128)(2,1)}, u32[]{:S(2)}, u32[]{:S(2)}) async-start(bf16[16,2,16,7168]{3,2,1,0:T(8,128)(2,1)} %bitcast.69), calls=%async_computation.3 | async-start | bytes 14680064 | tf_op jit(solution)/shard_map/all_to_all | solution.py:67
  599.0 7.2 %copy-start.4 = (f32[128,3584]{1,0:T(8,128)S(1)}, f32[128,3584]{1,0:T(8,128)}, u32[]{:S(2)}) copy-start(f32[128,3584]{1,0:T(8,128)} %get-tuple-element.8) | copy-start | bytes 5505028
  599.0 7.2 %copy-start.5 = (f32[128,3584]{1,0:T(8,128)S(1)}, f32[128,3584]{1,0:T(8,128)}, u32[]{:S(2)}) copy-start(f32[128,3584]{1,0:T(8,128)} %get-tuple-element.9) | copy-start | bytes 5505028
  606.2 7.0 %copy-start.1 = (bf16[1,7168,128]{2,1,0:T(8,128)(2,1)S(1)}, bf16[1,7168,128]{2,1,0:T(8,128)(2,1)}, u32[]{:S(2)}) copy-start(bf16[1,7168,128]{2,1,0:T(8,128)(2,1)} %param.7) | copy-start | bytes 5505028
where the time goes:
time: 617 us; the launch traced here: 614 us
  blocking collectives  359 us (58%)
  waiting for transfers between devices  160 us (26%)
  matrix products  41.8 us (7%)
  starting transfers between devices  29.8 us (5%)
  local copies, waits for them, and re-layouts  17.6 us (3%)
    psum x1, blocking collectives, shards(): dec_bias_grad = lax.psum(bias_part, 'latent')  195 us
    all_to_all x1, blocking collectives, shards(): lax.all_to_all(contrib, 'latent', split_axis=0, concat_axis=0, tiled=True)  164 us
    all_to_all x1, waiting for transfers between devices, shards(): lax.all_to_all(outgoing, 'latent', split_axis=0, concat_axis=0, tiled=True)  160 us
    all_to_all x1, starting transfers between devices, shards(): lax.all_to_all(outgoing, 'latent', split_axis=0, concat_axis=0, tiled=True)  17.5 us
    unnamed x21, local copies, waits for them, and re-layouts  16.6 us
  transfers between devices with their start and end apart: 3, of which 1 were waited for; matrix products, arithmetic and copies ran while one was open for 2% of the time, Pallas kernels for 0%

commit v1 on v0

v1 whole, which is shorter than its diff:
```python
import functools

import jax
import jax.numpy as jnp
from jax import lax
from jax.experimental import pallas as pl
from jax.experimental.pallas import tpu as pltpu
from jax.sharding import PartitionSpec as P

MOST = 2
AXIS = "latent"

penalty_weight = 0.1
grad_scale = 0.0625
epsilon = 1e-06

f32 = jnp.float32
bf16 = jnp.bfloat16


def swap(x, distance, count):
    return lax.ppermute(x, AXIS, [(i, i ^ distance) for i in range(count)])


def exchange(x, groups=None):
    return lax.all_to_all(
        x, AXIS, split_axis=0, concat_axis=0, tiled=True, axis_index_groups=groups
    )


def slot_tables(active, count):
    blocks = jnp.arange(count, dtype=jnp.int32)
    member = jnp.any(active[:, :, None] == blocks[None, None, :], axis=1).astype(jnp.int32)
    position = jnp.cumsum(member, axis=0) - member
    slots = jnp.arange(MOST, dtype=jnp.int32)
    chosen = member[:, :, None] * (position[:, :, None] == slots).astype(jnp.int32)
    spans = jnp.arange(active.shape[0], dtype=jnp.int32)
    span_of = jnp.sum(chosen * spans[:, None, None], axis=0)
    live = jnp.sum(chosen, axis=0)
    named = active[:, :, None] == blocks[None, None, :]
    slot_of = jnp.sum(jnp.where(named, position[:, None, :], 0), axis=2)
    return span_of, live, slot_of


def copy_block(index_ref, source_ref, out_ref):
    out_ref[...] = source_ref[...]


def pick_spans(rows, index):
    span_count, part_rows, width = rows.shape
    picked = index.shape[0]
    return pl.pallas_call(
        copy_block,
        grid_spec=pltpu.PrefetchScalarGridSpec(
            num_scalar_prefetch=1,
            grid=(picked,),
            in_specs=[pl.BlockSpec((1, part_rows, width), lambda i, at: (at[i], 0, 0))],
            out_specs=pl.BlockSpec((1, part_rows, width), lambda i, at: (i, 0, 0)),
        ),
        out_shape=jax.ShapeDtypeStruct((picked, part_rows, width), rows.dtype),
        name="pick_spans",
    )(index, rows)


def decode_kernel(names, skipped, place_ref, block_ref, core_ref, feat_ref, dec_ref, r_ref, y_ref, total):
    span_count = place_ref.shape[0] // names
    width = dec_ref.shape[-1]
    r_ref[...] = jnp.zeros_like(r_ref)
    total[...] = jnp.zeros_like(total)

    def span_step(span, carry):
        feats, decs, recon = [], [], None
        for name in range(names):
            feat = feat_ref[place_ref[span * names + name]]
            dec = dec_ref[block_ref[span * names + name]]
            contrib = jnp.dot(feat, dec, preferred_element_type=f32).astype(bf16).astype(f32)
            recon = contrib if recon is None else recon + contrib
            feats.append(feat)
            decs.append(dec)
        scaled = recon * grad_scale
        if skipped:
            lane = lax.broadcasted_iota(jnp.int32, scaled.shape, 1)
            scaled = jnp.where(lane >= core_ref[0] * skipped, scaled, 0.0)
        delta = scaled.astype(bf16)
        for name in range(names):
            part = lax.dot_general(
                delta, decs[name], (((1,), (1,)), ((), ())), preferred_element_type=f32
            )
            r_ref[place_ref[span * names + name]] = part.astype(bf16)
            grad = lax.dot_general(
                feats[name], delta, (((0,), (0,)), ((), ())), preferred_element_type=f32
            )
            total[block_ref[span * names + name]] += grad
        return carry

    lax.fori_loop(0, span_count, span_step, 0)
    y_ref[...] = total[...].astype(bf16)


def decode(names, skipped, place, block, core, feats, dec):
    vmem = pl.BlockSpec(memory_space=pltpu.VMEM)
    smem = pl.BlockSpec(memory_space=pltpu.SMEM)
    pairs, rows, latents, columns = place.shape[0], feats.shape[1], feats.shape[2], dec.shape[2]
    return pl.pallas_call(
        functools.partial(decode_kernel, names, skipped),
        in_specs=[smem, smem, smem, vmem, vmem],
        out_specs=[vmem, vmem],
        out_shape=[
            jax.ShapeDtypeStruct(feats.shape, bf16),
            jax.ShapeDtypeStruct(dec.shape, bf16),
        ],
        scratch_shapes=[pltpu.VMEM(dec.shape, f32)],
        compiler_params=pltpu.CompilerParams(vmem_limit_bytes=56 * 2**20),
        cost_estimate=pl.CostEstimate(
            flops=6 * pairs * rows * latents * columns,
            bytes_accessed=4 * (feats.size + dec.size),
            transcendentals=0,
        ),
        name="decode",
    )(place, block, core, feats, dec)


def decode_plain(names, skipped, place, block, core, feats, dec):
    span_count = place.shape[0] // names
    r_out = jnp.zeros(feats.shape, bf16)
    total = jnp.zeros(dec.shape, f32)
    width = dec.shape[-1]
    keep = (jnp.arange(width) >= core[0] * skipped).astype(f32)

    def span_step(span, carry):
        r_out, total = carry
        at = lax.dynamic_slice(place, (span * names,), (names,))
        which = lax.dynamic_slice(block, (span * names,), (names,))
        feat, mine = feats[at], dec[which]
        contrib = jnp.einsum("krl,klc->krc", feat, mine, preferred_element_type=f32).astype(bf16)
        recon = jnp.sum(contrib.astype(f32), axis=0)
        delta = (recon * grad_scale * keep).astype(bf16)
        part = jnp.einsum("rc,klc->krl", delta, mine, preferred_element_type=f32)
        grad = jnp.einsum("krl,rc->klc", feat, delta, preferred_element_type=f32)
        return r_out.at[at].set(part.astype(bf16)), total.at[which].add(grad)

    r_out, total = lax.fori_loop(0, span_count, span_step, (r_out, total))
    return r_out, total.astype(bf16)


def shards(activations, enc_weight, enc_bias, dec_weight, dec_bias, active):
    count = lax.axis_size(AXIS)
    me = lax.axis_index(AXIS)
    span_count, part_rows, width = activations.shape
    names = active.shape[1]
    latents = enc_weight.shape[-1]
    stream = width // 2
    half, chips = count // 2, count // 2
    halves = [[h * half + i for i in range(half)] for h in range(2)]
    same_core = [[2 * i + c for i in range(chips)] for c in range(2)]
    my_half, core = me // half, me % 2
    enc, dec = enc_weight[0], dec_weight[0]
    span_of, live, slot_of = slot_tables(active, count)

    mine = lax.dynamic_slice(span_of, (my_half * half, 0), (half, MOST)).reshape(-1)
    far = [swap(activations[:, :, i * stream : (i + 1) * stream], half, count) for i in range(2)]
    shape = (half, MOST, part_rows)
    x_own = exchange(pick_spans(activations, mine).reshape(shape + (width,)), halves)
    x_far = [exchange(pick_spans(a, mine).reshape(shape + (stream,)), halves) for a in far]

    per_chip = width // chips
    if per_chip % 128 == 0:
        window = -(-(per_chip // 2) // 128) * 128
    else:
        window = per_chip // 2
    skipped = 2 * window - per_chip
    starts = [(i // 2) * per_chip + (i % 2) * (per_chip - window) for i in range(count)]
    dec_all = exchange(jnp.stack([dec[:, s : s + window] for s in starts]))

    rows = half * MOST * part_rows
    own = x_own.reshape(rows, width)
    far = [x.reshape(rows, stream) for x in x_far]
    dot = functools.partial(jnp.dot, preferred_element_type=f32)
    preact_own = dot(own, enc) + enc_bias[0]
    preact_far = dot(far[0], enc[:stream]) + dot(far[1], enc[stream:]) + enc_bias[0]
    my_live = lax.dynamic_slice(live, (me, 0), (1, MOST)).astype(f32)
    mask = jnp.broadcast_to(my_live[0][None, :, None, None], shape + (1,)).reshape(rows, 1)
    feat_own = jnp.maximum(preact_own, 0.0) * mask
    feat_far = jnp.maximum(preact_far, 0.0) * mask
    fb_own, fb_far = feat_own.astype(bf16), feat_far.astype(bf16)

    def by_slot(x):
        return x.reshape(half, MOST, part_rows, latents).transpose(1, 0, 2, 3).reshape(MOST, -1, latents)

    def by_source(x):
        return x.reshape(MOST, half, part_rows, latents).transpose(1, 0, 2, 3).reshape(rows, latents)

    lower = my_half == 0
    a, b = by_slot(fb_own), by_slot(fb_far)
    feats = jnp.concatenate([jnp.where(lower, a, b), jnp.where(lower, b, a)], axis=1)

    span_rows = feats.shape[1]
    same = exchange(jnp.broadcast_to(feats[None], (chips,) + feats.shape), same_core)
    other = swap(same, 1, count)
    feats_all = jnp.concatenate([same, other]).reshape(count * MOST, span_rows, latents)
    place = (((active % 2) ^ core) * chips + active // 2) * MOST + slot_of

    small = feats_all.size * 4 + dec_all.size * 8 < 40 * 2**20
    r_out, y_out = (decode if small else decode_plain)(
        names, skipped, place.reshape(-1), active.reshape(-1), core.reshape(1), feats_all, dec_all
    )
    r_out = r_out.reshape(2, chips, MOST, span_rows, latents)
    r_near = swap(r_out[1], 1, count)
    r_sum = (r_out[0].astype(f32) + r_near.astype(f32)).astype(bf16)
    r_in = exchange(r_sum, same_core)
    y_in = exchange(y_out)
    recon_part = jnp.sum(r_in.astype(f32), axis=0)

    weights = dec.astype(f32)
    base_norm = jnp.sqrt(jnp.sum(weights[:, :stream] * weights[:, :stream], axis=1) + epsilon)
    chat_norm = jnp.sqrt(jnp.sum(weights[:, stream:] * weights[:, stream:], axis=1) + epsilon)
    bias_dec = jnp.sum(weights * dec_bias[None, :], axis=1)
    constant = grad_scale * bias_dec + penalty_weight * (base_norm + chat_norm)
    cross = functools.partial(
        lax.dot_general, dimension_numbers=(((1,), (1,)), ((), ())), preferred_element_type=f32
    )
    xd_own = cross(own, dec)
    xd_far = cross(far[0], dec[:, :stream]) + cross(far[1], dec[:, stream:])
    down = functools.partial(
        lax.dot_general, dimension_numbers=(((0,), (0,)), ((), ())), preferred_element_type=f32
    )
    fx = down(fb_own, own) + jnp.concatenate([down(fb_far, x) for x in far], axis=1)
    feature_sum = jnp.sum(feat_own, axis=0) + jnp.sum(feat_far, axis=0)
    rounded_sum = jnp.sum(fb_own.astype(f32), axis=0) + jnp.sum(fb_far.astype(f32), axis=0)
    inverse = jnp.concatenate(
        [
            jnp.broadcast_to(1.0 / base_norm[:, None], (latents, stream)),
            jnp.broadcast_to(1.0 / chat_norm[:, None], (latents, stream)),
        ],
        axis=1,
    )
    dec_part = (
        grad_scale * (rounded_sum[:, None] * dec_bias[None, :] - fx)
        + penalty_weight * feature_sum[:, None] * weights * inverse
    )

    act_sum = jnp.sum(activations.astype(f32), axis=(0, 1))
    bias_part = jnp.sum(rounded_sum[:, None] * weights, axis=0) - act_sum
    bias_cols = jnp.sum(exchange(bias_part.reshape(count, width // count)), axis=0)
    bias_all = exchange(jnp.broadcast_to(bias_cols[None], (count, width // count))).reshape(-1)
    dec_bias_grad = grad_scale * (bias_all + float(span_count * part_rows * count) * dec_bias)

    first, second = recon_part[:, : span_rows // 2], recon_part[:, span_rows // 2 :]
    r_own = by_source(jnp.where(lower, first, second))
    r_far = by_source(jnp.where(lower, second, first))
    grad_own = jnp.where((preact_own > 0.0) & (mask > 0.0), r_own - grad_scale * xd_own + constant, 0.0)
    grad_far = jnp.where((preact_far > 0.0) & (mask > 0.0), r_far - grad_scale * xd_far + constant, 0.0)
    bias_grad = jnp.sum(grad_own, axis=0) + jnp.sum(grad_far, axis=0)
    gb_own, gb_far = grad_own.astype(bf16), grad_far.astype(bf16)
    enc_grad = down(own, gb_own) + jnp.concatenate([down(x, gb_far) for x in far], axis=0)

    y_cols = jnp.concatenate(
        [y_in[i] if i % 2 == 0 else y_in[i][:, skipped:] for i in range(count)], axis=1
    )
    dec_grad = dec_part + y_cols.astype(f32)
    return (enc_grad[None], bias_grad[None], dec_grad[None], dec_bias_grad)


def solution(mesh):
    in_specs = (
        P("group", "latent", None),
        P(("group", "latent"), None, None),
        P(("group", "latent"), None),
        P(("group", "latent"), None, None),
        P("group"),
        P("group", None),
    )
    out_specs = (
        P(("group", "latent"), None, None),
        P(("group", "latent"), None),
        P(("group", "latent"), None, None),
        P("group"),
    )
    return jax.shard_map(shards, mesh=mesh, in_specs=in_specs, out_specs=out_specs, check_vma=False)
```

time: 617 us -> 413 us (0.67)
  blocking collectives: 359 us -> 0 us
  waiting for transfers between devices: 160 us -> 234 us
  Pallas kernels: 0 us -> 41.4 us
  starting transfers between devices: 29.8 us -> 57.6 us
  local copies, waits for them, and re-layouts: 17.6 us -> 34.2 us
  matrix products: 41.8 us -> 33.8 us
    psum x1 -> x0, blocking collectives: 195 us -> none  [shards(): dec_bias_grad = lax.psum(bias_part, 'latent')]
    all_to_all x1 -> x0, blocking collectives: 164 us -> none  [shards(): lax.all_to_all(contrib, 'latent', split_axis=0, concat_axis=0, tiled=True)]
    ppermute x0 -> x4, waiting for transfers between devices: none -> 99.5 us  [swap(): return lax.ppermute(x, AXIS, [(i, i ^ distance) for i in range(count)])]
    pallas_call x0 -> x4, Pallas kernels: none -> 41.4 us  [the longest x3 30.6 us: pick_spans(): pl.pallas_call(copy_block, grid_spec=pltpu.PrefetchScalarGridSpec(num_sca...]
    all_to_all x3 -> x9, waiting for transfers between devices: 160 us -> 134 us  [exchange(): lax.all_to_all(x, AXIS, split_axis=0, concat_axis=0, tiled=True, axis_ind...]
    all_to_all x3 -> x9, starting transfers between devices: 29.8 us -> 52.2 us  [exchange(): lax.all_to_all(x, AXIS, split_axis=0, concat_axis=0, tiled=True, axis_ind...]
    dot_general x8 -> x12, matrix products: 41.8 us -> 33.8 us  [the longest x1 5.77 us: shards(): down(fb_own, own) + jnp.concatenate([down(fb_far, x) for x in far], axis=1)]
    unnamed x21 -> x59, local copies, waits for them, and re-layouts: 16.6 us -> 22.6 us
  transfers between devices with their start and end apart: 3 -> 13, of which waited for: 1 -> 11; matrix products, arithmetic and copies ran while one was open for 2% -> 12% of each run, Pallas kernels for 0% -> 5%
where the time goes in v1:
time: 413 us; the launch traced here: 411 us
  waiting for transfers between devices  234 us (57%)
  starting transfers between devices  57.6 us (14%)
  Pallas kernels  41.4 us (10%)
  local copies, waits for them, and re-layouts  34.2 us (8%)
  matrix products  33.8 us (8%)
  other arithmetic  9.19 us (2%)
    all_to_all x9, waiting for transfers between devices, exchange(): lax.all_to_all(x, AXIS, split_axis=0, concat_axis=0, tiled=True, axis_ind...  134 us
    ppermute x4, waiting for transfers between devices, swap(): return lax.ppermute(x, AXIS, [(i, i ^ distance) for i in range(count)])  99.5 us
    all_to_all x9, starting transfers between devices, exchange(): lax.all_to_all(x, AXIS, split_axis=0, concat_axis=0, tiled=True, axis_ind...  52.2 us
    pallas_call x3, Pallas kernels, pick_spans(): pl.pallas_call(copy_block, grid_spec=pltpu.PrefetchScalarGridSpec(num_sca...  30.6 us
    unnamed x59, local copies, waits for them, and re-layouts  22.6 us
    pallas_call x1, Pallas kernels, decode(): pl.pallas_call(functools.partial(decode_kernel, names, skipped), in_specs...  10.9 us
  transfers between devices with their start and end apart: 13, of which 11 were waited for; matrix products, arithmetic and copies ran while one was open for 12% of the time, Pallas kernels for 5%

profile of v1, /device:TPU:15, one launch (start us, length us, event | category | flops | bytes accessed | tf_op | source)
XLA Modules:
  0.0 410.9 jit_solution(1922217929921694767)
XLA Ops:
  0.6 1.6 fusion.76
  2.2 2.4 collective-permute-start.1
  5.5 38.7 %collective-permute-done.1.source_ref = bf16[8,16,3584]{2,1,0:T(8,128)(2,1)S(1)} collective-permute-done((bf16[8,16,3584]{2,1,0:T(8,128)(2,1)S(1)}, bf16[8,16,3584]{2,1,0:T(8,128)(2,1)S(1)}, u32[]{:S(2)}, u32[]{:S(2)}) %collective-permute-start.1) | collective-permute-done | bytes 917536 | tf_op jit(solution)/shard_map/ppermute | solution.py:22
  44.2 0.9 copy-done.9
  45.1 9.9 %pick_spans.5 = bf16[16,16,3584]{2,1,0:T(8,128)(2,1)} custom-call(s32[16]{0:T(128)} %reshape.189.index_ref, bf16[8,16,3584]{2,1,0:T(8,128)(2,1)} %copy-done.9), custom_call_target="tpu_custom_call" | custom-call | tf_op jit(solution)/shard_map/pick_spans/pallas_call | solution.py:52
  55.1 5.0 %all-to-all-start.2 = ((bf16[8,2,16,3584]{3,2,1,0:T(8,128)(2,1)}), bf16[8,2,16,3584]{3,2,1,0:T(8,128)(2,1)S(1)}, u32[]{:S(2)}, u32[]{:S(2)}) async-start(bf16[8,2,16,3584]{3,2,1,0:T(8,128)(2,1)} %bitcast.210), calls=%async_computation.2 | async-start | bytes 3670016 | tf_op jit(solution)/shard_map/all_to_all | solution.py:26
  60.1 10.7 %pick_spans.3 = bf16[16,16,7168]{2,1,0:T(8,128)(2,1)} custom-call(s32[16]{0:T(128)} %reshape.189.index_ref, bf16[8,16,7168]{2,1,0:T(8,128)(2,1)} %source_ref.1), custom_call_target="tpu_custom_call" | custom-call | tf_op jit(solution)/shard_map/pick_spans/pallas_call | solution.py:52
  70.8 10.2 %all-to-all-done.2 = bf16[8,2,16,3584]{3,2,1,0:T(8,128)(2,1)S(1)} async-done(((bf16[8,2,16,3584]{3,2,1,0:T(8,128)(2,1)}), bf16[8,2,16,3584]{3,2,1,0:T(8,128)(2,1)S(1)}, u32[]{:S(2)}, u32[]{:S(2)}) %all-to-all-start.2) | async-done | bytes 1835040 | tf_op jit(solution)/shard_map/all_to_all | solution.py:26
  80.9 1.3 copy-done.1
  82.3 6.4 %all-to-all-start = ((bf16[8,2,16,7168]{3,2,1,0:T(8,128)(2,1)}), bf16[8,2,16,7168]{3,2,1,0:T(8,128)(2,1)}, u32[]{:S(2)}, u32[]{:S(2)}) async-start(bf16[8,2,16,7168]{3,2,1,0:T(8,128)(2,1)} %bitcast.208), calls=%async_computation | async-start | bytes 7340032 | tf_op jit(solution)/shard_map/all_to_all | solution.py:26
  88.7 2.5 collective-permute-start
  91.1 60.0 %collective-permute-done.source_ref = bf16[8,16,3584]{2,1,0:T(8,128)(2,1)S(1)} collective-permute-done((bf16[8,16,3584]{2,1,0:T(8,128)(2,1)S(1)}, bf16[8,16,3584]{2,1,0:T(8,128)(2,1)S(1)}, u32[]{:S(2)}, u32[]{:S(2)}) %collective-permute-start) | collective-permute-done | bytes 917536 | tf_op jit(solution)/shard_map/ppermute | solution.py:22
  151.1 0.9 copy-done.10
  152.0 9.9 %pick_spans.4 = bf16[16,16,3584]{2,1,0:T(8,128)(2,1)} custom-call(s32[16]{0:T(128)} %reshape.189.index_ref, bf16[8,16,3584]{2,1,0:T(8,128)(2,1)} %copy-done.10), custom_call_target="tpu_custom_call" | custom-call | tf_op jit(solution)/shard_map/pick_spans/pallas_call | solution.py:52
  161.9 4.8 %all-to-all-start.1 = ((bf16[8,2,16,3584]{3,2,1,0:T(8,128)(2,1)}), bf16[8,2,16,3584]{3,2,1,0:T(8,128)(2,1)}, u32[]{:S(2)}, u32[]{:S(2)}) async-start(bf16[8,2,16,3584]{3,2,1,0:T(8,128)(2,1)} %bitcast.209), calls=%async_computation.1 | async-start | bytes 3670016 | tf_op jit(solution)/shard_map/all_to_all | solution.py:26
  167.1 0.7 fusion.53
  167.8 0.7 fusion.52
  168.5 0.7 fusion.51
  169.1 0.7 fusion.50
  169.8 0.7 fusion.49
  172.5 1.8 fusion.25
  174.3 3.2 fusion.16
  177.5 10.3 %all-to-all-done.1 = bf16[8,2,16,3584]{3,2,1,0:T(8,128)(2,1)} async-done(((bf16[8,2,16,3584]{3,2,1,0:T(8,128)(2,1)}), bf16[8,2,16,3584]{3,2,1,0:T(8,128)(2,1)}, u32[]{:S(2)}, u32[]{:S(2)}) %all-to-all-start.1) | async-done | bytes 1835040 | tf_op jit(solution)/shard_map/all_to_all | solution.py:26
  187.8 2.4 fusion.56
  190.3 1.2 broadcast_in_dim.37
  191.4 4.7 %all-to-all-start.3 = ((bf16[8,2,256,128]{3,2,1,0:T(8,128)(2,1)}), bf16[8,2,256,128]{3,2,1,0:T(8,128)(2,1)S(1)}, u32[]{:S(2)}, u32[]{:S(2)}) async-start(bf16[8,2,256,128]{3,2,1,0:T(8,128)(2,1)} %broadcast_in_dim.37), calls=%async_computation.3 | async-start | bytes 2097152 | tf_op jit(solution)/shard_map/all_to_all | solution.py:26
  196.1 0.7 fusion.45
  201.4 17.9 %all-to-all-done.3 = bf16[8,2,256,128]{3,2,1,0:T(8,128)(2,1)S(1)} async-done(((bf16[8,2,256,128]{3,2,1,0:T(8,128)(2,1)}), bf16[8,2,256,128]{3,2,1,0:T(8,128)(2,1)S(1)}, u32[]{:S(2)}, u32[]{:S(2)}) %all-to-all-start.3) | async-done | bytes 1048608 | tf_op jit(solution)/shard_map/all_to_all | solution.py:26
  219.3 7.6 %all-to-all-start.4 = ((bf16[16,128,512]{2,1,0:T(8,128)(2,1)}), bf16[16,128,512]{2,1,0:T(8,128)(2,1)}, u32[]{:S(2)}, u32[]{:S(2)}) async-start(bf16[16,128,512]{2,1,0:T(8,128)(2,1)} %fusion.38), calls=%async_computation.4 | async-start | bytes 4194304 | tf_op jit(solution)/shard_map/all_to_all | solution.py:26
  228.9 0.8 collective-permute-done.2
  229.8 2.7 pad_maximum_fusion
  232.5 42.0 %all-to-all-done.4.dec_ref = bf16[16,128,512]{2,1,0:T(8,128)(2,1)} async-done(((bf16[16,128,512]{2,1,0:T(8,128)(2,1)}), bf16[16,128,512]{2,1,0:T(8,128)(2,1)}, u32[]{:S(2)}, u32[]{:S(2)}) %all-to-all-start.4) | async-done | bytes 2097184 | tf_op jit(solution)/shard_map/all_to_all | solution.py:26
  274.5 10.9 %decode.1 = (bf16[32,256,128]{2,1,0:T(8,128)(2,1)}, bf16[16,128,512]{2,1,0:T(8,128)(2,1)}) custom-call(s32[24]{0:T(128)} %reshape.192.place_ref, s32[24]{0:T(128)} %reshape.193.block_ref, s32[1]{0:T(128)} %bitcast.4.core_ref, bf16[32,256,128]{2,1,0:T(8,128)(2,1)} %bitcast.212, bf16[16,128,512]{2,1,0:T(8,128)(2,1)} %all-to-all-done.4.dec_ref), custom_call_target="tpu_custom_call" | custom-call | flops 2415919104 | bytes 8388608 | tf_op jit(solution)/shard_map/decode/pallas_call | solution.py:104
  285.4 2.8 fusion.75
  288.9 1.0 multiply_reduce_fusion
  289.9 0.7 sub.49
  290.6 4.9 %all-to-all-start.7 = ((f32[16,1,448]{2,1,0:T(1,128)}), f32[16,1,448]{2,1,0:T(1,128)S(1)}, u32[]{:S(2)}, u32[]{:S(2)}) async-start(f32[16,1,448]{2,1,0:T(1,128)} %sub.49), calls=%async_computation.7 | async-start | bytes 65536 | tf_op jit(solution)/shard_map/all_to_all | solution.py:26
  295.5 4.2 %all-to-all-done.7 = f32[16,1,448]{2,1,0:T(1,128)S(1)} async-done(((f32[16,1,448]{2,1,0:T(1,128)}), f32[16,1,448]{2,1,0:T(1,128)S(1)}, u32[]{:S(2)}, u32[]{:S(2)}) %all-to-all-start.7) | async-done | bytes 28704 | tf_op jit(solution)/shard_map/all_to_all | solution.py:26
  300.4 5.9 %all-to-all-start.8 = ((f32[16,1,448]{2,1,0:T(1,128)}), f32[16,1,448]{2,1,0:T(1,128)S(1)}, u32[]{:S(2)}, u32[]{:S(2)}) async-start(f32[16,1,448]{2,1,0:T(1,128)} %broadcast_in_dim.42), calls=%async_computation.8 | async-start | bytes 65536 | tf_op jit(solution)/shard_map/all_to_all | solution.py:26
  306.2 2.5 fusion.6
  308.7 1.7 all-to-all-done.8
  310.4 5.3 %all-to-all-start.5 = ((bf16[8,2,256,128]{3,2,1,0:T(8,128)(2,1)}), bf16[8,2,256,128]{3,2,1,0:T(8,128)(2,1)S(1)}, u32[]{:S(2)}, u32[]{:S(2)}) async-start(bf16[8,2,256,128]{3,2,1,0:T(8,128)(2,1)} %fusion.6), calls=%async_computation.5 | async-start | bytes 2097152 | tf_op jit(solution)/shard_map/all_to_all | solution.py:26
  316.5 22.5 %all-to-all-done.5 = bf16[8,2,256,128]{3,2,1,0:T(8,128)(2,1)S(1)} async-done(((bf16[8,2,256,128]{3,2,1,0:T(8,128)(2,1)}), bf16[8,2,256,128]{3,2,1,0:T(8,128)(2,1)S(1)}, u32[]{:S(2)}, u32[]{:S(2)}) %all-to-all-start.5) | async-done | bytes 1048608 | tf_op jit(solution)/shard_map/all_to_all | solution.py:26
  339.0 7.6 %all-to-all-start.6 = ((bf16[16,128,512]{2,1,0:T(8,128)(2,1)}), bf16[16,128,512]{2,1,0:T(8,128)(2,1)}, u32[]{:S(2)}, u32[]{:S(2)}) async-start(bf16[16,128,512]{2,1,0:T(8,128)(2,1)} %get-tuple-element.7), calls=%async_computation.6 | async-start | bytes 4194304 | tf_op jit(solution)/shard_map/all_to_all | solution.py:26
  346.6 2.3 fusion.22
  348.9 1.7 fusion.80
  350.6 3.2 fusion.79
  354.8 2.2 fusion.78
  357.0 3.3 fusion.77
  360.8 0.7 fusion.59
  361.5 2.2 fusion.61
  363.7 5.1 %fusion.3 = f32[1,7168,128]{2,1,0:T(8,128)} fusion(bf16[256,7168]{1,0:T(8,128)(2,1)} %bitcast.1, f32[3584,128]{1,0:T(8,128)S(1)} %fusion.59, f32[3584,128]{1,0:T(8,128)S(1)} %fusion.61, bf16[256,128]{1,0:T(8,128)(2,1)S(1)} %get-tuple-element.45), kind=kOutput, calls=%fused_computation.5 | convolution fusion | flops 471597056 | bytes 11075584 | tf_op jit(solution)/shard_map/dot_general | solution.py:255
  368.8 25.3 %all-to-all-done.6 = bf16[16,128,512]{2,1,0:T(8,128)(2,1)} async-done(((bf16[16,128,512]{2,1,0:T(8,128)(2,1)}), bf16[16,128,512]{2,1,0:T(8,128)(2,1)}, u32[]{:S(2)}, u32[]{:S(2)}) %all-to-all-start.6) | async-done | bytes 2097184 | tf_op jit(solution)/shard_map/all_to_all | solution.py:26
  394.2 1.4 slice_bitcast_fusion
  395.5 0.9 fusion.37
  396.5 0.9 fusion.36
  397.4 0.9 fusion.35
  398.3 0.9 fusion.34
  399.3 0.9 fusion.33
  400.2 0.9 fusion.32
  401.2 0.9 fusion.31
  402.1 0.9 fusion.30
  403.5 1.1 copy-done.6
  405.1 5.8 %fusion.5 = f32[1,128,7168]{2,1,0:T(8,128)} fusion(bf16[256,128]{1,0:T(8,128)(2,1)S(1)} %get-tuple-element.35, bf16[256,7168]{1,0:T(8,128)(2,1)} %bitcast.1, f32[128,3584]{1,0:T(8,128)S(1)} %copy-done.6, f32[128,3584]{1,0:T(8,128)S(1)} %copy-done.7, f32[128,3584]{1,0:T(8,128)S(1)} %broadcast_in_dim.40, f32[128,3584]{1,0:T(8,128)S(1)} %broadcast_in_dim.39, ...), kind=kOutput, calls=%fused_computation.7 | convolution fusion | flops 480772096 | bytes 18445312 | tf_op jit(solution)/shard_map/dot_general | solution.py:227
  (87 shorter events, 14.6 us)
Async XLA Ops:
  0.6 4.0 copy-start.12
  2.2 42.0 %collective-permute-start.1 = (bf16[8,16,3584]{2,1,0:T(8,128)(2,1)S(1)}, bf16[8,16,3584]{2,1,0:T(8,128)(2,1)S(1)}, u32[]{:S(2)}, u32[]{:S(2)}) collective-permute-start(bf16[8,16,3584]{2,1,0:T(8,128)(2,1)S(1)} %get-tuple-element.31), channel_id=1, source_target_pairs={{0,8},{1,9},{2,10},{3,11},{4,12},{5,13},{6,14},{7,15},{8,0},{9,1},... | collective-permute-start | bytes 2752520 | tf_op jit(solution)/shard_map/ppermute | solution.py:22
  44.2 0.9 copy-start.9
  55.1 25.9 %all-to-all-start.2 = ((bf16[8,2,16,3584]{3,2,1,0:T(8,128)(2,1)}), bf16[8,2,16,3584]{3,2,1,0:T(8,128)(2,1)S(1)}, u32[]{:S(2)}, u32[]{:S(2)}) async-start(bf16[8,2,16,3584]{3,2,1,0:T(8,128)(2,1)} %bitcast.210), calls=%async_computation.2 | async-start | bytes 3670016 | tf_op jit(solution)/shard_map/all_to_all | solution.py:26
  80.9 1.3 copy-start.1
  82.3 79.7 %all-to-all-start = ((bf16[8,2,16,7168]{3,2,1,0:T(8,128)(2,1)}), bf16[8,2,16,7168]{3,2,1,0:T(8,128)(2,1)}, u32[]{:S(2)}, u32[]{:S(2)}) async-start(bf16[8,2,16,7168]{3,2,1,0:T(8,128)(2,1)} %bitcast.208), calls=%async_computation | async-start | bytes 7340032 | tf_op jit(solution)/shard_map/all_to_all | solution.py:26
  88.7 62.4 %collective-permute-start = (bf16[8,16,3584]{2,1,0:T(8,128)(2,1)S(1)}, bf16[8,16,3584]{2,1,0:T(8,128)(2,1)S(1)}, u32[]{:S(2)}, u32[]{:S(2)}) collective-permute-start(bf16[8,16,3584]{2,1,0:T(8,128)(2,1)S(1)} %get-tuple-element.30), channel_id=1, source_target_pairs={{0,8},{1,9},{2,10},{3,11},{4,12},{5,13},{6,14},{7,15},{8,0},{9,1},... | collective-permute-start | bytes 2752520 | tf_op jit(solution)/shard_map/ppermute | solution.py:22
  151.1 0.9 copy-start.10
  161.9 5.2 %copy-start = (bf16[1,128,7168]{2,1,0:T(8,128)(2,1)S(1)}, bf16[1,128,7168]{2,1,0:T(8,128)(2,1)}, u32[]{:S(2)}) copy-start(bf16[1,128,7168]{2,1,0:T(8,128)(2,1)} %param.9) | copy-start | bytes 5505028
  161.9 25.9 %all-to-all-start.1 = ((bf16[8,2,16,3584]{3,2,1,0:T(8,128)(2,1)}), bf16[8,2,16,3584]{3,2,1,0:T(8,128)(2,1)}, u32[]{:S(2)}, u32[]{:S(2)}) async-start(bf16[8,2,16,3584]{3,2,1,0:T(8,128)(2,1)} %bitcast.209), calls=%async_computation.1 | async-start | bytes 3670016 | tf_op jit(solution)/shard_map/all_to_all | solution.py:26
  167.1 5.3 %copy-start.2 = (bf16[8,2,16,3584]{3,2,1,0:T(8,128)(2,1)S(1)}, bf16[8,2,16,3584]{3,2,1,0:T(8,128)(2,1)}, u32[]{:S(2)}) copy-start(bf16[8,2,16,3584]{3,2,1,0:T(8,128)(2,1)} %copy-done.1) | copy-start | bytes 5505028
  171.1 3.2 copy-start.8
  171.1 3.2 copy-start.13
  191.4 27.9 %all-to-all-start.3 = ((bf16[8,2,256,128]{3,2,1,0:T(8,128)(2,1)}), bf16[8,2,256,128]{3,2,1,0:T(8,128)(2,1)S(1)}, u32[]{:S(2)}, u32[]{:S(2)}) async-start(bf16[8,2,256,128]{3,2,1,0:T(8,128)(2,1)} %broadcast_in_dim.37), calls=%async_computation.3 | async-start | bytes 2097152 | tf_op jit(solution)/shard_map/all_to_all | solution.py:26
  219.3 55.2 %all-to-all-start.4 = ((bf16[16,128,512]{2,1,0:T(8,128)(2,1)}), bf16[16,128,512]{2,1,0:T(8,128)(2,1)}, u32[]{:S(2)}, u32[]{:S(2)}) async-start(bf16[16,128,512]{2,1,0:T(8,128)(2,1)} %fusion.38), calls=%async_computation.4 | async-start | bytes 4194304 | tf_op jit(solution)/shard_map/all_to_all | solution.py:26
  226.9 2.8 collective-permute-start.2
  285.4 3.1 copy-start.5
  288.2 0.7 copy-start.11
  288.2 18.1 %collective-permute-start.3 = (bf16[8,2,256,128]{3,2,1,0:T(8,128)(2,1)}, bf16[8,2,256,128]{3,2,1,0:T(8,128)(2,1)}, u32[]{:S(2)}, u32[]{:S(2)}) collective-permute-start(bf16[8,2,256,128]{3,2,1,0:T(8,128)(2,1)} %bitcast.36), channel_id=1, source_target_pairs={{0,1},{1,0},{2,3},{3,2},{4,5},{5,4},{6,7},{7,6},{8,9},{9,8},{10,11... | collective-permute-start | bytes 3145736 | tf_op jit(solution)/shard_map/ppermute | solution.py:22
  290.6 9.0 %all-to-all-start.7 = ((f32[16,1,448]{2,1,0:T(1,128)}), f32[16,1,448]{2,1,0:T(1,128)S(1)}, u32[]{:S(2)}, u32[]{:S(2)}) async-start(f32[16,1,448]{2,1,0:T(1,128)} %sub.49), calls=%async_computation.7 | async-start | bytes 65536 | tf_op jit(solution)/shard_map/all_to_all | solution.py:26
  300.4 10.1 %all-to-all-start.8 = ((f32[16,1,448]{2,1,0:T(1,128)}), f32[16,1,448]{2,1,0:T(1,128)S(1)}, u32[]{:S(2)}, u32[]{:S(2)}) async-start(f32[16,1,448]{2,1,0:T(1,128)} %broadcast_in_dim.42), calls=%async_computation.8 | async-start | bytes 65536 | tf_op jit(solution)/shard_map/all_to_all | solution.py:26
  310.4 28.5 %all-to-all-start.5 = ((bf16[8,2,256,128]{3,2,1,0:T(8,128)(2,1)}), bf16[8,2,256,128]{3,2,1,0:T(8,128)(2,1)S(1)}, u32[]{:S(2)}, u32[]{:S(2)}) async-start(bf16[8,2,256,128]{3,2,1,0:T(8,128)(2,1)} %fusion.6), calls=%async_computation.5 | async-start | bytes 2097152 | tf_op jit(solution)/shard_map/all_to_all | solution.py:26
  339.0 55.2 %all-to-all-start.6 = ((bf16[16,128,512]{2,1,0:T(8,128)(2,1)}), bf16[16,128,512]{2,1,0:T(8,128)(2,1)}, u32[]{:S(2)}, u32[]{:S(2)}) async-start(bf16[16,128,512]{2,1,0:T(8,128)(2,1)} %get-tuple-element.7), calls=%async_computation.6 | async-start | bytes 4194304 | tf_op jit(solution)/shard_map/all_to_all | solution.py:26
  346.6 2.3 copy-start.3
  357.0 3.8 copy-start.4
  403.1 1.5 copy-start.6
  403.1 2.0 copy-start.7

commit v2 on v1

--- a/solution.py
+++ b/solution.py
@@ -42,55 +42,109 @@
     return span_of, live, slot_of
 
 
-def copy_block(index_ref, source_ref, out_ref):
-    out_ref[...] = source_ref[...]
+def pick_kernel(index_ref, rows_ref, out_ref, sems):
+    picked = out_ref.shape[0]
+
+    def start(i, carry):
+        pltpu.make_async_copy(rows_ref.at[index_ref[i]], out_ref.at[i], sems.at[i]).start()
+        return carry
+
+    def wait(i, carry):
+        pltpu.make_async_copy(rows_ref.at[0], out_ref.at[i], sems.at[i]).wait()
+        return carry
+
+    lax.fori_loop(0, picked, start, 0)
+    lax.fori_loop(0, picked, wait, 0)
 
 
 def pick_spans(rows, index):
-    span_count, part_rows, width = rows.shape
-    picked = index.shape[0]
+    shape = (index.shape[0],) + rows.shape[1:]
     return pl.pallas_call(
-        copy_block,
-        grid_spec=pltpu.PrefetchScalarGridSpec(
-            num_scalar_prefetch=1,
-            grid=(picked,),
-            in_specs=[pl.BlockSpec((1, part_rows, width), lambda i, at: (at[i], 0, 0))],
-            out_specs=pl.BlockSpec((1, part_rows, width), lambda i, at: (i, 0, 0)),
-        ),
-        out_shape=jax.ShapeDtypeStruct((picked, part_rows, width), rows.dtype),
+        pick_kernel,
+        in_specs=[pl.BlockSpec(memory_space=pltpu.SMEM), pl.BlockSpec(memory_space=pl.ANY)],
+        out_specs=pl.BlockSpec(memory_space=pl.ANY),
+        out_shape=jax.ShapeDtypeStruct(shape, rows.dtype),
+        scratch_shapes=[pltpu.SemaphoreType.DMA((shape[0],))],
         name="pick_spans",
     )(index, rows)
 
 
-def decode_kernel(names, skipped, place_ref, block_ref, core_ref, feat_ref, dec_ref, r_ref, y_ref, total):
+def window_kernel(starts, dec_ref, out_ref, sems):
+    width = out_ref.shape[-1]
+    copies = [
+        pltpu.make_async_copy(dec_ref.at[:, pl.ds(s, width)], out_ref.at[i], sems.at[i])
+        for i, s in enumerate(starts)
+    ]
+    for copy in copies:
+        copy.start()
+    for copy in copies:
+        copy.wait()
+
+
+def cut_windows(dec, starts, window):
+    if any(s % 128 for s in starts) or window % 128:
+        return jnp.stack([dec[:, s : s + window] for s in starts])
+    return pl.pallas_call(
+        functools.partial(window_kernel, starts),
+        in_specs=[pl.BlockSpec(memory_space=pl.ANY)],
+        out_specs=pl.BlockSpec(memory_space=pl.ANY),
+        out_shape=jax.ShapeDtypeStruct((len(starts), dec.shape[0], window), dec.dtype),
+        scratch_shapes=[pltpu.SemaphoreType.DMA((len(starts),))],
+        name="cut_windows",
+    )(dec)
+
+
+def join_kernel(skipped, part_ref, y_ref, out_ref):
+    window = y_ref.shape[-1]
+    out_ref[:, :window] = part_ref[:, :window] + y_ref[0].astype(f32)
+    out_ref[:, window:] = part_ref[:, window:] + y_ref[1][:, skipped:].astype(f32)
+
+
+def join_windows(part, y, skipped):
+    count, latents, window = y.shape
+    if window % 128 or skipped % 128:
+        cols = [y[i] if i % 2 == 0 else y[i][:, skipped:] for i in range(count)]
+        return part + jnp.concatenate(cols, axis=1).astype(f32)
+    per_chip = 2 * window - skipped
+    return pl.pallas_call(
+        functools.partial(join_kernel, skipped),
+        grid=(count // 2,),
+        in_specs=[
+            pl.BlockSpec((latents, per_chip), lambda i: (0, i)),
+            pl.BlockSpec((2, latents, window), lambda i: (i, 0, 0)),
+        ],
+        out_specs=pl.BlockSpec((latents, per_chip), lambda i: (0, i)),
+        out_shape=jax.ShapeDtypeStruct(part.shape, f32),
+        name="join_windows",
+    )(part, y)
+
+
+def decode_kernel(names, skipped, place_ref, block_ref, core_ref, feat_ref, dec_ref, r_ref, y_ref, total, feats, decs):
     span_count = place_ref.shape[0] // names
-    width = dec_ref.shape[-1]
+    latents = feat_ref.shape[-1]
     r_ref[...] = jnp.zeros_like(r_ref)
     total[...] = jnp.zeros_like(total)
 
     def span_step(span, carry):
-        feats, decs, recon = [], [], None
+        at = [place_ref[span * names + name] for name in range(names)]
+        block = [block_ref[span * names + name] for name in range(names)]
         for name in range(names):
-            feat = feat_ref[place_ref[span * names + name]]
-            dec = dec_ref[block_ref[span * names + name]]
-            contrib = jnp.dot(feat, dec, preferred_element_type=f32).astype(bf16).astype(f32)
-            recon = contrib if recon is None else recon + contrib
-            feats.append(feat)
-            decs.append(dec)
-        scaled = recon * grad_scale
+            feats[:, name * latents : (name + 1) * latents] = feat_ref[at[name]]
+            decs[name * latents : (name + 1) * latents, :] = dec_ref[block[name]]
+        scaled = jnp.dot(feats[...], decs[...], preferred_element_type=f32) * grad_scale
         if skipped:
             lane = lax.broadcasted_iota(jnp.int32, scaled.shape, 1)
             scaled = jnp.where(lane >= core_ref[0] * skipped, scaled, 0.0)
         delta = scaled.astype(bf16)
+        part = lax.dot_general(
+            delta, decs[...], (((1,), (1,)), ((), ())), preferred_element_type=f32
+        ).astype(bf16)
+        grad = lax.dot_general(
+            feats[...], delta, (((0,), (0,)), ((), ())), preferred_element_type=f32
+        )
         for name in range(names):
-            part = lax.dot_general(
-                delta, decs[name], (((1,), (1,)), ((), ())), preferred_element_type=f32
-            )
-            r_ref[place_ref[span * names + name]] = part.astype(bf16)
-            grad = lax.dot_general(
-                feats[name], delta, (((0,), (0,)), ((), ())), preferred_element_type=f32
-            )
-            total[block_ref[span * names + name]] += grad
+            r_ref[at[name]] = part[:, name * latents : (name + 1) * latents]
+            total[block[name]] += grad[name * latents : (name + 1) * latents]
         return carry
 
     lax.fori_loop(0, span_count, span_step, 0)
@@ -109,7 +163,11 @@
             jax.ShapeDtypeStruct(feats.shape, bf16),
             jax.ShapeDtypeStruct(dec.shape, bf16),
         ],
-        scratch_shapes=[pltpu.VMEM(dec.shape, f32)],
+        scratch_shapes=[
+            pltpu.VMEM(dec.shape, f32),
+            pltpu.VMEM((rows, names * latents), bf16),
+            pltpu.VMEM((names * latents, columns), bf16),
+        ],
         compiler_params=pltpu.CompilerParams(vmem_limit_bytes=56 * 2**20),
         cost_estimate=pl.CostEstimate(
             flops=6 * pairs * rows * latents * columns,
@@ -157,12 +215,6 @@
     enc, dec = enc_weight[0], dec_weight[0]
     span_of, live, slot_of = slot_tables(active, count)
 
-    mine = lax.dynamic_slice(span_of, (my_half * half, 0), (half, MOST)).reshape(-1)
-    far = [swap(activations[:, :, i * stream : (i + 1) * stream], half, count) for i in range(2)]
-    shape = (half, MOST, part_rows)
-    x_own = exchange(pick_spans(activations, mine).reshape(shape + (width,)), halves)
-    x_far = [exchange(pick_spans(a, mine).reshape(shape + (stream,)), halves) for a in far]
-
     per_chip = width // chips
     if per_chip % 128 == 0:
         window = -(-(per_chip // 2) // 128) * 128
@@ -170,14 +222,22 @@
         window = per_chip // 2
     skipped = 2 * window - per_chip
     starts = [(i // 2) * per_chip + (i % 2) * (per_chip - window) for i in range(count)]
-    dec_all = exchange(jnp.stack([dec[:, s : s + window] for s in starts]))
+    dec_all = exchange(cut_windows(dec, starts, window))
+
+    mine = lax.dynamic_slice(span_of, (my_half * half, 0), (half, MOST)).reshape(-1)
+    across = swap(activations, half, count)
+    shape = (half, MOST, part_rows)
+    near, dec_all = lax.optimization_barrier((pick_spans(activations, mine), dec_all))
+    x_own = exchange(near.reshape(shape + (width,)), halves)
+    across, x_own = lax.optimization_barrier((pick_spans(across, mine), x_own))
+    x_far = exchange(across.reshape(shape + (width,)), halves)
 
     rows = half * MOST * part_rows
     own = x_own.reshape(rows, width)
-    far = [x.reshape(rows, stream) for x in x_far]
+    far = x_far.reshape(rows, width)
     dot = functools.partial(jnp.dot, preferred_element_type=f32)
     preact_own = dot(own, enc) + enc_bias[0]
-    preact_far = dot(far[0], enc[:stream]) + dot(far[1], enc[stream:]) + enc_bias[0]
+    preact_far = dot(far, enc) + enc_bias[0]
     my_live = lax.dynamic_slice(live, (me, 0), (1, MOST)).astype(f32)
     mask = jnp.broadcast_to(my_live[0][None, :, None, None], shape + (1,)).reshape(rows, 1)
     feat_own = jnp.maximum(preact_own, 0.0) * mask
@@ -207,7 +267,7 @@
     r_out = r_out.reshape(2, chips, MOST, span_rows, latents)
     r_near = swap(r_out[1], 1, count)
     r_sum = (r_out[0].astype(f32) + r_near.astype(f32)).astype(bf16)
-    r_in = exchange(r_sum, same_core)
+    r_in, y_out = lax.optimization_barrier((exchange(r_sum, same_core), y_out))
     y_in = exchange(y_out)
     recon_part = jnp.sum(r_in.astype(f32), axis=0)
 
@@ -220,11 +280,11 @@
         lax.dot_general, dimension_numbers=(((1,), (1,)), ((), ())), preferred_element_type=f32
     )
     xd_own = cross(own, dec)
-    xd_far = cross(far[0], dec[:, :stream]) + cross(far[1], dec[:, stream:])
+    xd_far = cross(far, dec)
     down = functools.partial(
         lax.dot_general, dimension_numbers=(((0,), (0,)), ((), ())), preferred_element_type=f32
     )
-    fx = down(fb_own, own) + jnp.concatenate([down(fb_far, x) for x in far], axis=1)
+    fx = down(fb_own, own) + down(fb_far, far)
     feature_sum = jnp.sum(feat_own, axis=0) + jnp.sum(feat_far, axis=0)
     rounded_sum = jnp.sum(fb_own.astype(f32), axis=0) + jnp.sum(fb_far.astype(f32), axis=0)
     inverse = jnp.concatenate(
@@ -239,12 +299,6 @@
         + penalty_weight * feature_sum[:, None] * weights * inverse
     )
 
-    act_sum = jnp.sum(activations.astype(f32), axis=(0, 1))
-    bias_part = jnp.sum(rounded_sum[:, None] * weights, axis=0) - act_sum
-    bias_cols = jnp.sum(exchange(bias_part.reshape(count, width // count)), axis=0)
-    bias_all = exchange(jnp.broadcast_to(bias_cols[None], (count, width // count))).reshape(-1)
-    dec_bias_grad = grad_scale * (bias_all + float(span_count * part_rows * count) * dec_bias)
-
     first, second = recon_part[:, : span_rows // 2], recon_part[:, span_rows // 2 :]
     r_own = by_source(jnp.where(lower, first, second))
     r_far = by_source(jnp.where(lower, second, first))
@@ -252,12 +306,17 @@
     grad_far = jnp.where((preact_far > 0.0) & (mask > 0.0), r_far - grad_scale * xd_far + constant, 0.0)
     bias_grad = jnp.sum(grad_own, axis=0) + jnp.sum(grad_far, axis=0)
     gb_own, gb_far = grad_own.astype(bf16), grad_far.astype(bf16)
-    enc_grad = down(own, gb_own) + jnp.concatenate([down(x, gb_far) for x in far], axis=0)
-
-    y_cols = jnp.concatenate(
-        [y_in[i] if i % 2 == 0 else y_in[i][:, skipped:] for i in range(count)], axis=1
-    )
-    dec_grad = dec_part + y_cols.astype(f32)
+    enc_grad = down(own, gb_own) + down(far, gb_far)
+
+    act_sum = jnp.sum(activations.astype(f32), axis=(0, 1))
+    bias_sum = jnp.sum(rounded_sum[:, None] * weights, axis=0) - act_sum
+    bias_sum, recon_part = lax.optimization_barrier((bias_sum, recon_part))
+    distance = 1
+    while distance < count:
+        bias_sum = bias_sum + swap(bias_sum, distance, count)
+        distance *= 2
+    dec_bias_grad = grad_scale * (bias_sum + float(span_count * part_rows * count) * dec_bias)
+    dec_grad = join_windows(dec_part, y_in, skipped)
     return (enc_grad[None], bias_grad[None], dec_grad[None], dec_bias_grad)
 
 

time: 413 us -> 580 us (1.40)
  Pallas kernels: 41.4 us -> 307 us
  waiting for transfers between devices: 234 us -> 161 us
  local copies, waits for them, and re-layouts: 34.2 us -> 4.81 us
  blocking collectives: 0 us -> 28.1 us
  starting transfers between devices: 57.6 us -> 37.8 us
    pallas_call x3 -> x4, Pallas kernels: 30.6 us -> 298 us  [the longest x2 226 us: pick_spans(): pl.pallas_call(pick_kernel, in_specs=[pl.BlockSpec(memory_space=pltpu.SME...]
    all_to_all x9 -> x5, waiting for transfers between devices: 134 us -> 60.1 us  [exchange(): lax.all_to_all(x, AXIS, split_axis=0, concat_axis=0, tiled=True, axis_ind...]
    all_to_all x0 -> x1, blocking collectives: none -> 28.1 us  [exchange(): lax.all_to_all(x, AXIS, split_axis=0, concat_axis=0, tiled=True, axis_ind...]
    all_to_all x9 -> x5, starting transfers between devices: 52.2 us -> 28.9 us  [exchange(): lax.all_to_all(x, AXIS, split_axis=0, concat_axis=0, tiled=True, axis_ind...]
    unnamed x59 -> x15, local copies, waits for them, and re-layouts: 22.6 us -> 0.16 us
    dot_general x10 -> x6, matrix products: 27.3 us -> 23.1 us  [the longest x2 8.41 us: shards(): fx = down(fb_own, own) + down(fb_far, far)]
    ppermute x4 -> x7, waiting for transfers between devices: 99.5 us -> 101 us  [swap(): return lax.ppermute(x, AXIS, [(i, i ^ distance) for i in range(count)])]
  transfers between devices with their start and end apart: 13 -> 12, of which waited for: 11 -> 8; matrix products, arithmetic and copies ran while one was open for 12% -> 6% of each run, Pallas kernels for 5% -> 39%
where the time goes in v2:
time: 580 us; the launch traced here: 576 us
  Pallas kernels  307 us (53%)
  waiting for transfers between devices  161 us (28%)
  starting transfers between devices  37.8 us (7%)
  matrix products  29.4 us (5%)
  blocking collectives  28.1 us (5%)
  other arithmetic  6.62 us (1%)
    pallas_call x2, Pallas kernels, pick_spans(): pl.pallas_call(pick_kernel, in_specs=[pl.BlockSpec(memory_space=pltpu.SME...  226 us
    ppermute x7, waiting for transfers between devices, swap(): return lax.ppermute(x, AXIS, [(i, i ^ distance) for i in range(count)])  101 us
    pallas_call x1, Pallas kernels, cut_windows(): pl.pallas_call(functools.partial(window_kernel, starts), in_specs=[pl.Blo...  64.8 us
    all_to_all x5, waiting for transfers between devices, exchange(): lax.all_to_all(x, AXIS, split_axis=0, concat_axis=0, tiled=True, axis_ind...  60.1 us
    all_to_all x5, starting transfers between devices, exchange(): lax.all_to_all(x, AXIS, split_axis=0, concat_axis=0, tiled=True, axis_ind...  28.9 us
    all_to_all x1, blocking collectives, exchange(): lax.all_to_all(x, AXIS, split_axis=0, concat_axis=0, tiled=True, axis_ind...  28.1 us
  transfers between devices with their start and end apart: 12, of which 8 were waited for; matrix products, arithmetic and copies ran while one was open for 6% of the time, Pallas kernels for 39%

profile of v2, /device:TPU:15, one launch (start us, length us, event | category | flops | bytes accessed | tf_op | source)
XLA Modules:
  0.0 576.0 jit_solution(4466333449963470623)
XLA Ops:
  0.6 0.0 copy-start
  0.7 64.8 %cut_windows.1 = bf16[16,128,512]{2,1,0:T(8,128)(2,1)} custom-call(bf16[128,7168]{1,0:T(8,128)(2,1)} %bitcast.67), custom_call_target="tpu_custom_call" | custom-call | tf_op jit(solution)/shard_map/cut_windows/pallas_call | solution.py:87
  65.4 6.6 %all-to-all-start = ((bf16[16,128,512]{2,1,0:T(8,128)(2,1)}), bf16[16,128,512]{2,1,0:T(8,128)(2,1)}, u32[]{:S(2)}, u32[]{:S(2)}) async-start(bf16[16,128,512]{2,1,0:T(8,128)(2,1)} %cut_windows.1), calls=%async_computation | async-start | bytes 4194304 | tf_op jit(solution)/shard_map/all_to_all | solution.py:26
  72.0 0.1 fusion.30
  72.2 0.1 constant_dynamic-slice_fusion
  72.2 0.1 copy.27
  72.3 0.6 reshape.148.index_ref
  72.9 113.1 %pick_spans.3 = bf16[16,16,7168]{2,1,0:T(8,128)(2,1)} custom-call(s32[16]{0:T(128)} %reshape.148.index_ref, bf16[8,16,7168]{2,1,0:T(8,128)(2,1)} %rows_ref.1), custom_call_target="tpu_custom_call" | custom-call | tf_op jit(solution)/shard_map/pick_spans/pallas_call | solution.py:62
  186.0 0.0 all-to-all-done.dec_ref
  186.0 4.6 all-to-all-start.1
  190.6 2.5 collective-permute-start
  193.1 79.7 %collective-permute-done.rows_ref = bf16[8,16,7168]{2,1,0:T(8,128)(2,1)} collective-permute-done((bf16[8,16,7168]{2,1,0:T(8,128)(2,1)}, bf16[8,16,7168]{2,1,0:T(8,128)(2,1)}, u32[]{:S(2)}, u32[]{:S(2)}) %collective-permute-start) | collective-permute-done | bytes 1835040 | tf_op jit(solution)/shard_map/ppermute | solution.py:22
  272.8 113.1 %pick_spans.2 = bf16[16,16,7168]{2,1,0:T(8,128)(2,1)} custom-call(s32[16]{0:T(128)} %reshape.148.index_ref, bf16[8,16,7168]{2,1,0:T(8,128)(2,1)} %collective-permute-done.rows_ref), custom_call_target="tpu_custom_call" | custom-call | tf_op jit(solution)/shard_map/pick_spans/pallas_call | solution.py:62
  385.9 0.0 copy-start.6
  385.9 4.7 all-to-all-start.2
  390.7 0.2 convert_reduce_fusion.4
  390.8 0.1 broadcast_in_dim.31
  390.9 0.1 broadcast_in_dim.32
  391.0 3.1 fusion.11
  394.2 37.2 %all-to-all-done.2 = bf16[8,2,16,7168]{3,2,1,0:T(8,128)(2,1)} async-done(((bf16[8,2,16,7168]{3,2,1,0:T(8,128)(2,1)}), bf16[8,2,16,7168]{3,2,1,0:T(8,128)(2,1)}, u32[]{:S(2)}, u32[]{:S(2)}) %all-to-all-start.2) | async-done | bytes 3670048 | tf_op jit(solution)/shard_map/all_to_all | solution.py:26
  431.3 3.2 fusion.25
  434.6 0.2 broadcast_in_dim.35
  434.8 28.1 %all_to_all.30 = bf16[8,2,256,128]{3,2,1,0:T(8,128)(2,1)S(1)} all-to-all(bf16[8,2,256,128]{3,2,1,0:T(8,128)(2,1)S(1)} %broadcast_in_dim.35), channel_id=1, replica_groups={{0,2,4,6,8,10,12,14},{1,3,5,7,9,11,13,15},{16,18,20,22,24,26,28,30},{17..., dimensions={0} | all-to-all | bytes 2097152 | tf_op jit(solution)/shard_map/all_to_all | solution.py:26
  462.9 2.3 collective-permute-start.1
  465.2 0.1 copy.29
  465.3 0.2 select_reduce_fusion
  465.5 0.1 copy.28
  465.6 0.6 reshape.151.place_ref
  466.2 0.6 reshape.152.block_ref
  466.8 0.6 collective-permute-done.1
  467.5 1.5 pad_maximum_fusion
  469.0 9.8 %decode.1 = (bf16[32,256,128]{2,1,0:T(8,128)(2,1)}, bf16[16,128,512]{2,1,0:T(8,128)(2,1)}) custom-call(s32[24]{0:T(128)} %reshape.151.place_ref, s32[24]{0:T(128)} %reshape.152.block_ref, s32[1]{0:T(128)} %bitcast.5.core_ref, bf16[32,256,128]{2,1,0:T(8,128)(2,1)} %bitcast.72, bf16[16,128,512]{2,1,0:T(8,128)(2,1)} %all-to-all-done.dec_ref), custom_call_target="tpu_custom_call" | custom-call | flops 2415919104 | bytes 8388608 | tf_op jit(solution)/shard_map/decode/pallas_call | solution.py:158
  478.8 1.8 fusion.43
  480.6 0.0 copy-start.2
  480.6 0.4 collective-permute-start.2
  481.0 0.3 convert_reduce_fusion
  481.3 2.0 collective-permute-done.2
  483.3 1.2 fusion.4
  484.6 5.4 all-to-all-start.4
  490.0 0.4 bitcast_convert_fusion
  490.3 0.3 fusion.6
  490.7 0.0 copy-done.4
  490.7 1.0 multiply_reduce_fusion
  491.7 21.5 %all-to-all-done.4 = bf16[8,2,256,128]{3,2,1,0:T(8,128)(2,1)S(1)} async-done(((bf16[8,2,256,128]{3,2,1,0:T(8,128)(2,1)}), bf16[8,2,256,128]{3,2,1,0:T(8,128)(2,1)S(1)}, u32[]{:S(2)}, u32[]{:S(2)}) %all-to-all-start.4) | async-done | bytes 1048608 | tf_op jit(solution)/shard_map/all_to_all | solution.py:26
  513.2 7.6 %all-to-all-start.5 = ((bf16[16,128,512]{2,1,0:T(8,128)(2,1)}), bf16[16,128,512]{2,1,0:T(8,128)(2,1)}, u32[]{:S(2)}, u32[]{:S(2)}) async-start(bf16[16,128,512]{2,1,0:T(8,128)(2,1)} %get-tuple-element.20), calls=%async_computation.5 | async-start | bytes 4194304 | tf_op jit(solution)/shard_map/all_to_all | solution.py:26
  520.9 2.7 fusion.46
  523.6 0.2 broadcast_in_dim.39
  523.8 0.2 broadcast_in_dim.37
  524.0 5.7 fusion.2.part_ref
  529.6 0.1 convert_reduce_fusion.1
  529.8 0.4 collective-permute-start.3
  530.3 3.2 fusion.44
  533.4 3.2 fusion.28
  536.7 0.3 collective-permute-start.4
  537.0 3.2 fusion.45
  540.2 2.1 collective-permute-start.5
  542.3 5.1 fusion.3
  547.4 9.5 %collective-permute-done.5 = f32[7168]{0:T(1024)S(1)} collective-permute-done((f32[7168]{0:T(1024)S(1)}, f32[7168]{0:T(1024)S(1)}, u32[]{:S(2)}, u32[]{:S(2)}) %collective-permute-start.5) | collective-permute-done | bytes 28704 | tf_op jit(solution)/shard_map/ppermute | solution.py:22
  557.0 0.8 collective-permute-start.6
  557.8 0.5 add_bitcast_fusion
  558.3 9.0 %collective-permute-done.6 = f32[7168]{0:T(1024)S(1)} collective-permute-done((f32[7168]{0:T(1024)S(1)}, f32[7168]{0:T(1024)S(1)}, u32[]{:S(2)}, u32[]{:S(2)}) %collective-permute-start.6) | collective-permute-done | bytes 28704 | tf_op jit(solution)/shard_map/ppermute | solution.py:22
  567.3 0.6 add_multiply_fusion
  567.9 1.4 all-to-all-done.5.y_ref
  569.3 6.7 %join_windows.1 = f32[128,7168]{1,0:T(8,128)} custom-call(f32[128,7168]{1,0:T(8,128)} %fusion.2.part_ref, bf16[16,128,512]{2,1,0:T(8,128)(2,1)} %all-to-all-done.5.y_ref), custom_call_target="tpu_custom_call" | custom-call | tf_op jit(solution)/shard_map/join_windows/pallas_call | solution.py:109
  (33 shorter events, 0.2 us)
Async XLA Ops:
  0.6 390.4 %copy-start = (bf16[1,7168,128]{2,1,0:T(8,128)(2,1)S(1)}, bf16[1,7168,128]{2,1,0:T(8,128)(2,1)}, u32[]{:S(2)}) copy-start(bf16[1,7168,128]{2,1,0:T(8,128)(2,1)} %param.7) | copy-start | bytes 5505028
  0.6 71.4 %copy-start.5 = (s32[8,3]{0,1:T(4,128)S(1)}, s32[8,3]{0,1:T(4,128)}, u32[]{:S(2)}) copy-start(s32[8,3]{0,1:T(4,128)} %param.11) | copy-start | bytes 292
  65.4 120.6 %all-to-all-start = ((bf16[16,128,512]{2,1,0:T(8,128)(2,1)}), bf16[16,128,512]{2,1,0:T(8,128)(2,1)}, u32[]{:S(2)}, u32[]{:S(2)}) async-start(bf16[16,128,512]{2,1,0:T(8,128)(2,1)} %cut_windows.1), calls=%async_computation | async-start | bytes 4194304 | tf_op jit(solution)/shard_map/all_to_all | solution.py:26
  186.0 199.9 %all-to-all-start.1 = ((bf16[8,2,16,7168]{3,2,1,0:T(8,128)(2,1)}), bf16[8,2,16,7168]{3,2,1,0:T(8,128)(2,1)}, u32[]{:S(2)}, u32[]{:S(2)}) async-start(bf16[8,2,16,7168]{3,2,1,0:T(8,128)(2,1)} %bitcast.69), calls=%async_computation.1 | async-start | bytes 7340032 | tf_op jit(solution)/shard_map/all_to_all | solution.py:26
  190.6 82.2 %collective-permute-start = (bf16[8,16,7168]{2,1,0:T(8,128)(2,1)}, bf16[8,16,7168]{2,1,0:T(8,128)(2,1)}, u32[]{:S(2)}, u32[]{:S(2)}) collective-permute-start(bf16[8,16,7168]{2,1,0:T(8,128)(2,1)} %rows_ref.1), channel_id=1, source_target_pairs={{0,8},{1,9},{2,10},{3,11},{4,12},{5,13},{6,14},{7,15},{8,0},{9,1},... | collective-permute-start | bytes 5505032 | tf_op jit(solution)/shard_map/ppermute | solution.py:22
  385.9 5.1 copy-start.6
  385.9 45.4 %all-to-all-start.2 = ((bf16[8,2,16,7168]{3,2,1,0:T(8,128)(2,1)}), bf16[8,2,16,7168]{3,2,1,0:T(8,128)(2,1)}, u32[]{:S(2)}, u32[]{:S(2)}) async-start(bf16[8,2,16,7168]{3,2,1,0:T(8,128)(2,1)} %bitcast.68), calls=%async_computation.2 | async-start | bytes 7340032 | tf_op jit(solution)/shard_map/all_to_all | solution.py:26
  462.9 4.6 collective-permute-start.1
  478.8 2.3 copy-start.3
  480.6 9.4 %copy-start.2 = (bf16[1,128,7168]{2,1,0:T(8,128)(2,1)S(1)}, bf16[1,128,7168]{2,1,0:T(8,128)(2,1)}, u32[]{:S(2)}) copy-start(bf16[1,128,7168]{2,1,0:T(8,128)(2,1)} %param.9) | copy-start | bytes 5505028
  480.6 2.7 collective-permute-start.2
  484.6 28.6 %all-to-all-start.4 = ((bf16[8,2,256,128]{3,2,1,0:T(8,128)(2,1)}), bf16[8,2,256,128]{3,2,1,0:T(8,128)(2,1)S(1)}, u32[]{:S(2)}, u32[]{:S(2)}) async-start(bf16[8,2,256,128]{3,2,1,0:T(8,128)(2,1)} %fusion.4), calls=%async_computation.4 | async-start | bytes 2097152 | tf_op jit(solution)/shard_map/all_to_all | solution.py:26
  490.0 0.7 copy-start.4
  513.2 56.1 %all-to-all-start.5 = ((bf16[16,128,512]{2,1,0:T(8,128)(2,1)}), bf16[16,128,512]{2,1,0:T(8,128)(2,1)}, u32[]{:S(2)}, u32[]{:S(2)}) async-start(bf16[16,128,512]{2,1,0:T(8,128)(2,1)} %get-tuple-element.20), calls=%async_computation.5 | async-start | bytes 4194304 | tf_op jit(solution)/shard_map/all_to_all | solution.py:26
  529.8 6.8 %collective-permute-start.3 = (f32[7168]{0:T(1024)S(1)}, f32[7168]{0:T(1024)S(1)}, u32[]{:S(2)}, u32[]{:S(2)}) collective-permute-start(f32[7168]{0:T(1024)S(1)} %sub.37), channel_id=1, source_target_pairs={{0,1},{1,0},{2,3},{3,2},{4,5},{5,4},{6,7},{7,6},{8,9},{9,8},{10,11... | collective-permute-start | bytes 86024 | tf_op jit(solution)/shard_map/ppermute | solution.py:22
  536.7 3.5 collective-permute-start.4
  540.2 16.8 %collective-permute-start.5 = (f32[7168]{0:T(1024)S(1)}, f32[7168]{0:T(1024)S(1)}, u32[]{:S(2)}, u32[]{:S(2)}) collective-permute-start(f32[7168]{0:T(1024)S(1)} %add.170), channel_id=1, source_target_pairs={{0,4},{1,5},{2,6},{3,7},{4,0},{5,1},{6,2},{7,3},{8,12},{9,13},{10,... | collective-permute-start | bytes 86024 | tf_op jit(solution)/shard_map/ppermute | solution.py:22
  557.0 10.3 %collective-permute-start.6 = (f32[7168]{0:T(1024)S(1)}, f32[7168]{0:T(1024)S(1)}, u32[]{:S(2)}, u32[]{:S(2)}) collective-permute-start(f32[7168]{0:T(1024)S(1)} %add.171), channel_id=1, source_target_pairs={{0,8},{1,9},{2,10},{3,11},{4,12},{5,13},{6,14},{7,15},{8,0},{9,1},... | collective-permute-start | bytes 86024 | tf_op jit(solution)/shard_map/ppermute | solution.py:22
  567.3 8.7 %copy-start.1 = (bf16[1,7168,128]{2,1,0:T(8,128)(2,1)S(1)}, bf16[1,7168,128]{2,1,0:T(8,128)(2,1)}, u32[]{:S(2)}) copy-start(bf16[1,7168,128]{2,1,0:T(8,128)(2,1)} %param.7) | copy-start | bytes 5505028

commit v3 on v2

--- a/solution.py
+++ b/solution.py
@@ -42,31 +42,43 @@
     return span_of, live, slot_of
 
 
-def pick_kernel(index_ref, rows_ref, out_ref, sems):
+def pick_kernel(firsts, index_ref, *refs):
+    parts, out_ref, sems = refs[: len(firsts)], refs[-2], refs[-1]
     picked = out_ref.shape[0]
 
     def start(i, carry):
-        pltpu.make_async_copy(rows_ref.at[index_ref[i]], out_ref.at[i], sems.at[i]).start()
+        span = index_ref[i]
+        for first, part in zip(firsts, parts):
+
+            @pl.when((span >= first) & (span < first + part.shape[0]))
+            def _():
+                pltpu.make_async_copy(part.at[span - first], out_ref.at[i], sems.at[i]).start()
+
         return carry
 
     def wait(i, carry):
-        pltpu.make_async_copy(rows_ref.at[0], out_ref.at[i], sems.at[i]).wait()
+        pltpu.make_async_copy(parts[0].at[0], out_ref.at[i], sems.at[i]).wait()
         return carry
 
     lax.fori_loop(0, picked, start, 0)
     lax.fori_loop(0, picked, wait, 0)
 
 
-def pick_spans(rows, index):
-    shape = (index.shape[0],) + rows.shape[1:]
+def pick_spans(parts, index):
+    shape = (index.shape[0],) + parts[0].shape[1:]
+    firsts = [sum(p.shape[0] for p in parts[:i]) for i in range(len(parts))]
+    size = sum(p.size for p in parts) * 2
     return pl.pallas_call(
-        pick_kernel,
-        in_specs=[pl.BlockSpec(memory_space=pltpu.SMEM), pl.BlockSpec(memory_space=pl.ANY)],
+        functools.partial(pick_kernel, firsts),
+        in_specs=[pl.BlockSpec(memory_space=pltpu.SMEM)]
+        + [pl.BlockSpec(memory_space=pltpu.VMEM)] * len(parts),
         out_specs=pl.BlockSpec(memory_space=pl.ANY),
-        out_shape=jax.ShapeDtypeStruct(shape, rows.dtype),
+        out_shape=jax.ShapeDtypeStruct(shape, parts[0].dtype),
         scratch_shapes=[pltpu.SemaphoreType.DMA((shape[0],))],
+        compiler_params=pltpu.CompilerParams(vmem_limit_bytes=48 * 2**20),
+        cost_estimate=pl.CostEstimate(flops=0, bytes_accessed=3 * size, transcendentals=0),
         name="pick_spans",
-    )(index, rows)
+    )(index, *parts)
 
 
 def window_kernel(starts, dec_ref, out_ref, sems):
@@ -86,10 +98,11 @@
         return jnp.stack([dec[:, s : s + window] for s in starts])
     return pl.pallas_call(
         functools.partial(window_kernel, starts),
-        in_specs=[pl.BlockSpec(memory_space=pl.ANY)],
+        in_specs=[pl.BlockSpec(memory_space=pltpu.VMEM)],
         out_specs=pl.BlockSpec(memory_space=pl.ANY),
         out_shape=jax.ShapeDtypeStruct((len(starts), dec.shape[0], window), dec.dtype),
         scratch_shapes=[pltpu.SemaphoreType.DMA((len(starts),))],
+        cost_estimate=pl.CostEstimate(flops=0, bytes_accessed=4 * dec.size, transcendentals=0),
         name="cut_windows",
     )(dec)
 
@@ -222,27 +235,23 @@
         window = per_chip // 2
     skipped = 2 * window - per_chip
     starts = [(i // 2) * per_chip + (i % 2) * (per_chip - window) for i in range(count)]
-    dec_all = exchange(cut_windows(dec, starts, window))
 
     mine = lax.dynamic_slice(span_of, (my_half * half, 0), (half, MOST)).reshape(-1)
-    across = swap(activations, half, count)
+    first = (span_count * 5 + 7) // 8
+    across = [swap(activations[:first], half, count), swap(activations[first:], half, count)]
     shape = (half, MOST, part_rows)
-    near, dec_all = lax.optimization_barrier((pick_spans(activations, mine), dec_all))
-    x_own = exchange(near.reshape(shape + (width,)), halves)
-    across, x_own = lax.optimization_barrier((pick_spans(across, mine), x_own))
-    x_far = exchange(across.reshape(shape + (width,)), halves)
+    x_own = exchange(pick_spans([activations], mine).reshape(shape + (width,)), halves)
+    windows, across[0], x_own = lax.optimization_barrier(
+        (cut_windows(dec, starts, window), across[0], x_own)
+    )
+    dec_all = exchange(windows)
+    across[1], dec_all = lax.optimization_barrier((across[1], dec_all))
+    x_far = exchange(pick_spans(across, mine).reshape(shape + (width,)), halves)
 
     rows = half * MOST * part_rows
-    own = x_own.reshape(rows, width)
-    far = x_far.reshape(rows, width)
     dot = functools.partial(jnp.dot, preferred_element_type=f32)
-    preact_own = dot(own, enc) + enc_bias[0]
-    preact_far = dot(far, enc) + enc_bias[0]
     my_live = lax.dynamic_slice(live, (me, 0), (1, MOST)).astype(f32)
     mask = jnp.broadcast_to(my_live[0][None, :, None, None], shape + (1,)).reshape(rows, 1)
-    feat_own = jnp.maximum(preact_own, 0.0) * mask
-    feat_far = jnp.maximum(preact_far, 0.0) * mask
-    fb_own, fb_far = feat_own.astype(bf16), feat_far.astype(bf16)
 
     def by_slot(x):
         return x.reshape(half, MOST, part_rows, latents).transpose(1, 0, 2, 3).reshape(MOST, -1, latents)
@@ -250,26 +259,47 @@
     def by_source(x):
         return x.reshape(MOST, half, part_rows, latents).transpose(1, 0, 2, 3).reshape(rows, latents)
 
+    def encode(x):
+        preact = dot(x, enc) + enc_bias[0]
+        feat = jnp.maximum(preact, 0.0) * mask
+        return preact, feat, feat.astype(bf16)
+
+    def spread(x):
+        same = [x] + [swap(x, 2 * i, count) for i in range(1, chips)]
+        return same
+
+    own = x_own.reshape(rows, width)
+    preact_own, feat_own, fb_own = encode(own)
+    all_own = spread(by_slot(fb_own))
+    barred = lax.optimization_barrier((x_far, *all_own))
+    x_far, all_own = barred[0], barred[1:]
+    far = x_far.reshape(rows, width)
+    preact_far, feat_far, fb_far = encode(far)
+    all_far = spread(by_slot(fb_far))
+
     lower = my_half == 0
-    a, b = by_slot(fb_own), by_slot(fb_far)
-    feats = jnp.concatenate([jnp.where(lower, a, b), jnp.where(lower, b, a)], axis=1)
-
-    span_rows = feats.shape[1]
-    same = exchange(jnp.broadcast_to(feats[None], (chips,) + feats.shape), same_core)
+    same_own, same_far = jnp.stack(all_own), jnp.stack(all_far)
+    near_chip = (jnp.arange(chips) < chips // 2)[:, None, None, None]
+    flip = jnp.logical_xor(near_chip, lower)
+    low = jnp.where(flip, same_far, same_own)
+    high = jnp.where(flip, same_own, same_far)
+    same = jnp.concatenate([low, high], axis=2)
+    span_rows = same.shape[2]
     other = swap(same, 1, count)
     feats_all = jnp.concatenate([same, other]).reshape(count * MOST, span_rows, latents)
-    place = (((active % 2) ^ core) * chips + active // 2) * MOST + slot_of
+    place = (((active % 2) ^ core) * chips + ((active // 2) ^ (me // 2))) * MOST + slot_of
 
     small = feats_all.size * 4 + dec_all.size * 8 < 40 * 2**20
     r_out, y_out = (decode if small else decode_plain)(
         names, skipped, place.reshape(-1), active.reshape(-1), core.reshape(1), feats_all, dec_all
     )
+    y_in = exchange(y_out)
     r_out = r_out.reshape(2, chips, MOST, span_rows, latents)
     r_near = swap(r_out[1], 1, count)
     r_sum = (r_out[0].astype(f32) + r_near.astype(f32)).astype(bf16)
-    r_in, y_out = lax.optimization_barrier((exchange(r_sum, same_core), y_out))
-    y_in = exchange(y_out)
-    recon_part = jnp.sum(r_in.astype(f32), axis=0)
+    recon_part = r_sum[0].astype(f32)
+    for i in range(1, chips):
+        recon_part = recon_part + swap(r_sum[i], 2 * i, count).astype(f32)
 
     weights = dec.astype(f32)
     base_norm = jnp.sqrt(jnp.sum(weights[:, :stream] * weights[:, :stream], axis=1) + epsilon)
@@ -306,17 +336,20 @@
     grad_far = jnp.where((preact_far > 0.0) & (mask > 0.0), r_far - grad_scale * xd_far + constant, 0.0)
     bias_grad = jnp.sum(grad_own, axis=0) + jnp.sum(grad_far, axis=0)
     gb_own, gb_far = grad_own.astype(bf16), grad_far.astype(bf16)
-    enc_grad = down(own, gb_own) + down(far, gb_far)
 
     act_sum = jnp.sum(activations.astype(f32), axis=(0, 1))
     bias_sum = jnp.sum(rounded_sum[:, None] * weights, axis=0) - act_sum
     bias_sum, recon_part = lax.optimization_barrier((bias_sum, recon_part))
     distance = 1
     while distance < count:
+        if distance == count // 2:
+            bias_sum, gb_own, gb_far = lax.optimization_barrier((bias_sum, gb_own, gb_far))
         bias_sum = bias_sum + swap(bias_sum, distance, count)
         distance *= 2
     dec_bias_grad = grad_scale * (bias_sum + float(span_count * part_rows * count) * dec_bias)
+    enc_grad = down(own, gb_own) + down(far, gb_far)
     dec_grad = join_windows(dec_part, y_in, skipped)
+
     return (enc_grad[None], bias_grad[None], dec_grad[None], dec_bias_grad)
 
 

time: 580 us -> 392 us (0.68)
  Pallas kernels: 307 us -> 31 us
  waiting for transfers between devices: 161 us -> 238 us
  blocking collectives: 28.1 us -> 0 us
  starting transfers between devices: 37.8 us -> 55.3 us
  local copies, waits for them, and re-layouts: 4.81 us -> 16 us
  other arithmetic: 6.62 us -> 14.1 us
    pallas_call x2, Pallas kernels: 226 us -> 11.5 us  [pick_spans(): pl.pallas_call(functools.partial(pick_kernel, firsts), in_specs=[pl.Block...]
    ppermute x7 -> x29, waiting for transfers between devices: 101 us -> 238 us  [swap(): return lax.ppermute(x, AXIS, [(i, i ^ distance) for i in range(count)])]
    pallas_call x1, Pallas kernels: 64.8 us -> 2.93 us  [cut_windows(): pl.pallas_call(functools.partial(window_kernel, starts), in_specs=[pl.Blo...]
    all_to_all x5 -> x4, waiting for transfers between devices: 60.1 us -> 0.01 us  [exchange(): lax.all_to_all(x, AXIS, split_axis=0, concat_axis=0, tiled=True, axis_ind...]
    all_to_all x1 -> x0, blocking collectives: 28.1 us -> none  [exchange(): lax.all_to_all(x, AXIS, split_axis=0, concat_axis=0, tiled=True, axis_ind...]
    ppermute x7 -> x29, starting transfers between devices: 8.87 us -> 32.4 us  [swap(): return lax.ppermute(x, AXIS, [(i, i ^ distance) for i in range(count)])]
    unnamed x15 -> x45, local copies, waits for them, and re-layouts: 0.16 us -> 7.43 us
    all_to_all x5 -> x4, starting transfers between devices: 28.9 us -> 23 us  [exchange(): lax.all_to_all(x, AXIS, split_axis=0, concat_axis=0, tiled=True, axis_ind...]
  transfers between devices with their start and end apart: 12 -> 33, of which waited for: 8 -> 13; matrix products, arithmetic and copies ran while one was open for 6% -> 11% of each run, Pallas kernels for 39% -> 1%
where the time goes in v3:
time: 392 us; the launch traced here: 387 us
  waiting for transfers between devices  238 us (61%)
  starting transfers between devices  55.3 us (14%)
  matrix products  31.3 us (8%)
  Pallas kernels  31 us (8%)
  local copies, waits for them, and re-layouts  16 us (4%)
  other arithmetic  14.1 us (4%)
    ppermute x29, waiting for transfers between devices, swap(): return lax.ppermute(x, AXIS, [(i, i ^ distance) for i in range(count)])  238 us
    ppermute x29, starting transfers between devices, swap(): return lax.ppermute(x, AXIS, [(i, i ^ distance) for i in range(count)])  32.4 us
    all_to_all x4, starting transfers between devices, exchange(): lax.all_to_all(x, AXIS, split_axis=0, concat_axis=0, tiled=True, axis_ind...  23 us
    pallas_call x2, Pallas kernels, pick_spans(): pl.pallas_call(functools.partial(pick_kernel, firsts), in_specs=[pl.Block...  11.5 us
    dot_general x2, matrix products, shards(): fx = down(fb_own, own) + down(fb_far, far)  10.3 us
    pallas_call x1, Pallas kernels, decode(): pl.pallas_call(functools.partial(decode_kernel, names, skipped), in_specs...  9.84 us
    dot_general x2, matrix products, shards(): enc_grad = down(own, gb_own) + down(far, gb_far)  8.35 us
  transfers between devices with their start and end apart: 33, of which 13 were waited for; matrix products, arithmetic and copies ran while one was open for 11% of the time, Pallas kernels for 1%

profile of v3, /device:TPU:15, one launch (start us, length us, event | category | flops | bytes accessed | tf_op | source)
XLA Modules:
  0.0 387.0 jit_solution(2381383268918639272)
XLA Ops:
  0.7 0.9 fusion.33
  1.9 1.5 copy-done.2
  3.4 5.7 %pick_spans.2 = bf16[16,16,7168]{2,1,0:T(8,128)(2,1)S(1)} custom-call(s32[16]{0:T(128)S(1)} %reshape.155.index_ref, bf16[8,16,7168]{2,1,0:T(8,128)(2,1)S(1)} %copy-done.2), custom_call_target="tpu_custom_call" | custom-call | bytes 5505024 | tf_op jit(solution)/shard_map/pick_spans/pallas_call | solution.py:71
  9.1 1.8 copy-done.5
  10.9 5.1 %all-to-all-start = ((bf16[8,2,16,7168]{3,2,1,0:T(8,128)(2,1)}), bf16[8,2,16,7168]{3,2,1,0:T(8,128)(2,1)}, u32[]{:S(2)}, u32[]{:S(2)}) async-start(bf16[8,2,16,7168]{3,2,1,0:T(8,128)(2,1)} %bitcast.120), calls=%async_computation | async-start | bytes 7340032 | tf_op jit(solution)/shard_map/all_to_all | solution.py:26
  16.1 2.3 slice.52
  18.4 2.3 collective-permute-start
  20.7 2.9 cut_windows.1
  23.7 59.6 %collective-permute-done.refs_0_ = bf16[5,16,7168]{2,1,0:T(8,128)(2,1)S(1)} collective-permute-done((bf16[5,16,7168]{2,1,0:T(8,128)(2,1)}, bf16[5,16,7168]{2,1,0:T(8,128)(2,1)S(1)}, u32[]{:S(2)}, u32[]{:S(2)}) %collective-permute-start) | collective-permute-done | bytes 1146912 | tf_op jit(solution)/shard_map/ppermute | solution.py:22
  83.3 4.8 %all-to-all-start.1 = ((bf16[16,128,512]{2,1,0:T(8,128)(2,1)}), bf16[16,128,512]{2,1,0:T(8,128)(2,1)}, u32[]{:S(2)}, u32[]{:S(2)}) async-start(bf16[16,128,512]{2,1,0:T(8,128)(2,1)} %cut_windows.1), calls=%async_computation.1 | async-start | bytes 4194304 | tf_op jit(solution)/shard_map/all_to_all | solution.py:26
  88.1 1.1 slice.53
  89.2 2.2 collective-permute-start.1
  91.4 71.4 %collective-permute-done.1.refs_1_ = bf16[3,16,7168]{2,1,0:T(8,128)(2,1)S(1)} collective-permute-done((bf16[3,16,7168]{2,1,0:T(8,128)(2,1)S(1)}, bf16[3,16,7168]{2,1,0:T(8,128)(2,1)S(1)}, u32[]{:S(2)}, u32[]{:S(2)}) %collective-permute-start.1) | collective-permute-done | bytes 688160 | tf_op jit(solution)/shard_map/ppermute | solution.py:22
  162.8 0.8 copy-done.6
  163.6 1.1 copy-done.7
  164.7 5.8 %pick_spans.3 = bf16[16,16,7168]{2,1,0:T(8,128)(2,1)S(1)} custom-call(s32[16]{0:T(128)S(1)} %reshape.155.index_ref, bf16[5,16,7168]{2,1,0:T(8,128)(2,1)S(1)} %collective-permute-done.refs_0_, bf16[3,16,7168]{2,1,0:T(8,128)(2,1)S(1)} %copy-done.7), custom_call_target="tpu_custom_call" | custom-call | bytes 5505024 | tf_op jit(solution)/shard_map/pick_spans/pallas_call | solution.py:71
  170.5 1.8 copy-done.4
  172.4 8.5 %all-to-all-start.2 = ((bf16[8,2,16,7168]{3,2,1,0:T(8,128)(2,1)}), bf16[8,2,16,7168]{3,2,1,0:T(8,128)(2,1)}, u32[]{:S(2)}, u32[]{:S(2)}) async-start(bf16[8,2,16,7168]{3,2,1,0:T(8,128)(2,1)} %bitcast.119), calls=%async_computation.2 | async-start | bytes 7340032 | tf_op jit(solution)/shard_map/all_to_all | solution.py:26
  181.2 3.2 convert_reduce_fusion.2
  184.8 2.3 collective-permute-start.4
  187.1 2.3 collective-permute-start.6
  189.4 33.7 %collective-permute-done.2 = bf16[2,128,128]{2,1,0:T(8,128)(2,1)S(1)} collective-permute-done((bf16[2,128,128]{2,1,0:T(8,128)(2,1)S(1)}, bf16[2,128,128]{2,1,0:T(8,128)(2,1)S(1)}, u32[]{:S(2)}, u32[]{:S(2)}) %collective-permute-start.2) | collective-permute-done | bytes 65568 | tf_op jit(solution)/shard_map/ppermute | solution.py:22
  223.2 1.5 collective-permute-done.3
  224.6 0.6 collective-permute-start.8
  225.3 0.8 collective-permute-done.4
  226.0 2.5 collective-permute-done.7
  228.6 2.2 collective-permute-done.8
  230.7 3.2 fusion.31
  233.9 1.3 collective-permute-start.9
  235.2 1.0 collective-permute-start.10
  236.2 0.9 collective-permute-start.11
  237.1 2.6 collective-permute-start.12
  240.4 2.7 collective-permute-start.14
  243.6 1.8 collective-permute-done.13
  245.4 5.9 %collective-permute-done.14 = bf16[2,128,128]{2,1,0:T(8,128)(2,1)S(1)} collective-permute-done((bf16[2,128,128]{2,1,0:T(8,128)(2,1)S(1)}, bf16[2,128,128]{2,1,0:T(8,128)(2,1)S(1)}, u32[]{:S(2)}, u32[]{:S(2)}) %collective-permute-start.14) | collective-permute-done | bytes 65568 | tf_op jit(solution)/shard_map/ppermute | solution.py:22
  251.3 1.7 collective-permute-done.15
  253.2 1.0 pad_maximum_fusion.1
  254.2 1.5 collective-permute-start.16
  255.8 2.2 bitcast_convert_fusion
  259.0 0.6 reshape.163.block_ref
  259.6 2.4 fusion.6
  262.0 2.7 pad_maximum_fusion
  264.7 9.8 %decode.1 = (bf16[32,256,128]{2,1,0:T(8,128)(2,1)}, bf16[16,128,512]{2,1,0:T(8,128)(2,1)}) custom-call(s32[24]{0:T(128)} %reshape.162.place_ref, s32[24]{0:T(128)} %reshape.163.block_ref, s32[1]{0:T(128)} %bitcast.10.core_ref, bf16[32,256,128]{2,1,0:T(8,128)(2,1)} %bitcast.124, bf16[16,128,512]{2,1,0:T(8,128)(2,1)} %all-to-all-done.1.dec_ref), custom_call_target="tpu_custom_call" | custom-call | flops 2415919104 | bytes 8388608 | tf_op jit(solution)/shard_map/decode/pallas_call | solution.py:171
  274.5 2.9 fusion.47
  277.8 1.0 multiply_reduce_fusion
  278.8 4.6 %fusion.51 = f32[128,7168]{1,0:T(8,128)} fusion(bf16[256,128]{1,0:T(8,128)(2,1)S(1)} %get-tuple-element.70, bf16[256,7168]{1,0:T(8,128)(2,1)} %bitcast.9), kind=kOutput, calls=%fused_computation.114 | convolution fusion | flops 469762048 | bytes 7405568 | tf_op jit(solution)/shard_map/dot_general | solution.py:317
  283.3 4.5 %all-to-all-start.3 = ((bf16[16,128,512]{2,1,0:T(8,128)(2,1)}), bf16[16,128,512]{2,1,0:T(8,128)(2,1)}, u32[]{:S(2)}, u32[]{:S(2)}) async-start(bf16[16,128,512]{2,1,0:T(8,128)(2,1)} %get-tuple-element.42), calls=%async_computation.3 | async-start | bytes 4194304 | tf_op jit(solution)/shard_map/all_to_all | solution.py:26
  287.9 1.7 fusion.4
  289.6 1.3 collective-permute-start.24
  290.9 0.9 collective-permute-start.23
  291.8 4.2 %collective-permute-start.22 = (bf16[2,256,128]{2,1,0:T(8,128)(2,1)S(1)}, bf16[2,256,128]{2,1,0:T(8,128)(2,1)S(1)}, u32[]{:S(2)}, u32[]{:S(2)}) collective-permute-start(bf16[2,256,128]{2,1,0:T(8,128)(2,1)S(1)} %get-tuple-element.63), channel_id=1, source_target_pairs={{0,10},{1,11},{2,8},{3,9},{4,14},{5,15},{6,12},{7,13},{8,2},{9,3},... | collective-permute-start | bytes 393224 | tf_op jit(solution)/shard_map/ppermute | solution.py:22
  296.4 52.7 %collective-permute-done.24 = bf16[2,256,128]{2,1,0:T(8,128)(2,1)S(1)} collective-permute-done((bf16[2,256,128]{2,1,0:T(8,128)(2,1)S(1)}, bf16[2,256,128]{2,1,0:T(8,128)(2,1)S(1)}, u32[]{:S(2)}, u32[]{:S(2)}) %collective-permute-start.24) | collective-permute-done | bytes 131104 | tf_op jit(solution)/shard_map/ppermute | solution.py:22
  349.1 2.9 collective-permute-done.23
  352.6 5.7 %fusion.2.part_ref = f32[128,7168]{1,0:T(8,128)} fusion(f32[128,7168]{1,0:T(8,128)S(1)} %copy-done.11, bf16[256,128]{1,0:T(8,128)(2,1)S(1)} %get-tuple-element.55, bf16[256,7168]{1,0:T(8,128)(2,1)} %bitcast.2, f32[128,3584]{1,0:T(8,128)S(1)} %broadcast_in_dim.79, f32[128,3584]{1,0:T(8,128)S(1)} %broadcast_in_dim.78, f32[128]{0:T(128)S(1)} %add_multiply_fusion.1, ...), kind=kOutput, calls=%fused_computation.3 | convolution fusion | flops 478019584 | bytes 16610304 | tf_op jit(solution)/shard_map/dot_general | solution.py:317
  358.5 1.7 collective-permute-start.25
  360.2 3.2 fusion.49
  363.4 1.3 collective-permute-start.26
  364.8 3.2 fusion.48
  367.9 0.7 collective-permute-start.27
  369.2 1.5 collective-permute-done.27
  371.3 3.2 fusion.50
  374.5 5.1 %fusion.3 = f32[1,7168,128]{2,1,0:T(8,128)} fusion(f32[7168,128]{1,0:T(8,128)S(1)} %fusion.50, bf16[256,7168]{1,0:T(8,128)(2,1)} %bitcast.2, bf16[256,128]{1,0:T(8,128)(2,1)S(1)} %get-tuple-element.40), kind=kOutput, calls=%fused_computation.5 | convolution fusion | flops 470679552 | bytes 11075584 | tf_op jit(solution)/shard_map/dot_general | solution.py:350
  379.6 0.6 add_multiply_fusion
  380.3 6.7 %join_windows.1 = f32[128,7168]{1,0:T(8,128)} custom-call(f32[128,7168]{1,0:T(8,128)} %fusion.2.part_ref, bf16[16,128,512]{2,1,0:T(8,128)(2,1)} %all-to-all-done.3.y_ref), custom_call_target="tpu_custom_call" | custom-call | tf_op jit(solution)/shard_map/join_windows/pallas_call | solution.py:122
  (109 shorter events, 6.1 us)
Async XLA Ops:
  0.6 180.6 %copy-start = (bf16[1,7168,128]{2,1,0:T(8,128)(2,1)S(1)}, bf16[1,7168,128]{2,1,0:T(8,128)(2,1)}, u32[]{:S(2)}) copy-start(bf16[1,7168,128]{2,1,0:T(8,128)(2,1)} %param.7) | copy-start | bytes 5505028
  1.9 1.5 copy-start.2
  9.1 1.8 copy-start.5
  10.9 72.3 %all-to-all-start = ((bf16[8,2,16,7168]{3,2,1,0:T(8,128)(2,1)}), bf16[8,2,16,7168]{3,2,1,0:T(8,128)(2,1)}, u32[]{:S(2)}, u32[]{:S(2)}) async-start(bf16[8,2,16,7168]{3,2,1,0:T(8,128)(2,1)} %bitcast.120), calls=%async_computation | async-start | bytes 7340032 | tf_op jit(solution)/shard_map/all_to_all | solution.py:26
  18.4 64.9 %collective-permute-start = (bf16[5,16,7168]{2,1,0:T(8,128)(2,1)}, bf16[5,16,7168]{2,1,0:T(8,128)(2,1)S(1)}, u32[]{:S(2)}, u32[]{:S(2)}) collective-permute-start(bf16[5,16,7168]{2,1,0:T(8,128)(2,1)} %slice.52), channel_id=1, source_target_pairs={{0,8},{1,9},{2,10},{3,11},{4,12},{5,13},{6,14},{7,15},{8,0},{9,1},... | collective-permute-start | bytes 3440648 | tf_op jit(solution)/shard_map/ppermute | solution.py:22
  83.3 80.4 %all-to-all-start.1 = ((bf16[16,128,512]{2,1,0:T(8,128)(2,1)}), bf16[16,128,512]{2,1,0:T(8,128)(2,1)}, u32[]{:S(2)}, u32[]{:S(2)}) async-start(bf16[16,128,512]{2,1,0:T(8,128)(2,1)} %cut_windows.1), calls=%async_computation.1 | async-start | bytes 4194304 | tf_op jit(solution)/shard_map/all_to_all | solution.py:26
  89.2 73.6 %collective-permute-start.1 = (bf16[3,16,7168]{2,1,0:T(8,128)(2,1)S(1)}, bf16[3,16,7168]{2,1,0:T(8,128)(2,1)S(1)}, u32[]{:S(2)}, u32[]{:S(2)}) collective-permute-start(bf16[3,16,7168]{2,1,0:T(8,128)(2,1)S(1)} %slice.53), channel_id=1, source_target_pairs={{0,8},{1,9},{2,10},{3,11},{4,12},{5,13},{6,14},{7,15},{8,0},{9,1},... | collective-permute-start | bytes 2064392 | tf_op jit(solution)/shard_map/ppermute | solution.py:22
  162.8 0.8 copy-start.6
  163.6 1.1 copy-start.7
  170.5 1.8 copy-start.4
  172.4 8.8 %copy-start.14 = (f32[1,128]{1,0:T(1,128)S(1)}, f32[1,128]{1,0:T(1,128)}, u32[]{:S(2)}) copy-start(f32[1,128]{1,0:T(1,128)} %param.8) | copy-start | bytes 1540
  172.4 58.4 %all-to-all-start.2 = ((bf16[8,2,16,7168]{3,2,1,0:T(8,128)(2,1)}), bf16[8,2,16,7168]{3,2,1,0:T(8,128)(2,1)}, u32[]{:S(2)}, u32[]{:S(2)}) async-start(bf16[8,2,16,7168]{3,2,1,0:T(8,128)(2,1)} %bitcast.119), calls=%async_computation.2 | async-start | bytes 7340032 | tf_op jit(solution)/shard_map/all_to_all | solution.py:26
  184.4 38.8 %collective-permute-start.2 = (bf16[2,128,128]{2,1,0:T(8,128)(2,1)S(1)}, bf16[2,128,128]{2,1,0:T(8,128)(2,1)S(1)}, u32[]{:S(2)}, u32[]{:S(2)}) collective-permute-start(bf16[2,128,128]{2,1,0:T(8,128)(2,1)S(1)} %bitcast.139), channel_id=1, source_target_pairs={{0,2},{1,3},{2,0},{3,1},{4,6},{5,7},{6,4},{7,5},{8,10},{9,11},{10,... | collective-permute-start | bytes 196616 | tf_op jit(solution)/shard_map/ppermute | solution.py:22
  184.7 39.9 %collective-permute-start.3 = (bf16[2,128,128]{2,1,0:T(8,128)(2,1)S(1)}, bf16[2,128,128]{2,1,0:T(8,128)(2,1)S(1)}, u32[]{:S(2)}, u32[]{:S(2)}) collective-permute-start(bf16[2,128,128]{2,1,0:T(8,128)(2,1)S(1)} %bitcast.140), channel_id=1, source_target_pairs={{0,4},{1,5},{2,6},{3,7},{4,0},{5,1},{6,2},{7,3},{8,12},{9,13},{10,... | collective-permute-start | bytes 196616 | tf_op jit(solution)/shard_map/ppermute | solution.py:22
  184.8 41.2 %collective-permute-start.4 = (bf16[2,128,128]{2,1,0:T(8,128)(2,1)S(1)}, bf16[2,128,128]{2,1,0:T(8,128)(2,1)S(1)}, u32[]{:S(2)}, u32[]{:S(2)}) collective-permute-start(bf16[2,128,128]{2,1,0:T(8,128)(2,1)S(1)} %bitcast.141), channel_id=1, source_target_pairs={{0,6},{1,7},{2,4},{3,5},{4,2},{5,3},{6,0},{7,1},{8,14},{9,15},{10,... | collective-permute-start | bytes 196616 | tf_op jit(solution)/shard_map/ppermute | solution.py:22
  187.1 38.9 %collective-permute-start.5 = (bf16[2,128,128]{2,1,0:T(8,128)(2,1)S(1)}, bf16[2,128,128]{2,1,0:T(8,128)(2,1)S(1)}, u32[]{:S(2)}, u32[]{:S(2)}) collective-permute-start(bf16[2,128,128]{2,1,0:T(8,128)(2,1)S(1)} %bitcast.142), channel_id=1, source_target_pairs={{0,8},{1,9},{2,10},{3,11},{4,12},{5,13},{6,14},{7,15},{8,0},{9,1},... | collective-permute-start | bytes 196616 | tf_op jit(solution)/shard_map/ppermute | solution.py:22
  187.1 38.9 %collective-permute-start.6 = (bf16[2,128,128]{2,1,0:T(8,128)(2,1)S(1)}, bf16[2,128,128]{2,1,0:T(8,128)(2,1)S(1)}, u32[]{:S(2)}, u32[]{:S(2)}) collective-permute-start(bf16[2,128,128]{2,1,0:T(8,128)(2,1)S(1)} %bitcast.143), channel_id=1, source_target_pairs={{0,10},{1,11},{2,8},{3,9},{4,14},{5,15},{6,12},{7,13},{8,2},{9,3},... | collective-permute-start | bytes 196616 | tf_op jit(solution)/shard_map/ppermute | solution.py:22
  223.2 5.4 %collective-permute-start.7 = (bf16[2,128,128]{2,1,0:T(8,128)(2,1)S(1)}, bf16[2,128,128]{2,1,0:T(8,128)(2,1)S(1)}, u32[]{:S(2)}, u32[]{:S(2)}) collective-permute-start(bf16[2,128,128]{2,1,0:T(8,128)(2,1)S(1)} %bitcast.144), channel_id=1, source_target_pairs={{0,12},{1,13},{2,14},{3,15},{4,8},{5,9},{6,10},{7,11},{8,4},{9,5},... | collective-permute-start | bytes 196616 | tf_op jit(solution)/shard_map/ppermute | solution.py:22
  224.6 6.1 %collective-permute-start.8 = (bf16[2,128,128]{2,1,0:T(8,128)(2,1)S(1)}, bf16[2,128,128]{2,1,0:T(8,128)(2,1)S(1)}, u32[]{:S(2)}, u32[]{:S(2)}) collective-permute-start(bf16[2,128,128]{2,1,0:T(8,128)(2,1)S(1)} %bitcast.145), channel_id=1, source_target_pairs={{0,14},{1,15},{2,12},{3,13},{4,10},{5,11},{6,8},{7,9},{8,6},{9,7},... | collective-permute-start | bytes 196616 | tf_op jit(solution)/shard_map/ppermute | solution.py:22
  233.9 21.9 %copy-start.8 = (bf16[1,128,7168]{2,1,0:T(8,128)(2,1)S(1)}, bf16[1,128,7168]{2,1,0:T(8,128)(2,1)}, u32[]{:S(2)}) copy-start(bf16[1,128,7168]{2,1,0:T(8,128)(2,1)} %param.9) | copy-start | bytes 5505028
  233.9 6.5 %collective-permute-start.9 = (bf16[2,128,128]{2,1,0:T(8,128)(2,1)S(1)}, bf16[2,128,128]{2,1,0:T(8,128)(2,1)S(1)}, u32[]{:S(2)}, u32[]{:S(2)}) collective-permute-start(bf16[2,128,128]{2,1,0:T(8,128)(2,1)S(1)} %bitcast.131), channel_id=1, source_target_pairs={{0,2},{1,3},{2,0},{3,1},{4,6},{5,7},{6,4},{7,5},{8,10},{9,11},{10,... | collective-permute-start | bytes 196616 | tf_op jit(solution)/shard_map/ppermute | solution.py:22
  235.2 7.9 %collective-permute-start.10 = (bf16[2,128,128]{2,1,0:T(8,128)(2,1)S(1)}, bf16[2,128,128]{2,1,0:T(8,128)(2,1)S(1)}, u32[]{:S(2)}, u32[]{:S(2)}) collective-permute-start(bf16[2,128,128]{2,1,0:T(8,128)(2,1)S(1)} %bitcast.132), channel_id=1, source_target_pairs={{0,4},{1,5},{2,6},{3,7},{4,0},{5,1},{6,2},{7,3},{8,12},{9,13},{10,... | collective-permute-start | bytes 196616 | tf_op jit(solution)/shard_map/ppermute | solution.py:22
  236.2 7.3 %collective-permute-start.11 = (bf16[2,128,128]{2,1,0:T(8,128)(2,1)S(1)}, bf16[2,128,128]{2,1,0:T(8,128)(2,1)S(1)}, u32[]{:S(2)}, u32[]{:S(2)}) collective-permute-start(bf16[2,128,128]{2,1,0:T(8,128)(2,1)S(1)} %bitcast.133), channel_id=1, source_target_pairs={{0,6},{1,7},{2,4},{3,5},{4,2},{5,3},{6,0},{7,1},{8,14},{9,15},{10,... | collective-permute-start | bytes 196616 | tf_op jit(solution)/shard_map/ppermute | solution.py:22
  237.1 6.5 %collective-permute-start.12 = (bf16[2,128,128]{2,1,0:T(8,128)(2,1)S(1)}, bf16[2,128,128]{2,1,0:T(8,128)(2,1)S(1)}, u32[]{:S(2)}, u32[]{:S(2)}) collective-permute-start(bf16[2,128,128]{2,1,0:T(8,128)(2,1)S(1)} %bitcast.134), channel_id=1, source_target_pairs={{0,8},{1,9},{2,10},{3,11},{4,12},{5,13},{6,14},{7,15},{8,0},{9,1},... | collective-permute-start | bytes 196616 | tf_op jit(solution)/shard_map/ppermute | solution.py:22
  239.7 5.7 %collective-permute-start.13 = (bf16[2,128,128]{2,1,0:T(8,128)(2,1)S(1)}, bf16[2,128,128]{2,1,0:T(8,128)(2,1)S(1)}, u32[]{:S(2)}, u32[]{:S(2)}) collective-permute-start(bf16[2,128,128]{2,1,0:T(8,128)(2,1)S(1)} %bitcast.135), channel_id=1, source_target_pairs={{0,10},{1,11},{2,8},{3,9},{4,14},{5,15},{6,12},{7,13},{8,2},{9,3},... | collective-permute-start | bytes 196616 | tf_op jit(solution)/shard_map/ppermute | solution.py:22
  240.4 10.9 %collective-permute-start.14 = (bf16[2,128,128]{2,1,0:T(8,128)(2,1)S(1)}, bf16[2,128,128]{2,1,0:T(8,128)(2,1)S(1)}, u32[]{:S(2)}, u32[]{:S(2)}) collective-permute-start(bf16[2,128,128]{2,1,0:T(8,128)(2,1)S(1)} %bitcast.137), channel_id=1, source_target_pairs={{0,12},{1,13},{2,14},{3,15},{4,8},{5,9},{6,10},{7,11},{8,4},{9,5},... | collective-permute-start | bytes 196616 | tf_op jit(solution)/shard_map/ppermute | solution.py:22
  243.1 9.9 %collective-permute-start.15 = (bf16[2,128,128]{2,1,0:T(8,128)(2,1)S(1)}, bf16[2,128,128]{2,1,0:T(8,128)(2,1)S(1)}, u32[]{:S(2)}, u32[]{:S(2)}) collective-permute-start(bf16[2,128,128]{2,1,0:T(8,128)(2,1)S(1)} %bitcast.138), channel_id=1, source_target_pairs={{0,14},{1,15},{2,12},{3,13},{4,10},{5,11},{6,8},{7,9},{8,6},{9,7},... | collective-permute-start | bytes 196616 | tf_op jit(solution)/shard_map/ppermute | solution.py:22
  253.2 4.8 %copy-start.13 = (s32[8,3]{0,1:T(4,128)S(1)}, s32[8,3]{0,1:T(4,128)}, u32[]{:S(2)}) copy-start(s32[8,3]{0,1:T(4,128)} %param.11) | copy-start | bytes 292
  254.2 7.7 %collective-permute-start.16 = (bf16[8,2,256,128]{3,2,1,0:T(8,128)(2,1)}, bf16[8,2,256,128]{3,2,1,0:T(8,128)(2,1)}, u32[]{:S(2)}, u32[]{:S(2)}) collective-permute-start(bf16[8,2,256,128]{3,2,1,0:T(8,128)(2,1)} %pad_maximum_fusion.1), channel_id=1, source_target_pairs={{0,1},{1,0},{2,3},{3,2},{4,5},{5,4},{6,7},{7,6},{8,9},{9,8},{10,11... | collective-permute-start | bytes 3145736 | tf_op jit(solution)/shard_map/ppermute | solution.py:22
  274.5 2.9 copy-start.3
  274.5 3.2 copy-start.9
  274.5 3.2 copy-start.12
  277.4 10.4 %collective-permute-start.17 = (bf16[8,2,256,128]{3,2,1,0:T(8,128)(2,1)}, bf16[8,2,256,128]{3,2,1,0:T(8,128)(2,1)}, u32[]{:S(2)}, u32[]{:S(2)}) collective-permute-start(bf16[8,2,256,128]{3,2,1,0:T(8,128)(2,1)} %bitcast.33), channel_id=1, source_target_pairs={{0,1},{1,0},{2,3},{3,2},{4,5},{5,4},{6,7},{7,6},{8,9},{9,8},{10,11... | collective-permute-start | bytes 3145736 | tf_op jit(solution)/shard_map/ppermute | solution.py:22
  283.3 96.9 %all-to-all-start.3 = ((bf16[16,128,512]{2,1,0:T(8,128)(2,1)}), bf16[16,128,512]{2,1,0:T(8,128)(2,1)}, u32[]{:S(2)}, u32[]{:S(2)}) async-start(bf16[16,128,512]{2,1,0:T(8,128)(2,1)} %get-tuple-element.42), calls=%async_computation.3 | async-start | bytes 4194304 | tf_op jit(solution)/shard_map/all_to_all | solution.py:26
  287.9 64.7 %copy-start.10 = (bf16[1,128,7168]{2,1,0:T(8,128)(2,1)S(1)}, bf16[1,128,7168]{2,1,0:T(8,128)(2,1)}, u32[]{:S(2)}) copy-start(bf16[1,128,7168]{2,1,0:T(8,128)(2,1)} %param.9) | copy-start | bytes 5505028
  287.9 64.7 %copy-start.11 = (f32[128,7168]{1,0:T(8,128)S(1)}, f32[128,7168]{1,0:T(8,128)}, u32[]{:S(2)}) copy-start(f32[128,7168]{1,0:T(8,128)} %fusion.51) | copy-start | bytes 11010052
  289.6 59.5 %collective-permute-start.24 = (bf16[2,256,128]{2,1,0:T(8,128)(2,1)S(1)}, bf16[2,256,128]{2,1,0:T(8,128)(2,1)S(1)}, u32[]{:S(2)}, u32[]{:S(2)}) collective-permute-start(bf16[2,256,128]{2,1,0:T(8,128)(2,1)S(1)} %get-tuple-element.61), channel_id=1, source_target_pairs={{0,14},{1,15},{2,12},{3,13},{4,10},{5,11},{6,8},{7,9},{8,6},{9,7},... | collective-permute-start | bytes 393224 | tf_op jit(solution)/shard_map/ppermute | solution.py:22
  290.9 61.1 %collective-permute-start.23 = (bf16[2,256,128]{2,1,0:T(8,128)(2,1)S(1)}, bf16[2,256,128]{2,1,0:T(8,128)(2,1)S(1)}, u32[]{:S(2)}, u32[]{:S(2)}) collective-permute-start(bf16[2,256,128]{2,1,0:T(8,128)(2,1)S(1)} %get-tuple-element.62), channel_id=1, source_target_pairs={{0,12},{1,13},{2,14},{3,15},{4,8},{5,9},{6,10},{7,11},{8,4},{9,5},... | collective-permute-start | bytes 393224 | tf_op jit(solution)/shard_map/ppermute | solution.py:22
  291.8 66.6 %collective-permute-start.22 = (bf16[2,256,128]{2,1,0:T(8,128)(2,1)S(1)}, bf16[2,256,128]{2,1,0:T(8,128)(2,1)S(1)}, u32[]{:S(2)}, u32[]{:S(2)}) collective-permute-start(bf16[2,256,128]{2,1,0:T(8,128)(2,1)S(1)} %get-tuple-element.63), channel_id=1, source_target_pairs={{0,10},{1,11},{2,8},{3,9},{4,14},{5,15},{6,12},{7,13},{8,2},{9,3},... | collective-permute-start | bytes 393224 | tf_op jit(solution)/shard_map/ppermute | solution.py:22
  296.0 62.3 %collective-permute-start.21 = (bf16[2,256,128]{2,1,0:T(8,128)(2,1)S(1)}, bf16[2,256,128]{2,1,0:T(8,128)(2,1)S(1)}, u32[]{:S(2)}, u32[]{:S(2)}) collective-permute-start(bf16[2,256,128]{2,1,0:T(8,128)(2,1)S(1)} %get-tuple-element.64), channel_id=1, source_target_pairs={{0,8},{1,9},{2,10},{3,11},{4,12},{5,13},{6,14},{7,15},{8,0},{9,1},... | collective-permute-start | bytes 393224 | tf_op jit(solution)/shard_map/ppermute | solution.py:22
  296.0 62.3 %collective-permute-start.20 = (bf16[2,256,128]{2,1,0:T(8,128)(2,1)S(1)}, bf16[2,256,128]{2,1,0:T(8,128)(2,1)S(1)}, u32[]{:S(2)}, u32[]{:S(2)}) collective-permute-start(bf16[2,256,128]{2,1,0:T(8,128)(2,1)S(1)} %get-tuple-element.65), channel_id=1, source_target_pairs={{0,6},{1,7},{2,4},{3,5},{4,2},{5,3},{6,0},{7,1},{8,14},{9,15},{10,... | collective-permute-start | bytes 393224 | tf_op jit(solution)/shard_map/ppermute | solution.py:22
  349.1 9.2 %collective-permute-start.19 = (bf16[2,256,128]{2,1,0:T(8,128)(2,1)S(1)}, bf16[2,256,128]{2,1,0:T(8,128)(2,1)S(1)}, u32[]{:S(2)}, u32[]{:S(2)}) collective-permute-start(bf16[2,256,128]{2,1,0:T(8,128)(2,1)S(1)} %get-tuple-element.66), channel_id=1, source_target_pairs={{0,4},{1,5},{2,6},{3,7},{4,0},{5,1},{6,2},{7,3},{8,12},{9,13},{10,... | collective-permute-start | bytes 393224 | tf_op jit(solution)/shard_map/ppermute | solution.py:22
  352.0 6.4 %collective-permute-start.18 = (bf16[2,256,128]{2,1,0:T(8,128)(2,1)S(1)}, bf16[2,256,128]{2,1,0:T(8,128)(2,1)S(1)}, u32[]{:S(2)}, u32[]{:S(2)}) collective-permute-start(bf16[2,256,128]{2,1,0:T(8,128)(2,1)S(1)} %get-tuple-element.60), channel_id=1, source_target_pairs={{0,2},{1,3},{2,0},{3,1},{4,6},{5,7},{6,4},{7,5},{8,10},{9,11},{10,... | collective-permute-start | bytes 393224 | tf_op jit(solution)/shard_map/ppermute | solution.py:22
  358.5 4.9 %collective-permute-start.25 = (f32[7168]{0:T(1024)S(1)}, f32[7168]{0:T(1024)S(1)}, u32[]{:S(2)}, u32[]{:S(2)}) collective-permute-start(f32[7168]{0:T(1024)S(1)} %sub.36), channel_id=1, source_target_pairs={{0,1},{1,0},{2,3},{3,2},{4,5},{5,4},{6,7},{7,6},{8,9},{9,8},{10,11... | collective-permute-start | bytes 86024 | tf_op jit(solution)/shard_map/ppermute | solution.py:22
  363.4 4.5 %collective-permute-start.26 = (f32[7168]{0:T(1024)S(1)}, f32[7168]{0:T(1024)S(1)}, u32[]{:S(2)}, u32[]{:S(2)}) collective-permute-start(f32[7168]{0:T(1024)S(1)} %add.185), channel_id=1, source_target_pairs={{0,2},{1,3},{2,0},{3,1},{4,6},{5,7},{6,4},{7,5},{8,10},{9,11},{10,... | collective-permute-start | bytes 86024 | tf_op jit(solution)/shard_map/ppermute | solution.py:22
  367.9 2.8 collective-permute-start.27
  370.7 8.9 %collective-permute-start.28 = (f32[7168]{0:T(1024)S(1)}, f32[7168]{0:T(1024)S(1)}, u32[]{:S(2)}, u32[]{:S(2)}) collective-permute-start(f32[7168]{0:T(1024)S(1)} %add.187), channel_id=1, source_target_pairs={{0,8},{1,9},{2,10},{3,11},{4,12},{5,13},{6,14},{7,15},{8,0},{9,1},... | collective-permute-start | bytes 86024 | tf_op jit(solution)/shard_map/ppermute | solution.py:22
  379.6 7.4 %copy-start.1 = (bf16[1,7168,128]{2,1,0:T(8,128)(2,1)S(1)}, bf16[1,7168,128]{2,1,0:T(8,128)(2,1)}, u32[]{:S(2)}) copy-start(bf16[1,7168,128]{2,1,0:T(8,128)(2,1)} %param.7) | copy-start | bytes 5505028

commit v4 on v2

--- a/solution.py
+++ b/solution.py
@@ -61,12 +61,74 @@
     shape = (index.shape[0],) + rows.shape[1:]
     return pl.pallas_call(
         pick_kernel,
-        in_specs=[pl.BlockSpec(memory_space=pltpu.SMEM), pl.BlockSpec(memory_space=pl.ANY)],
+        in_specs=[
+            pl.BlockSpec(memory_space=pltpu.SMEM),
+            pl.BlockSpec(memory_space=pltpu.VMEM),
+        ],
         out_specs=pl.BlockSpec(memory_space=pl.ANY),
         out_shape=jax.ShapeDtypeStruct(shape, rows.dtype),
         scratch_shapes=[pltpu.SemaphoreType.DMA((shape[0],))],
+        compiler_params=pltpu.CompilerParams(vmem_limit_bytes=48 * 2**20),
+        cost_estimate=pl.CostEstimate(flops=0, bytes_accessed=6 * rows.size, transcendentals=0),
         name="pick_spans",
     )(index, rows)
+
+
+def deal_kernel(index_ref, rows_ref, *refs):
+    outs, sems = refs[:-1], refs[-1]
+    copies = [
+        pltpu.make_async_copy(rows_ref.at[index_ref[i * MOST + slot]], out.at[slot], sems.at[i, slot])
+        for i, out in enumerate(outs)
+        for slot in range(MOST)
+    ]
+    for copy in copies:
+        copy.start()
+    for copy in copies:
+        copy.wait()
+
+
+def deal_spans(rows, index):
+    parts = index.shape[0] // MOST
+    vmem = pl.BlockSpec(memory_space=pltpu.VMEM)
+    return pl.pallas_call(
+        deal_kernel,
+        in_specs=[pl.BlockSpec(memory_space=pltpu.SMEM), vmem],
+        out_specs=[vmem] * parts,
+        out_shape=[jax.ShapeDtypeStruct((MOST,) + rows.shape[1:], rows.dtype)] * parts,
+        scratch_shapes=[pltpu.SemaphoreType.DMA((parts, MOST))],
+        compiler_params=pltpu.CompilerParams(vmem_limit_bytes=48 * 2**20),
+        cost_estimate=pl.CostEstimate(flops=0, bytes_accessed=6 * rows.size, transcendentals=0),
+        name="deal_spans",
+    )(index, rows)
+
+
+def gather_kernel(place_ref, *refs):
+    parts, out_ref, sems = refs[:-2], refs[-2], refs[-1]
+    copies = [
+        pltpu.make_async_copy(part, out_ref.at[i ^ place_ref[0]], sems.at[i])
+        for i, part in enumerate(parts)
+    ]
+    for copy in copies:
+        copy.start()
+    for copy in copies:
+        copy.wait()
+
+
+def gather_rows(parts, place):
+    count = len(parts)
+    return pl.pallas_call(
+        gather_kernel,
+        in_specs=[pl.BlockSpec(memory_space=pltpu.SMEM)]
+        + [pl.BlockSpec(memory_space=pltpu.VMEM)] * count,
+        out_specs=pl.BlockSpec(memory_space=pl.ANY),
+        out_shape=jax.ShapeDtypeStruct((count,) + parts[0].shape, parts[0].dtype),
+        scratch_shapes=[pltpu.SemaphoreType.DMA((count,))],
+        compiler_params=pltpu.CompilerParams(vmem_limit_bytes=48 * 2**20),
+        cost_estimate=pl.CostEstimate(
+            flops=0, bytes_accessed=4 * count * parts[0].size, transcendentals=0
+        ),
+        name="gather_rows",
+    )(place, *parts)
 
 
 def window_kernel(starts, dec_ref, out_ref, sems):
@@ -86,10 +148,11 @@
         return jnp.stack([dec[:, s : s + window] for s in starts])
     return pl.pallas_call(
         functools.partial(window_kernel, starts),
-        in_specs=[pl.BlockSpec(memory_space=pl.ANY)],
+        in_specs=[pl.BlockSpec(memory_space=pltpu.VMEM)],
         out_specs=pl.BlockSpec(memory_space=pl.ANY),
         out_shape=jax.ShapeDtypeStruct((len(starts), dec.shape[0], window), dec.dtype),
         scratch_shapes=[pltpu.SemaphoreType.DMA((len(starts),))],
+        cost_estimate=pl.CostEstimate(flops=0, bytes_accessed=4 * dec.size, transcendentals=0),
         name="cut_windows",
     )(dec)
 
@@ -119,9 +182,10 @@
     )(part, y)
 
 
-def decode_kernel(names, skipped, place_ref, block_ref, core_ref, feat_ref, dec_ref, r_ref, y_ref, total, feats, decs):
+def decode_kernel(names, skipped, place_ref, land_ref, block_ref, mine_ref, *refs):
+    own_refs, far_refs, dec_ref, r_ref, y_ref, total, feats, decs = refs[:2], refs[2:4], *refs[4:]
     span_count = place_ref.shape[0] // names
-    latents = feat_ref.shape[-1]
+    chips, most, rows, latents = own_refs[0].shape
     r_ref[...] = jnp.zeros_like(r_ref)
     total[...] = jnp.zeros_like(total)
 
@@ -129,12 +193,23 @@
         at = [place_ref[span * names + name] for name in range(names)]
         block = [block_ref[span * names + name] for name in range(names)]
         for name in range(names):
-            feats[:, name * latents : (name + 1) * latents] = feat_ref[at[name]]
-            decs[name * latents : (name + 1) * latents, :] = dec_ref[block[name]]
+            cols = slice(name * latents, (name + 1) * latents)
+            slot = at[name] % most
+            chip = at[name] // most % chips
+            lower = (chip < chips // 2) == (mine_ref[1] == 0)
+            first = pl.multiple_of(jnp.where(lower, 0, rows), rows)
+            for core in range(2):
+
+                @pl.when(at[name] // (most * chips) == core)
+                def _():
+                    feats[pl.ds(first, rows), cols] = own_refs[core][chip, slot]
+                    feats[pl.ds(rows - first, rows), cols] = far_refs[core][chip, slot]
+
+            decs[cols, :] = dec_ref[block[name]]
         scaled = jnp.dot(feats[...], decs[...], preferred_element_type=f32) * grad_scale
         if skipped:
             lane = lax.broadcasted_iota(jnp.int32, scaled.shape, 1)
-            scaled = jnp.where(lane >= core_ref[0] * skipped, scaled, 0.0)
+            scaled = jnp.where(lane >= mine_ref[0] * skipped, scaled, 0.0)
         delta = scaled.astype(bf16)
         part = lax.dot_general(
             delta, decs[...], (((1,), (1,)), ((), ())), preferred_element_type=f32
@@ -143,7 +218,7 @@
             feats[...], delta, (((0,), (0,)), ((), ())), preferred_element_type=f32
         )
         for name in range(names):
-            r_ref[at[name]] = part[:, name * latents : (name + 1) * latents]
+            r_ref[land_ref[span * names + name]] = part[:, name * latents : (name + 1) * latents]
             total[block[name]] += grad[name * latents : (name + 1) * latents]
         return carry
 
@@ -151,39 +226,48 @@
     y_ref[...] = total[...].astype(bf16)
 
 
-def decode(names, skipped, place, block, core, feats, dec):
+def decode(names, skipped, place, land, block, mine, own, far, dec):
     vmem = pl.BlockSpec(memory_space=pltpu.VMEM)
     smem = pl.BlockSpec(memory_space=pltpu.SMEM)
-    pairs, rows, latents, columns = place.shape[0], feats.shape[1], feats.shape[2], dec.shape[2]
+    pairs, columns = place.shape[0], dec.shape[2]
+    chips, most, rows, latents = own[0].shape
     return pl.pallas_call(
         functools.partial(decode_kernel, names, skipped),
-        in_specs=[smem, smem, smem, vmem, vmem],
+        in_specs=[smem] * 4 + [vmem] * 5,
         out_specs=[vmem, vmem],
         out_shape=[
-            jax.ShapeDtypeStruct(feats.shape, bf16),
+            jax.ShapeDtypeStruct((2 * chips * most, 2 * rows, latents), bf16),
             jax.ShapeDtypeStruct(dec.shape, bf16),
         ],
         scratch_shapes=[
             pltpu.VMEM(dec.shape, f32),
-            pltpu.VMEM((rows, names * latents), bf16),
+            pltpu.VMEM((2 * rows, names * latents), bf16),
             pltpu.VMEM((names * latents, columns), bf16),
         ],
         compiler_params=pltpu.CompilerParams(vmem_limit_bytes=56 * 2**20),
         cost_estimate=pl.CostEstimate(
-            flops=6 * pairs * rows * latents * columns,
-            bytes_accessed=4 * (feats.size + dec.size),
+            flops=12 * pairs * rows * latents * columns,
+            bytes_accessed=4 * (8 * own[0].size + dec.size),
             transcendentals=0,
         ),
         name="decode",
-    )(place, block, core, feats, dec)
-
-
-def decode_plain(names, skipped, place, block, core, feats, dec):
+    )(place, land, block, mine, *own, *far, dec)
+
+
+def decode_plain(names, skipped, place, land, block, mine, own, far, dec):
     span_count = place.shape[0] // names
+    chips, most, rows, latents = own[0].shape
+    lower = ((jnp.arange(chips) < chips // 2) == (mine[1] == 0))[:, None, None, None]
+    feats = jnp.concatenate(
+        [
+            jnp.concatenate([jnp.where(lower, a, b), jnp.where(lower, b, a)], axis=2)
+            for a, b in zip(own, far)
+        ]
+    ).reshape(-1, 2 * rows, latents)
     r_out = jnp.zeros(feats.shape, bf16)
     total = jnp.zeros(dec.shape, f32)
     width = dec.shape[-1]
-    keep = (jnp.arange(width) >= core[0] * skipped).astype(f32)
+    keep = (jnp.arange(width) >= mine[0] * skipped).astype(f32)
 
     def span_step(span, carry):
         r_out, total = carry
@@ -195,7 +279,8 @@
         delta = (recon * grad_scale * keep).astype(bf16)
         part = jnp.einsum("rc,klc->krl", delta, mine, preferred_element_type=f32)
         grad = jnp.einsum("krl,rc->klc", feat, delta, preferred_element_type=f32)
-        return r_out.at[at].set(part.astype(bf16)), total.at[which].add(grad)
+        to = lax.dynamic_slice(land, (span * names,), (names,))
+        return r_out.at[to].set(part.astype(bf16)), total.at[which].add(grad)
 
     r_out, total = lax.fori_loop(0, span_count, span_step, (r_out, total))
     return r_out, total.astype(bf16)
@@ -222,27 +307,16 @@
         window = per_chip // 2
     skipped = 2 * window - per_chip
     starts = [(i // 2) * per_chip + (i % 2) * (per_chip - window) for i in range(count)]
-    dec_all = exchange(cut_windows(dec, starts, window))
-
+
+    shape = (half, MOST, part_rows)
     mine = lax.dynamic_slice(span_of, (my_half * half, 0), (half, MOST)).reshape(-1)
     across = swap(activations, half, count)
-    shape = (half, MOST, part_rows)
-    near, dec_all = lax.optimization_barrier((pick_spans(activations, mine), dec_all))
-    x_own = exchange(near.reshape(shape + (width,)), halves)
-    across, x_own = lax.optimization_barrier((pick_spans(across, mine), x_own))
-    x_far = exchange(across.reshape(shape + (width,)), halves)
+    x_own = exchange(pick_spans(activations, mine).reshape(shape + (width,)), halves)
 
     rows = half * MOST * part_rows
-    own = x_own.reshape(rows, width)
-    far = x_far.reshape(rows, width)
     dot = functools.partial(jnp.dot, preferred_element_type=f32)
-    preact_own = dot(own, enc) + enc_bias[0]
-    preact_far = dot(far, enc) + enc_bias[0]
     my_live = lax.dynamic_slice(live, (me, 0), (1, MOST)).astype(f32)
     mask = jnp.broadcast_to(my_live[0][None, :, None, None], shape + (1,)).reshape(rows, 1)
-    feat_own = jnp.maximum(preact_own, 0.0) * mask
-    feat_far = jnp.maximum(preact_far, 0.0) * mask
-    fb_own, fb_far = feat_own.astype(bf16), feat_far.astype(bf16)
 
     def by_slot(x):
         return x.reshape(half, MOST, part_rows, latents).transpose(1, 0, 2, 3).reshape(MOST, -1, latents)
@@ -250,26 +324,38 @@
     def by_source(x):
         return x.reshape(MOST, half, part_rows, latents).transpose(1, 0, 2, 3).reshape(rows, latents)
 
+    def encode(x):
+        preact = dot(x, enc) + enc_bias[0]
+        feat = jnp.maximum(preact, 0.0) * mask
+        return preact, feat, feat.astype(bf16)
+
+    def spread(x):
+        same = [x] + [swap(x, 2 * i, count) for i in range(1, chips)]
+        return same
+
+    def to_both(x):
+        same = jnp.stack(x)
+        return same, swap(same, 1, count)
+
+    own = x_own.reshape(rows, width)
+    preact_own, feat_own, fb_own = encode(own)
+    all_own = to_both(spread(by_slot(fb_own)))
+    across, *all_own = lax.optimization_barrier((across, *all_own))
+    theirs = span_of[me ^ jnp.arange(half)].reshape(-1)
+    parts = deal_spans(across, theirs)
+    dec_all = exchange(cut_windows(dec, starts, window))
+    parts = [parts[0]] + [swap(parts[i], i, count) for i in range(1, half)]
+    barred = lax.optimization_barrier((dec_all, *parts))
+    dec_all, parts = barred[0], barred[1:]
+    far = gather_rows(parts, (me % half).reshape(1)).reshape(rows, width)
+    preact_far, feat_far, fb_far = encode(far)
+    all_far = to_both(spread(by_slot(fb_far)))
+
     lower = my_half == 0
-    a, b = by_slot(fb_own), by_slot(fb_far)
-    feats = jnp.concatenate([jnp.where(lower, a, b), jnp.where(lower, b, a)], axis=1)
-
-    span_rows = feats.shape[1]
-    same = exchange(jnp.broadcast_to(feats[None], (chips,) + feats.shape), same_core)
-    other = swap(same, 1, count)
-    feats_all = jnp.concatenate([same, other]).reshape(count * MOST, span_rows, latents)
-    place = (((active % 2) ^ core) * chips + active // 2) * MOST + slot_of
-
-    small = feats_all.size * 4 + dec_all.size * 8 < 40 * 2**20
-    r_out, y_out = (decode if small else decode_plain)(
-        names, skipped, place.reshape(-1), active.reshape(-1), core.reshape(1), feats_all, dec_all
-    )
-    r_out = r_out.reshape(2, chips, MOST, span_rows, latents)
-    r_near = swap(r_out[1], 1, count)
-    r_sum = (r_out[0].astype(f32) + r_near.astype(f32)).astype(bf16)
-    r_in, y_out = lax.optimization_barrier((exchange(r_sum, same_core), y_out))
-    y_in = exchange(y_out)
-    recon_part = jnp.sum(r_in.astype(f32), axis=0)
+    span_rows = 2 * half * part_rows
+    side = ((active % 2) ^ core) * chips
+    place = (side + ((active // 2) ^ (me // 2))) * MOST + slot_of
+    land = (side + active // 2) * MOST + slot_of
 
     weights = dec.astype(f32)
     base_norm = jnp.sqrt(jnp.sum(weights[:, :stream] * weights[:, :stream], axis=1) + epsilon)
@@ -298,6 +384,26 @@
         grad_scale * (rounded_sum[:, None] * dec_bias[None, :] - fx)
         + penalty_weight * feature_sum[:, None] * weights * inverse
     )
+    all_far, dec_part, xd_own, xd_far = lax.optimization_barrier((all_far, dec_part, xd_own, xd_far))
+
+    small = 16 * all_own[0].size + dec_all.size * 8 < 40 * 2**20
+    r_out, y_out = (decode if small else decode_plain)(
+        names,
+        skipped,
+        place.reshape(-1),
+        land.reshape(-1),
+        active.reshape(-1),
+        jnp.stack([core, my_half]),
+        all_own,
+        all_far,
+        dec_all,
+    )
+    r_out = r_out.reshape(2, chips, MOST, span_rows, latents)
+    r_near = swap(r_out[1], 1, count)
+    r_sum = (r_out[0].astype(f32) + r_near.astype(f32)).astype(bf16)
+    r_in, y_out = lax.optimization_barrier((exchange(r_sum, same_core), y_out))
+    y_in = exchange(y_out)
+    recon_part = jnp.sum(r_in.astype(f32), axis=0)
 
     first, second = recon_part[:, : span_rows // 2], recon_part[:, span_rows // 2 :]
     r_own = by_source(jnp.where(lower, first, second))
@@ -306,17 +412,20 @@
     grad_far = jnp.where((preact_far > 0.0) & (mask > 0.0), r_far - grad_scale * xd_far + constant, 0.0)
     bias_grad = jnp.sum(grad_own, axis=0) + jnp.sum(grad_far, axis=0)
     gb_own, gb_far = grad_own.astype(bf16), grad_far.astype(bf16)
-    enc_grad = down(own, gb_own) + down(far, gb_far)
 
     act_sum = jnp.sum(activations.astype(f32), axis=(0, 1))
     bias_sum = jnp.sum(rounded_sum[:, None] * weights, axis=0) - act_sum
     bias_sum, recon_part = lax.optimization_barrier((bias_sum, recon_part))
     distance = 1
     while distance < count:
+        if distance == count // 2:
+            bias_sum, gb_own, gb_far = lax.optimization_barrier((bias_sum, gb_own, gb_far))
         bias_sum = bias_sum + swap(bias_sum, distance, count)
         distance *= 2
     dec_bias_grad = grad_scale * (bias_sum + float(span_count * part_rows * count) * dec_bias)
+    enc_grad = down(own, gb_own) + down(far, gb_far)
     dec_grad = join_windows(dec_part, y_in, skipped)
+
     return (enc_grad[None], bias_grad[None], dec_grad[None], dec_bias_grad)
 
 

time: 580 us -> 369 us (0.64)
  Pallas kernels: 307 us -> 37.7 us
  waiting for transfers between devices: 161 us -> 194 us
  starting transfers between devices: 37.8 us -> 56.9 us
    pallas_call x2 -> x1, Pallas kernels: 226 us -> 5.65 us  [pick_spans(): pl.pallas_call(pick_kernel, in_specs=[pl.BlockSpec(memory_space=pltpu.SME...]
    pallas_call x1, Pallas kernels: 64.8 us -> 3.06 us  [cut_windows(): pl.pallas_call(functools.partial(window_kernel, starts), in_specs=[pl.Blo...]
    ppermute x7 -> x29, starting transfers between devices: 8.87 us -> 36.9 us  [swap(): return lax.ppermute(x, AXIS, [(i, i ^ distance) for i in range(count)])]
    ppermute x7 -> x29, waiting for transfers between devices: 101 us -> 119 us  [swap(): return lax.ppermute(x, AXIS, [(i, i ^ distance) for i in range(count)])]
    all_to_all x5 -> x3, waiting for transfers between devices: 60.1 us -> 74.7 us  [exchange(): lax.all_to_all(x, AXIS, split_axis=0, concat_axis=0, tiled=True, axis_ind...]
    pallas_call x0 -> x2, Pallas kernels: none -> 11.7 us  [the longest x1 8.11 us: deal_spans(): pl.pallas_call(deal_kernel, in_specs=[pl.BlockSpec(memory_space=pltpu.SME...]
    all_to_all x5 -> x3, starting transfers between devices: 28.9 us -> 20.1 us  [exchange(): lax.all_to_all(x, AXIS, split_axis=0, concat_axis=0, tiled=True, axis_ind...]
  transfers between devices with their start and end apart: 12 -> 32, of which waited for: 8 -> 17; matrix products, arithmetic and copies ran while one was open for 6% -> 9% of each run, Pallas kernels for 39% -> 3%
where the time goes in v4:
time: 369 us; the launch traced here: 366 us
  waiting for transfers between devices  194 us (53%)
  starting transfers between devices  56.9 us (15%)
  Pallas kernels  37.7 us (10%)
  blocking collectives  28.2 us (8%)
  matrix products  27.2 us (7%)
  other arithmetic  10.5 us (3%)
  local copies, waits for them, and re-layouts  9.81 us (3%)
    ppermute x29, waiting for transfers between devices, swap(): return lax.ppermute(x, AXIS, [(i, i ^ distance) for i in range(count)])  119 us
    all_to_all x3, waiting for transfers between devices, exchange(): lax.all_to_all(x, AXIS, split_axis=0, concat_axis=0, tiled=True, axis_ind...  74.7 us
    ppermute x29, starting transfers between devices, swap(): return lax.ppermute(x, AXIS, [(i, i ^ distance) for i in range(count)])  36.9 us
    all_to_all x1, blocking collectives, exchange(): lax.all_to_all(x, AXIS, split_axis=0, concat_axis=0, tiled=True, axis_ind...  28.2 us
    all_to_all x3, starting transfers between devices, exchange(): lax.all_to_all(x, AXIS, split_axis=0, concat_axis=0, tiled=True, axis_ind...  20.1 us
    pallas_call x1, Pallas kernels, decode(): pl.pallas_call(functools.partial(decode_kernel, names, skipped), in_specs...  10.5 us
    dot_general x2, matrix products, shards(): fx = down(fb_own, own) + down(fb_far, far)  8.21 us
    pallas_call x1, Pallas kernels, deal_spans(): pl.pallas_call(deal_kernel, in_specs=[pl.BlockSpec(memory_space=pltpu.SME...  8.11 us
  transfers between devices with their start and end apart: 32, of which 17 were waited for; matrix products, arithmetic and copies ran while one was open for 9% of the time, Pallas kernels for 3%

profile of v4, /device:TPU:15, one launch (start us, length us, event | category | flops | bytes accessed | tf_op | source)
XLA Modules:
  0.0 365.5 jit_solution(13092454187857387811)
XLA Ops:
  0.7 0.9 fusion.25
  1.9 1.5 copy-done.3
  3.4 5.6 %pick_spans.1 = bf16[16,16,7168]{2,1,0:T(8,128)(2,1)S(1)} custom-call(s32[16]{0:T(128)S(1)} %reshape.163.index_ref, bf16[8,16,7168]{2,1,0:T(8,128)(2,1)S(1)} %copy-done.3), custom_call_target="tpu_custom_call" | custom-call | bytes 5505024 | tf_op jit(solution)/shard_map/pick_spans/pallas_call | solution.py:62
  9.0 1.8 copy-done.2
  10.9 5.1 %all-to-all-start = ((bf16[8,2,16,7168]{3,2,1,0:T(8,128)(2,1)}), bf16[8,2,16,7168]{3,2,1,0:T(8,128)(2,1)}, u32[]{:S(2)}, u32[]{:S(2)}) async-start(bf16[8,2,16,7168]{3,2,1,0:T(8,128)(2,1)} %bitcast.111), calls=%async_computation | async-start | bytes 7340032 | tf_op jit(solution)/shard_map/all_to_all | solution.py:26
  16.0 2.3 collective-permute-start
  18.7 3.1 cut_windows.1
  21.7 73.3 %all-to-all-done = bf16[8,2,16,7168]{3,2,1,0:T(8,128)(2,1)} async-done(((bf16[8,2,16,7168]{3,2,1,0:T(8,128)(2,1)}), bf16[8,2,16,7168]{3,2,1,0:T(8,128)(2,1)}, u32[]{:S(2)}, u32[]{:S(2)}) %all-to-all-start) | async-done | bytes 3670048 | tf_op jit(solution)/shard_map/all_to_all | solution.py:26
  95.0 7.2 %all-to-all-start.1 = ((bf16[16,128,512]{2,1,0:T(8,128)(2,1)}), bf16[16,128,512]{2,1,0:T(8,128)(2,1)}, u32[]{:S(2)}, u32[]{:S(2)}) async-start(bf16[16,128,512]{2,1,0:T(8,128)(2,1)} %cut_windows.1), calls=%async_computation.1 | async-start | bytes 4194304 | tf_op jit(solution)/shard_map/all_to_all | solution.py:26
  102.2 3.8 %convert_reduce_fusion.3 = (f32[128]{0:T(128)}, bf16[256,128]{1,0:T(8,128)(2,1)S(1)}, f32[256,128]{1,0:T(8,128)S(1)}) fusion(f32[256]{0:T(256)S(1)} %broadcast_in_dim.30, f32[128]{0:T(128)S(1)} %bitcast.140, bf16[256,7168]{1,0:T(8,128)(2,1)} %bitcast.1, bf16[1,7168,128]{2,1,0:T(8,128)(2,1)S(1)} %copy-done), kind=kOutput, calls=%fused_computation.32 | convolution fusion | flops 469958528 | bytes 5703680 | tf_op jit(solution)/shard_map/dot_general | solution.py:328
  106.0 1.2 collective-permute-start.7
  107.4 4.8 %collective-permute-start.5 = (bf16[2,128,128]{2,1,0:T(8,128)(2,1)S(1)}, bf16[2,128,128]{2,1,0:T(8,128)(2,1)S(1)}, u32[]{:S(2)}, u32[]{:S(2)}) collective-permute-start(bf16[2,128,128]{2,1,0:T(8,128)(2,1)S(1)} %bitcast.134), channel_id=1, source_target_pairs={{0,10},{1,11},{2,8},{3,9},{4,14},{5,15},{6,12},{7,13},{8,2},{9,3},... | collective-permute-start | bytes 196616 | tf_op jit(solution)/shard_map/ppermute | solution.py:22
  112.6 5.9 %collective-permute-done.1 = bf16[2,128,128]{2,1,0:T(8,128)(2,1)S(1)} collective-permute-done((bf16[2,128,128]{2,1,0:T(8,128)(2,1)S(1)}, bf16[2,128,128]{2,1,0:T(8,128)(2,1)S(1)}, u32[]{:S(2)}, u32[]{:S(2)}) %collective-permute-start.1) | collective-permute-done | bytes 65568 | tf_op jit(solution)/shard_map/ppermute | solution.py:22
  118.4 24.8 %collective-permute-done.2 = bf16[2,128,128]{2,1,0:T(8,128)(2,1)S(1)} collective-permute-done((bf16[2,128,128]{2,1,0:T(8,128)(2,1)S(1)}, bf16[2,128,128]{2,1,0:T(8,128)(2,1)S(1)}, u32[]{:S(2)}, u32[]{:S(2)}) %collective-permute-start.2) | collective-permute-done | bytes 65568 | tf_op jit(solution)/shard_map/ppermute | solution.py:22
  143.3 5.4 %collective-permute-done.3 = bf16[2,128,128]{2,1,0:T(8,128)(2,1)S(1)} collective-permute-done((bf16[2,128,128]{2,1,0:T(8,128)(2,1)S(1)}, bf16[2,128,128]{2,1,0:T(8,128)(2,1)S(1)}, u32[]{:S(2)}, u32[]{:S(2)}) %collective-permute-start.3) | collective-permute-done | bytes 65568 | tf_op jit(solution)/shard_map/ppermute | solution.py:22
  148.7 10.0 %collective-permute-done.4 = bf16[2,128,128]{2,1,0:T(8,128)(2,1)S(1)} collective-permute-done((bf16[2,128,128]{2,1,0:T(8,128)(2,1)S(1)}, bf16[2,128,128]{2,1,0:T(8,128)(2,1)S(1)}, u32[]{:S(2)}, u32[]{:S(2)}) %collective-permute-start.4) | collective-permute-done | bytes 65568 | tf_op jit(solution)/shard_map/ppermute | solution.py:22
  158.8 0.9 collective-permute-start.8
  159.7 2.2 bitcast_convert_fusion
  163.0 8.1 %deal_spans.1 = (bf16[2,16,7168]{2,1,0:T(8,128)(2,1)S(1)}, bf16[2,16,7168]{2,1,0:T(8,128)(2,1)}, bf16[2,16,7168]{2,1,0:T(8,128)(2,1)}, bf16[2,16,7168]{2,1,0:T(8...) custom-call(s32[16]{0:T(128)S(1)} %reshape.167.index_ref, ...), custom_call_target="tpu_custom_call" | custom-call | bytes 5505024 | tf_op jit(solution)/shard_map/deal_spans/pallas_call | solution.py:93
  171.7 0.7 reshape.172.land_ref
  172.4 0.6 reshape.171.place_ref
  173.0 0.7 reshape.173.block_ref
  174.3 2.4 fusion.6
  176.7 1.8 collective-permute-start.11
  178.5 3.3 collective-permute-start.12
  181.8 1.5 collective-permute-start.14
  183.3 5.1 %collective-permute-start.15 = (bf16[2,16,7168]{2,1,0:T(8,128)(2,1)}, bf16[2,16,7168]{2,1,0:T(8,128)(2,1)}, u32[]{:S(2)}, u32[]{:S(2)}) collective-permute-start(bf16[2,16,7168]{2,1,0:T(8,128)(2,1)} %get-tuple-element.45), channel_id=1, source_target_pairs={{0,7},{1,6},{2,5},{3,4},{4,3},{5,2},{6,1},{7,0},{8,15},{9,14},{10,... | collective-permute-start | bytes 1376264 | tf_op jit(solution)/shard_map/ppermute | solution.py:22
  188.4 3.2 fusion.33
  191.5 4.6 %fusion.42 = f32[128,7168]{1,0:T(8,128)} fusion(bf16[256,128]{1,0:T(8,128)(2,1)S(1)} %get-tuple-element.85, bf16[256,7168]{1,0:T(8,128)(2,1)} %bitcast.1), kind=kOutput, calls=%fused_computation.97 | convolution fusion | flops 469762048 | bytes 7405568 | tf_op jit(solution)/shard_map/dot_general | solution.py:373
  196.1 6.8 %collective-permute-done.13.refs_5_ = bf16[2,16,7168]{2,1,0:T(8,128)(2,1)} collective-permute-done((bf16[2,16,7168]{2,1,0:T(8,128)(2,1)}, bf16[2,16,7168]{2,1,0:T(8,128)(2,1)}, u32[]{:S(2)}, u32[]{:S(2)}) %collective-permute-start.13) | collective-permute-done | bytes 458784 | tf_op jit(solution)/shard_map/ppermute | solution.py:22
  202.9 9.7 %collective-permute-done.14.refs_6_ = bf16[2,16,7168]{2,1,0:T(8,128)(2,1)} collective-permute-done((bf16[2,16,7168]{2,1,0:T(8,128)(2,1)}, bf16[2,16,7168]{2,1,0:T(8,128)(2,1)}, u32[]{:S(2)}, u32[]{:S(2)}) %collective-permute-start.14) | collective-permute-done | bytes 458784 | tf_op jit(solution)/shard_map/ppermute | solution.py:22
  212.6 9.8 %collective-permute-done.15.refs_7_ = bf16[2,16,7168]{2,1,0:T(8,128)(2,1)} collective-permute-done((bf16[2,16,7168]{2,1,0:T(8,128)(2,1)}, bf16[2,16,7168]{2,1,0:T(8,128)(2,1)}, u32[]{:S(2)}, u32[]{:S(2)}) %collective-permute-start.15) | collective-permute-done | bytes 458784 | tf_op jit(solution)/shard_map/ppermute | solution.py:22
  222.4 3.6 gather_rows.1
  226.0 4.0 %fusion.31 = f32[256,128]{1,0:T(8,128)} fusion(bf16[256,7168]{1,0:T(8,128)(2,1)} %bitcast.112, bf16[1,128,7168]{2,1,0:T(8,128)(2,1)S(1)} %copy-done.9), kind=kOutput, calls=%fused_computation.89 | convolution fusion | flops 469762048 | bytes 5636096 | tf_op jit(solution)/shard_map/dot_general | solution.py:369
  230.0 1.8 fusion.23
  231.9 1.3 collective-permute-start.22
  233.1 1.3 collective-permute-start.21
  234.5 2.9 collective-permute-start.20
  237.4 1.2 collective-permute-start.16
  238.6 1.0 multiply_reduce_fusion
  239.6 2.5 collective-permute-done.16
  242.1 0.9 collective-permute-start.17
  242.9 3.5 collective-permute-done.17
  246.4 2.0 collective-permute-start.18
  248.4 2.0 collective-permute-done.18
  250.6 3.6 collective-permute-start.23
  254.6 3.7 %fusion.3.part_ref = f32[128,7168]{1,0:T(8,128)} fusion(f32[128,7168]{1,0:T(8,128)S(1)} %copy-done.10, bf16[256,128]{1,0:T(8,128)(2,1)S(1)} %get-tuple-element.91, bf16[256,7168]{1,0:T(8,128)(2,1)S(1)} %bitcast.114, f32[128,3584]{1,0:T(8,128)S(1)} %broadcast_in_dim.34, f32[128,3584]{1,0:T(8,128)S(1)} %broadcast_in_dim.33, f32[128]{0:T(128)S(1)} %add_multiply_fusion.1, ...), kind=kOutput, calls=%fused_computation.6 | convolution fusion | flops 478019584 | bytes 16610304 | tf_op jit(solution)/shard_map/dot_general | solution.py:373
  258.3 0.8 copy-done.17
  259.1 10.5 %decode.1 = (bf16[32,256,128]{2,1,0:T(8,128)(2,1)}, bf16[16,128,512]{2,1,0:T(8,128)(2,1)}) custom-call(s32[24]{0:T(128)} %reshape.171.place_ref, s32[24]{0:T(128)} %reshape.172.land_ref, s32[24]{0:T(128)} %reshape.173.block_ref, s32[2]{0:T(128)} %pad_add_fusion.mine_ref, bf16[8,2,128,128]{3,2,1,0:T(8,128)(2,1)} %copy-done.13, ...), custom_call_target="tpu_custom_call" | custom-call | flops 2415919104 | bytes 12582912 | tf_op jit(solution)/shard_map/decode/pallas_call | solution.py:234
  269.6 1.7 fusion.41
  271.4 2.6 collective-permute-done.24
  274.3 28.2 %all_to_all.20 = bf16[8,2,256,128]{3,2,1,0:T(8,128)(2,1)S(1)} all-to-all(bf16[8,2,256,128]{3,2,1,0:T(8,128)(2,1)S(1)} %fusion.4), channel_id=1, replica_groups={{0,2,4,6,8,10,12,14},{1,3,5,7,9,11,13,15},{16,18,20,22,24,26,28,30},{17..., dimensions={0} | all-to-all | bytes 2097152 | tf_op jit(solution)/shard_map/all_to_all | solution.py:26
  302.6 7.7 %all-to-all-start.3 = ((bf16[16,128,512]{2,1,0:T(8,128)(2,1)}), bf16[16,128,512]{2,1,0:T(8,128)(2,1)}, u32[]{:S(2)}, u32[]{:S(2)}) async-start(bf16[16,128,512]{2,1,0:T(8,128)(2,1)} %get-tuple-element.68), calls=%async_computation.3 | async-start | bytes 4194304 | tf_op jit(solution)/shard_map/all_to_all | solution.py:26
  311.3 0.8 collective-permute-done.25
  312.4 1.1 fusion.35
  313.5 7.2 %collective-permute-done.26 = f32[7168]{0:T(1024)S(1)} collective-permute-done((f32[7168]{0:T(1024)S(1)}, f32[7168]{0:T(1024)S(1)}, u32[]{:S(2)}, u32[]{:S(2)}) %collective-permute-start.26) | collective-permute-done | bytes 28704 | tf_op jit(solution)/shard_map/ppermute | solution.py:22
  321.5 25.0 %collective-permute-done.27 = f32[7168]{0:T(1024)S(1)} collective-permute-done((f32[7168]{0:T(1024)S(1)}, f32[7168]{0:T(1024)S(1)}, u32[]{:S(2)}, u32[]{:S(2)}) %collective-permute-start.27) | collective-permute-done | bytes 28704 | tf_op jit(solution)/shard_map/ppermute | solution.py:22
  346.5 0.8 collective-permute-start.28
  347.3 1.2 fusion.43
  348.5 5.1 %fusion = f32[1,7168,128]{2,1,0:T(8,128)} fusion(f32[7168,128]{1,0:T(8,128)S(1)} %fusion.43, bf16[256,7168]{1,0:T(8,128)(2,1)} %bitcast.1, bf16[256,128]{1,0:T(8,128)(2,1)S(1)} %get-tuple-element.65), kind=kOutput, calls=%fused_computation.2 | convolution fusion | flops 470679552 | bytes 11075584 | tf_op jit(solution)/shard_map/dot_general | solution.py:426
  353.6 3.2 collective-permute-done.28
  356.8 0.6 add_multiply_fusion
  357.4 1.4 all-to-all-done.3.y_ref
  358.8 6.7 %join_windows.1 = f32[128,7168]{1,0:T(8,128)} custom-call(f32[128,7168]{1,0:T(8,128)} %fusion.3.part_ref, bf16[16,128,512]{2,1,0:T(8,128)(2,1)} %all-to-all-done.3.y_ref), custom_call_target="tpu_custom_call" | custom-call | tf_op jit(solution)/shard_map/join_windows/pallas_call | solution.py:172
  (117 shorter events, 6.5 us)
Async XLA Ops:
  0.6 101.6 %copy-start = (bf16[1,7168,128]{2,1,0:T(8,128)(2,1)S(1)}, bf16[1,7168,128]{2,1,0:T(8,128)(2,1)}, u32[]{:S(2)}) copy-start(bf16[1,7168,128]{2,1,0:T(8,128)(2,1)} %param.7) | copy-start | bytes 5505028
  1.9 1.5 copy-start.3
  9.0 1.8 copy-start.2
  10.9 84.1 %all-to-all-start = ((bf16[8,2,16,7168]{3,2,1,0:T(8,128)(2,1)}), bf16[8,2,16,7168]{3,2,1,0:T(8,128)(2,1)}, u32[]{:S(2)}, u32[]{:S(2)}) async-start(bf16[8,2,16,7168]{3,2,1,0:T(8,128)(2,1)} %bitcast.111), calls=%async_computation | async-start | bytes 7340032 | tf_op jit(solution)/shard_map/all_to_all | solution.py:26
  16.0 147.0 %collective-permute-start = (bf16[8,16,7168]{2,1,0:T(8,128)(2,1)}, bf16[8,16,7168]{2,1,0:T(8,128)(2,1)}, u32[]{:S(2)}, u32[]{:S(2)}) collective-permute-start(bf16[8,16,7168]{2,1,0:T(8,128)(2,1)} %rows_ref.1), channel_id=1, source_target_pairs={{0,8},{1,9},{2,10},{3,11},{4,12},{5,13},{6,14},{7,15},{8,0},{9,1},... | collective-permute-start | bytes 5505032 | tf_op jit(solution)/shard_map/ppermute | solution.py:22
  18.7 83.5 %copy-start.15 = (f32[1,128]{1,0:T(1,128)S(1)}, f32[1,128]{1,0:T(1,128)}, u32[]{:S(2)}) copy-start(f32[1,128]{1,0:T(1,128)} %param.8) | copy-start | bytes 1540
  95.0 101.1 %all-to-all-start.1 = ((bf16[16,128,512]{2,1,0:T(8,128)(2,1)}), bf16[16,128,512]{2,1,0:T(8,128)(2,1)}, u32[]{:S(2)}, u32[]{:S(2)}) async-start(bf16[16,128,512]{2,1,0:T(8,128)(2,1)} %cut_windows.1), calls=%async_computation.1 | async-start | bytes 4194304 | tf_op jit(solution)/shard_map/all_to_all | solution.py:26
  102.2 57.6 %copy-start.7 = (bf16[1,128,7168]{2,1,0:T(8,128)(2,1)S(1)}, bf16[1,128,7168]{2,1,0:T(8,128)(2,1)}, u32[]{:S(2)}) copy-start(bf16[1,128,7168]{2,1,0:T(8,128)(2,1)} %param.9) | copy-start | bytes 5505028
  106.0 56.0 %copy-start.12 = (s32[8,3]{0,1:T(4,128)S(1)}, s32[8,3]{0,1:T(4,128)}, u32[]{:S(2)}) copy-start(s32[8,3]{0,1:T(4,128)} %param.11) | copy-start | bytes 292
  106.0 52.8 %collective-permute-start.7 = (bf16[2,128,128]{2,1,0:T(8,128)(2,1)S(1)}, bf16[2,128,128]{2,1,0:T(8,128)(2,1)S(1)}, u32[]{:S(2)}, u32[]{:S(2)}) collective-permute-start(bf16[2,128,128]{2,1,0:T(8,128)(2,1)S(1)} %bitcast.132), channel_id=1, source_target_pairs={{0,14},{1,15},{2,12},{3,13},{4,10},{5,11},{6,8},{7,9},{8,6},{9,7},... | collective-permute-start | bytes 196616 | tf_op jit(solution)/shard_map/ppermute | solution.py:22
  107.2 51.5 %collective-permute-start.6 = (bf16[2,128,128]{2,1,0:T(8,128)(2,1)S(1)}, bf16[2,128,128]{2,1,0:T(8,128)(2,1)S(1)}, u32[]{:S(2)}, u32[]{:S(2)}) collective-permute-start(bf16[2,128,128]{2,1,0:T(8,128)(2,1)S(1)} %bitcast.133), channel_id=1, source_target_pairs={{0,12},{1,13},{2,14},{3,15},{4,8},{5,9},{6,10},{7,11},{8,4},{9,5},... | collective-permute-start | bytes 196616 | tf_op jit(solution)/shard_map/ppermute | solution.py:22
  107.4 51.3 %collective-permute-start.5 = (bf16[2,128,128]{2,1,0:T(8,128)(2,1)S(1)}, bf16[2,128,128]{2,1,0:T(8,128)(2,1)S(1)}, u32[]{:S(2)}, u32[]{:S(2)}) collective-permute-start(bf16[2,128,128]{2,1,0:T(8,128)(2,1)S(1)} %bitcast.134), channel_id=1, source_target_pairs={{0,10},{1,11},{2,8},{3,9},{4,14},{5,15},{6,12},{7,13},{8,2},{9,3},... | collective-permute-start | bytes 196616 | tf_op jit(solution)/shard_map/ppermute | solution.py:22
  112.3 6.2 %collective-permute-start.1 = (bf16[2,128,128]{2,1,0:T(8,128)(2,1)S(1)}, bf16[2,128,128]{2,1,0:T(8,128)(2,1)S(1)}, u32[]{:S(2)}, u32[]{:S(2)}) collective-permute-start(bf16[2,128,128]{2,1,0:T(8,128)(2,1)S(1)} %bitcast.135), channel_id=1, source_target_pairs={{0,2},{1,3},{2,0},{3,1},{4,6},{5,7},{6,4},{7,5},{8,10},{9,11},{10,... | collective-permute-start | bytes 196616 | tf_op jit(solution)/shard_map/ppermute | solution.py:22
  118.4 24.8 %collective-permute-start.2 = (bf16[2,128,128]{2,1,0:T(8,128)(2,1)S(1)}, bf16[2,128,128]{2,1,0:T(8,128)(2,1)S(1)}, u32[]{:S(2)}, u32[]{:S(2)}) collective-permute-start(bf16[2,128,128]{2,1,0:T(8,128)(2,1)S(1)} %bitcast.137), channel_id=1, source_target_pairs={{0,4},{1,5},{2,6},{3,7},{4,0},{5,1},{6,2},{7,3},{8,12},{9,13},{10,... | collective-permute-start | bytes 196616 | tf_op jit(solution)/shard_map/ppermute | solution.py:22
  143.3 5.4 %collective-permute-start.3 = (bf16[2,128,128]{2,1,0:T(8,128)(2,1)S(1)}, bf16[2,128,128]{2,1,0:T(8,128)(2,1)S(1)}, u32[]{:S(2)}, u32[]{:S(2)}) collective-permute-start(bf16[2,128,128]{2,1,0:T(8,128)(2,1)S(1)} %bitcast.138), channel_id=1, source_target_pairs={{0,6},{1,7},{2,4},{3,5},{4,2},{5,3},{6,0},{7,1},{8,14},{9,15},{10,... | collective-permute-start | bytes 196616 | tf_op jit(solution)/shard_map/ppermute | solution.py:22
  148.7 10.0 %collective-permute-start.4 = (bf16[2,128,128]{2,1,0:T(8,128)(2,1)S(1)}, bf16[2,128,128]{2,1,0:T(8,128)(2,1)S(1)}, u32[]{:S(2)}, u32[]{:S(2)}) collective-permute-start(bf16[2,128,128]{2,1,0:T(8,128)(2,1)S(1)} %bitcast.139), channel_id=1, source_target_pairs={{0,8},{1,9},{2,10},{3,11},{4,12},{5,13},{6,14},{7,15},{8,0},{9,1},... | collective-permute-start | bytes 196616 | tf_op jit(solution)/shard_map/ppermute | solution.py:22
  158.8 12.3 %copy-start.13 = (bf16[8,2,128,128]{3,2,1,0:T(8,128)(2,1)}, bf16[8,2,128,128]{3,2,1,0:T(8,128)(2,1)S(1)}, u32[]{:S(2)}) copy-start(bf16[8,2,128,128]{3,2,1,0:T(8,128)(2,1)S(1)} %bitcast_dynamic-update-slice_fusion.7.refs_0_) | copy-start | bytes 1572868
  158.8 4.2 %collective-permute-start.8 = (bf16[8,2,128,128]{3,2,1,0:T(8,128)(2,1)S(1)}, bf16[8,2,128,128]{3,2,1,0:T(8,128)(2,1)}, u32[]{:S(2)}, u32[]{:S(2)}) collective-permute-start(bf16[8,2,128,128]{3,2,1,0:T(8,128)(2,1)S(1)} %bitcast_dynamic-update-slice_fusion.7.refs_0_), channel_id=1, source_target_pairs={{0,1},{1,0},{2,3},{3,2},{4,5},{5,4},{6,7},{7,6},{8,9},{9,8},{10,11... | collective-permute-start | bytes 1572872 | tf_op jit(solution)/shard_map/ppermute | solution.py:22
  171.1 10.6 %collective-permute-start.9 = (bf16[2,16,7168]{2,1,0:T(8,128)(2,1)}, bf16[2,16,7168]{2,1,0:T(8,128)(2,1)S(1)}, u32[]{:S(2)}, u32[]{:S(2)}) collective-permute-start(bf16[2,16,7168]{2,1,0:T(8,128)(2,1)} %get-tuple-element.39), channel_id=1, source_target_pairs={{0,1},{1,0},{2,3},{3,2},{4,5},{5,4},{6,7},{7,6},{8,9},{9,8},{10,11... | collective-permute-start | bytes 1376264 | tf_op jit(solution)/shard_map/ppermute | solution.py:22
  171.2 12.1 %collective-permute-start.10 = (bf16[2,16,7168]{2,1,0:T(8,128)(2,1)}, bf16[2,16,7168]{2,1,0:T(8,128)(2,1)S(1)}, u32[]{:S(2)}, u32[]{:S(2)}) collective-permute-start(bf16[2,16,7168]{2,1,0:T(8,128)(2,1)} %get-tuple-element.40), channel_id=1, source_target_pairs={{0,2},{1,3},{2,0},{3,1},{4,6},{5,7},{6,4},{7,5},{8,10},{9,11},{10,... | collective-permute-start | bytes 1376264 | tf_op jit(solution)/shard_map/ppermute | solution.py:22
  173.7 14.7 %copy-start.8 = (bf16[1,128,7168]{2,1,0:T(8,128)(2,1)S(1)}, bf16[1,128,7168]{2,1,0:T(8,128)(2,1)}, u32[]{:S(2)}) copy-start(bf16[1,128,7168]{2,1,0:T(8,128)(2,1)} %param.9) | copy-start | bytes 5505028
  176.7 19.4 %collective-permute-start.11 = (bf16[2,16,7168]{2,1,0:T(8,128)(2,1)}, bf16[2,16,7168]{2,1,0:T(8,128)(2,1)}, u32[]{:S(2)}, u32[]{:S(2)}) collective-permute-start(bf16[2,16,7168]{2,1,0:T(8,128)(2,1)} %get-tuple-element.41), channel_id=1, source_target_pairs={{0,3},{1,2},{2,1},{3,0},{4,7},{5,6},{6,5},{7,4},{8,11},{9,10},{10,... | collective-permute-start | bytes 1376264 | tf_op jit(solution)/shard_map/ppermute | solution.py:22
  178.5 17.6 %collective-permute-start.12 = (bf16[2,16,7168]{2,1,0:T(8,128)(2,1)}, bf16[2,16,7168]{2,1,0:T(8,128)(2,1)}, u32[]{:S(2)}, u32[]{:S(2)}) collective-permute-start(bf16[2,16,7168]{2,1,0:T(8,128)(2,1)} %get-tuple-element.42), channel_id=1, source_target_pairs={{0,4},{1,5},{2,6},{3,7},{4,0},{5,1},{6,2},{7,3},{8,12},{9,13},{10,... | collective-permute-start | bytes 1376264 | tf_op jit(solution)/shard_map/ppermute | solution.py:22
  181.8 21.2 %collective-permute-start.13 = (bf16[2,16,7168]{2,1,0:T(8,128)(2,1)}, bf16[2,16,7168]{2,1,0:T(8,128)(2,1)}, u32[]{:S(2)}, u32[]{:S(2)}) collective-permute-start(bf16[2,16,7168]{2,1,0:T(8,128)(2,1)} %get-tuple-element.43), channel_id=1, source_target_pairs={{0,5},{1,4},{2,7},{3,6},{4,1},{5,0},{6,3},{7,2},{8,13},{9,12},{10,... | collective-permute-start | bytes 1376264 | tf_op jit(solution)/shard_map/ppermute | solution.py:22
  181.8 30.8 %collective-permute-start.14 = (bf16[2,16,7168]{2,1,0:T(8,128)(2,1)}, bf16[2,16,7168]{2,1,0:T(8,128)(2,1)}, u32[]{:S(2)}, u32[]{:S(2)}) collective-permute-start(bf16[2,16,7168]{2,1,0:T(8,128)(2,1)} %get-tuple-element.44), channel_id=1, source_target_pairs={{0,6},{1,7},{2,4},{3,5},{4,2},{5,3},{6,0},{7,1},{8,14},{9,15},{10,... | collective-permute-start | bytes 1376264 | tf_op jit(solution)/shard_map/ppermute | solution.py:22
  183.3 39.1 %collective-permute-start.15 = (bf16[2,16,7168]{2,1,0:T(8,128)(2,1)}, bf16[2,16,7168]{2,1,0:T(8,128)(2,1)}, u32[]{:S(2)}, u32[]{:S(2)}) collective-permute-start(bf16[2,16,7168]{2,1,0:T(8,128)(2,1)} %get-tuple-element.45), channel_id=1, source_target_pairs={{0,7},{1,6},{2,5},{3,4},{4,3},{5,2},{6,1},{7,0},{8,15},{9,14},{10,... | collective-permute-start | bytes 1376264 | tf_op jit(solution)/shard_map/ppermute | solution.py:22
  222.4 3.6 copy-start.9
  226.0 4.0 %copy-start.5 = (bf16[8,2,16,7168]{3,2,1,0:T(8,128)(2,1)S(1)}, bf16[8,2,16,7168]{3,2,1,0:T(8,128)(2,1)}, u32[]{:S(2)}) copy-start(bf16[8,2,16,7168]{3,2,1,0:T(8,128)(2,1)} %gather_rows.1) | copy-start | bytes 11010052
  230.0 8.5 %copy-start.16 = (f32[128]{0:T(128)S(1)}, f32[128]{0:T(128)}, u32[]{:S(2)}) copy-start(f32[128]{0:T(128)} %get-tuple-element.84) | copy-start | bytes 1540
  230.0 8.5 %copy-start.11 = (f32[7168]{0:T(1024)S(1)}, f32[7168]{0:T(1024)}, u32[]{:S(2)}) copy-start(f32[7168]{0:T(1024)} %param.10) | copy-start | bytes 86020
  231.9 22.8 %copy-start.10 = (f32[128,7168]{1,0:T(8,128)S(1)}, f32[128,7168]{1,0:T(8,128)}, u32[]{:S(2)}) copy-start(f32[128,7168]{1,0:T(8,128)} %fusion.42) | copy-start | bytes 11010052
  231.9 18.7 %collective-permute-start.22 = (bf16[2,128,128]{2,1,0:T(8,128)(2,1)S(1)}, bf16[2,128,128]{2,1,0:T(8,128)(2,1)S(1)}, u32[]{:S(2)}, u32[]{:S(2)}) collective-permute-start(bf16[2,128,128]{2,1,0:T(8,128)(2,1)S(1)} %bitcast.124), channel_id=1, source_target_pairs={{0,14},{1,15},{2,12},{3,13},{4,10},{5,11},{6,8},{7,9},{8,6},{9,7},... | collective-permute-start | bytes 196616 | tf_op jit(solution)/shard_map/ppermute | solution.py:22
  233.1 17.4 %collective-permute-start.21 = (bf16[2,128,128]{2,1,0:T(8,128)(2,1)S(1)}, bf16[2,128,128]{2,1,0:T(8,128)(2,1)S(1)}, u32[]{:S(2)}, u32[]{:S(2)}) collective-permute-start(bf16[2,128,128]{2,1,0:T(8,128)(2,1)S(1)} %bitcast.125), channel_id=1, source_target_pairs={{0,12},{1,13},{2,14},{3,15},{4,8},{5,9},{6,10},{7,11},{8,4},{9,5},... | collective-permute-start | bytes 196616 | tf_op jit(solution)/shard_map/ppermute | solution.py:22
  234.5 16.0 %collective-permute-start.20 = (bf16[2,128,128]{2,1,0:T(8,128)(2,1)S(1)}, bf16[2,128,128]{2,1,0:T(8,128)(2,1)S(1)}, u32[]{:S(2)}, u32[]{:S(2)}) collective-permute-start(bf16[2,128,128]{2,1,0:T(8,128)(2,1)S(1)} %bitcast.126), channel_id=1, source_target_pairs={{0,10},{1,11},{2,8},{3,9},{4,14},{5,15},{6,12},{7,13},{8,2},{9,3},... | collective-permute-start | bytes 196616 | tf_op jit(solution)/shard_map/ppermute | solution.py:22
  237.4 13.1 %collective-permute-start.19 = (bf16[2,128,128]{2,1,0:T(8,128)(2,1)S(1)}, bf16[2,128,128]{2,1,0:T(8,128)(2,1)S(1)}, u32[]{:S(2)}, u32[]{:S(2)}) collective-permute-start(bf16[2,128,128]{2,1,0:T(8,128)(2,1)S(1)} %bitcast.127), channel_id=1, source_target_pairs={{0,8},{1,9},{2,10},{3,11},{4,12},{5,13},{6,14},{7,15},{8,0},{9,1},... | collective-permute-start | bytes 196616 | tf_op jit(solution)/shard_map/ppermute | solution.py:22
  237.4 4.7 %collective-permute-start.16 = (bf16[2,128,128]{2,1,0:T(8,128)(2,1)S(1)}, bf16[2,128,128]{2,1,0:T(8,128)(2,1)S(1)}, u32[]{:S(2)}, u32[]{:S(2)}) collective-permute-start(bf16[2,128,128]{2,1,0:T(8,128)(2,1)S(1)} %bitcast.128), channel_id=1, source_target_pairs={{0,2},{1,3},{2,0},{3,1},{4,6},{5,7},{6,4},{7,5},{8,10},{9,11},{10,... | collective-permute-start | bytes 196616 | tf_op jit(solution)/shard_map/ppermute | solution.py:22
  242.1 4.4 %collective-permute-start.17 = (bf16[2,128,128]{2,1,0:T(8,128)(2,1)S(1)}, bf16[2,128,128]{2,1,0:T(8,128)(2,1)S(1)}, u32[]{:S(2)}, u32[]{:S(2)}) collective-permute-start(bf16[2,128,128]{2,1,0:T(8,128)(2,1)S(1)} %bitcast.130), channel_id=1, source_target_pairs={{0,4},{1,5},{2,6},{3,7},{4,0},{5,1},{6,2},{7,3},{8,12},{9,13},{10,... | collective-permute-start | bytes 196616 | tf_op jit(solution)/shard_map/ppermute | solution.py:22
  246.4 4.0 %collective-permute-start.18 = (bf16[2,128,128]{2,1,0:T(8,128)(2,1)S(1)}, bf16[2,128,128]{2,1,0:T(8,128)(2,1)S(1)}, u32[]{:S(2)}, u32[]{:S(2)}) collective-permute-start(bf16[2,128,128]{2,1,0:T(8,128)(2,1)S(1)} %bitcast.131), channel_id=1, source_target_pairs={{0,6},{1,7},{2,4},{3,5},{4,2},{5,3},{6,0},{7,1},{8,14},{9,15},{10,... | collective-permute-start | bytes 196616 | tf_op jit(solution)/shard_map/ppermute | solution.py:22
  250.6 7.7 %copy-start.14 = (bf16[8,2,128,128]{3,2,1,0:T(8,128)(2,1)}, bf16[8,2,128,128]{3,2,1,0:T(8,128)(2,1)S(1)}, u32[]{:S(2)}) copy-start(bf16[8,2,128,128]{3,2,1,0:T(8,128)(2,1)S(1)} %bitcast_dynamic-update-slice_fusion.refs_2_) | copy-start | bytes 1572868
  250.6 7.7 %collective-permute-start.23 = (bf16[8,2,128,128]{3,2,1,0:T(8,128)(2,1)S(1)}, bf16[8,2,128,128]{3,2,1,0:T(8,128)(2,1)S(1)}, u32[]{:S(2)}, u32[]{:S(2)}) collective-permute-start(bf16[8,2,128,128]{3,2,1,0:T(8,128)(2,1)S(1)} %bitcast_dynamic-update-slice_fusion.refs_2_), channel_id=1, source_target_pairs={{0,1},{1,0},{2,3},{3,2},{4,5},{5,4},{6,7},{7,6},{8,9},{9,8},{10,11... | collective-permute-start | bytes 1572872 | tf_op jit(solution)/shard_map/ppermute | solution.py:22
  258.3 0.8 copy-start.17
  271.3 2.7 collective-permute-start.24
  274.3 36.0 %copy-start.4 = (bf16[8,16,7168]{2,1,0:T(8,128)(2,1)S(1)}, bf16[8,16,7168]{2,1,0:T(8,128)(2,1)}, u32[]{:S(2)}) copy-start(bf16[8,16,7168]{2,1,0:T(8,128)(2,1)} %rows_ref.1) | copy-start | bytes 5505028
  302.6 56.2 %all-to-all-start.3 = ((bf16[16,128,512]{2,1,0:T(8,128)(2,1)}), bf16[16,128,512]{2,1,0:T(8,128)(2,1)}, u32[]{:S(2)}, u32[]{:S(2)}) async-start(bf16[16,128,512]{2,1,0:T(8,128)(2,1)} %get-tuple-element.68), calls=%async_computation.3 | async-start | bytes 4194304 | tf_op jit(solution)/shard_map/all_to_all | solution.py:26
  310.3 37.0 %copy-start.6 = (bf16[8,2,16,7168]{3,2,1,0:T(8,128)(2,1)S(1)}, bf16[8,2,16,7168]{3,2,1,0:T(8,128)(2,1)}, u32[]{:S(2)}) copy-start(bf16[8,2,16,7168]{3,2,1,0:T(8,128)(2,1)} %gather_rows.1) | copy-start | bytes 11010052
  310.8 1.3 collective-permute-start.25
  312.1 8.6 %collective-permute-start.26 = (f32[7168]{0:T(1024)S(1)}, f32[7168]{0:T(1024)S(1)}, u32[]{:S(2)}, u32[]{:S(2)}) collective-permute-start(f32[7168]{0:T(1024)S(1)} %add.185), channel_id=1, source_target_pairs={{0,2},{1,3},{2,0},{3,1},{4,6},{5,7},{6,4},{7,5},{8,10},{9,11},{10,... | collective-permute-start | bytes 86024 | tf_op jit(solution)/shard_map/ppermute | solution.py:22
  320.7 25.8 %collective-permute-start.27 = (f32[7168]{0:T(1024)S(1)}, f32[7168]{0:T(1024)S(1)}, u32[]{:S(2)}, u32[]{:S(2)}) collective-permute-start(f32[7168]{0:T(1024)S(1)} %add.186), channel_id=1, source_target_pairs={{0,4},{1,5},{2,6},{3,7},{4,0},{5,1},{6,2},{7,3},{8,12},{9,13},{10,... | collective-permute-start | bytes 86024 | tf_op jit(solution)/shard_map/ppermute | solution.py:22
  346.5 10.3 %collective-permute-start.28 = (f32[7168]{0:T(1024)S(1)}, f32[7168]{0:T(1024)S(1)}, u32[]{:S(2)}, u32[]{:S(2)}) collective-permute-start(f32[7168]{0:T(1024)S(1)} %add.187), channel_id=1, source_target_pairs={{0,8},{1,9},{2,10},{3,11},{4,12},{5,13},{6,14},{7,15},{8,0},{9,1},... | collective-permute-start | bytes 86024 | tf_op jit(solution)/shard_map/ppermute | solution.py:22
  356.8 8.7 %copy-start.1 = (bf16[1,7168,128]{2,1,0:T(8,128)(2,1)S(1)}, bf16[1,7168,128]{2,1,0:T(8,128)(2,1)}, u32[]{:S(2)}) copy-start(bf16[1,7168,128]{2,1,0:T(8,128)(2,1)} %param.7) | copy-start | bytes 5505028

commit v5 on v4

v5 whole, which is shorter than its diff:
```python
import functools

import jax
import jax.numpy as jnp
from jax import lax
from jax.experimental import pallas as pl
from jax.experimental.pallas import tpu as pltpu
from jax.sharding import PartitionSpec as P

MOST = 2
UNROLL = 4
AXIS = "latent"

penalty_weight = 0.1
grad_scale = 0.0625
epsilon = 1e-06

f32 = jnp.float32
bf16 = jnp.bfloat16


def swap(x, distance, count):
    return lax.ppermute(x, AXIS, [(i, i ^ distance) for i in range(count)])


def exchange(x, groups=None):
    return lax.all_to_all(
        x, AXIS, split_axis=0, concat_axis=0, tiled=True, axis_index_groups=groups
    )


def slot_tables(active, count):
    blocks = jnp.arange(count, dtype=jnp.int32)
    member = jnp.any(active[:, :, None] == blocks[None, None, :], axis=1).astype(jnp.int32)
    position = jnp.cumsum(member, axis=0) - member
    slots = jnp.arange(MOST, dtype=jnp.int32)
    chosen = member[:, :, None] * (position[:, :, None] == slots).astype(jnp.int32)
    spans = jnp.arange(active.shape[0], dtype=jnp.int32)
    span_of = jnp.sum(chosen * spans[:, None, None], axis=0)
    live = jnp.sum(chosen, axis=0)
    named = active[:, :, None] == blocks[None, None, :]
    slot_of = jnp.sum(jnp.where(named, position[:, None, :], 0), axis=2)
    name_of = jnp.argmax(active[span_of] == blocks[:, None, None], axis=2).astype(jnp.int32)
    return span_of, live, slot_of, name_of


def pick_kernel(index_ref, rows_ref, out_ref):
    def copy(i, carry):
        out_ref[i] = rows_ref[index_ref[i]]
        return carry

    lax.fori_loop(0, out_ref.shape[0], copy, 0)


def pick_spans(rows, index):
    vmem = pl.BlockSpec(memory_space=pltpu.VMEM)
    return pl.pallas_call(
        pick_kernel,
        in_specs=[pl.BlockSpec(memory_space=pltpu.SMEM), vmem],
        out_specs=vmem,
        out_shape=jax.ShapeDtypeStruct(index.shape + rows.shape[1:], rows.dtype),
        compiler_params=pltpu.CompilerParams(vmem_limit_bytes=48 * 2**20),
        cost_estimate=pl.CostEstimate(flops=0, bytes_accessed=6 * rows.size, transcendentals=0),
        name="pick_spans",
    )(index, rows)


def deal_kernel(index_ref, rows_ref, *outs):
    for i, out in enumerate(outs):
        for slot in range(MOST):
            out[slot] = rows_ref[index_ref[i * MOST + slot]]


def deal_spans(rows, index):
    parts = index.shape[0] // MOST
    vmem = pl.BlockSpec(memory_space=pltpu.VMEM)
    return pl.pallas_call(
        deal_kernel,
        in_specs=[pl.BlockSpec(memory_space=pltpu.SMEM), vmem],
        out_specs=[vmem] * parts,
        out_shape=[jax.ShapeDtypeStruct((MOST,) + rows.shape[1:], rows.dtype)] * parts,
        compiler_params=pltpu.CompilerParams(vmem_limit_bytes=48 * 2**20),
        cost_estimate=pl.CostEstimate(flops=0, bytes_accessed=6 * rows.size, transcendentals=0),
        name="deal_spans",
    )(index, rows)


def gather_kernel(place_ref, *refs):
    parts, out_ref, sems = refs[:-2], refs[-2], refs[-1]
    copies = [
        pltpu.make_async_copy(part, out_ref.at[i ^ place_ref[0]], sems.at[i])
        for i, part in enumerate(parts)
    ]
    for copy in copies:
        copy.start()
    for copy in copies:
        copy.wait()


def gather_rows(parts, place):
    count = len(parts)
    return pl.pallas_call(
        gather_kernel,
        in_specs=[pl.BlockSpec(memory_space=pltpu.SMEM)]
        + [pl.BlockSpec(memory_space=pl.ANY)] * count,
        out_specs=pl.BlockSpec(memory_space=pltpu.VMEM),
        out_shape=jax.ShapeDtypeStruct((count,) + parts[0].shape, parts[0].dtype),
        scratch_shapes=[pltpu.SemaphoreType.DMA((count,))],
        compiler_params=pltpu.CompilerParams(vmem_limit_bytes=48 * 2**20),
        cost_estimate=pl.CostEstimate(
            flops=0, bytes_accessed=4 * count * parts[0].size, transcendentals=0
        ),
        name="gather_rows",
    )(place, *parts)


def pack_kernel(*refs):
    for i, part in enumerate(refs[:-1]):
        refs[-1][i] = part[...]


def pack(parts):
    vmem = pl.BlockSpec(memory_space=pltpu.VMEM)
    return pl.pallas_call(
        pack_kernel,
        in_specs=[vmem] * len(parts),
        out_specs=vmem,
        out_shape=jax.ShapeDtypeStruct((len(parts),) + parts[0].shape, parts[0].dtype),
        compiler_params=pltpu.CompilerParams(vmem_limit_bytes=48 * 2**20),
        cost_estimate=pl.CostEstimate(
            flops=0, bytes_accessed=4 * len(parts) * parts[0].size, transcendentals=0
        ),
        name="pack",
    )(*parts)


def window_kernel(starts, dec_ref, out_ref, sems):
    width = out_ref.shape[-1]
    copies = [
        pltpu.make_async_copy(dec_ref.at[:, pl.ds(s, width)], out_ref.at[i], sems.at[i])
        for i, s in enumerate(starts)
    ]
    for copy in copies:
        copy.start()
    for copy in copies:
        copy.wait()


def cut_windows(dec, starts, window):
    if any(s % 128 for s in starts) or window % 128:
        return jnp.stack([dec[:, s : s + window] for s in starts])
    return pl.pallas_call(
        functools.partial(window_kernel, starts),
        in_specs=[pl.BlockSpec(memory_space=pltpu.VMEM)],
        out_specs=pl.BlockSpec(memory_space=pl.ANY),
        out_shape=jax.ShapeDtypeStruct((len(starts), dec.shape[0], window), dec.dtype),
        scratch_shapes=[pltpu.SemaphoreType.DMA((len(starts),))],
        cost_estimate=pl.CostEstimate(flops=0, bytes_accessed=4 * dec.size, transcendentals=0),
        name="cut_windows",
    )(dec)


def join_kernel(skipped, part_ref, y_ref, out_ref, windows, joined, in_sems, out_sems):
    count, _, window = y_ref.shape
    per_chip = 2 * window - skipped
    arriving, leaving = [], []
    for chip in range(count // 2):
        pair = pl.ds(2 * chip, 2)
        arriving.append(pltpu.make_async_copy(y_ref.at[pair], windows.at[pair], in_sems.at[chip]))
        arriving[-1].start()
    for chip in range(count // 2):
        at = chip * per_chip
        arriving[chip].wait()
        joined[chip, :, :window] = part_ref[:, at : at + window] + windows[2 * chip].astype(f32)
        joined[chip, :, window:] = (
            part_ref[:, at + window : at + per_chip]
            + windows[2 * chip + 1][:, skipped:].astype(f32)
        )
        leaving.append(
            pltpu.make_async_copy(
                joined.at[chip], out_ref.at[:, pl.ds(at, per_chip)], out_sems.at[chip]
            )
        )
        leaving[-1].start()
    for copy in leaving:
        copy.wait()


def join_windows(part, y, skipped):
    count, latents, window = y.shape
    if window % 128 or skipped % 128:
        cols = [y[i] if i % 2 == 0 else y[i][:, skipped:] for i in range(count)]
        return part + jnp.concatenate(cols, axis=1).astype(f32)
    vmem = pl.BlockSpec(memory_space=pltpu.VMEM)
    return pl.pallas_call(
        functools.partial(join_kernel, skipped),
        in_specs=[vmem, pl.BlockSpec(memory_space=pl.ANY)],
        out_specs=pl.BlockSpec(memory_space=pl.ANY),
        out_shape=jax.ShapeDtypeStruct(part.shape, f32),
        scratch_shapes=[
            pltpu.VMEM(y.shape, y.dtype),
            pltpu.VMEM((count // 2, latents, 2 * window - skipped), f32),
            pltpu.SemaphoreType.DMA((count // 2,)),
            pltpu.SemaphoreType.DMA((count // 2,)),
        ],
        compiler_params=pltpu.CompilerParams(vmem_limit_bytes=48 * 2**20),
        cost_estimate=pl.CostEstimate(
            flops=part.size, bytes_accessed=8 * part.size, transcendentals=0
        ),
        name="join_windows",
    )(part, y)


def take_feats(place, rows, feat_refs, store):
    chips, most = feat_refs[0].shape[:2]
    slot = place % most
    chip = place // most % chips
    for core in range(2):

        @pl.when(place // (most * chips) == core)
        def _():
            store(
                chip < chips // 2,
                feat_refs[core][chip, slot, : rows // 2],
                feat_refs[core][chip, slot, rows // 2 : rows],
            )


def decode_kernel(names, place_ref, block_ref, same_ref, other_ref, dec_ref, y_ref, total, feats, decs):
    span_count = place_ref.shape[0] // names
    rows, latents = feats.shape[0], same_ref.shape[3]
    total[...] = jnp.zeros_like(total)

    def span_step(span, carry):
        block = [block_ref[span * names + name] for name in range(names)]
        for name in range(names):
            cols = slice(name * latents, (name + 1) * latents)

            def store(same, own, far):
                first = pl.multiple_of(jnp.where(same, 0, rows // 2), rows // 2)
                feats[pl.ds(first, rows // 2), cols] = own
                feats[pl.ds(rows // 2 - first, rows // 2), cols] = far

            take_feats(place_ref[span * names + name], rows, (same_ref, other_ref), store)
            decs[cols, :] = dec_ref[block[name]]
        scaled = jnp.dot(feats[...], decs[...], preferred_element_type=f32) * grad_scale
        grad = lax.dot_general(
            feats[...], scaled.astype(bf16), (((0,), (0,)), ((), ())), preferred_element_type=f32
        )
        for name in range(names):
            total[block[name]] += grad[name * latents : (name + 1) * latents]
        return carry

    lax.fori_loop(0, span_count, span_step, 0, unroll=UNROLL)
    y_ref[...] = total[...].astype(bf16)


def decode(names, rows, place, block, feats, dec):
    vmem = pl.BlockSpec(memory_space=pltpu.VMEM)
    smem = pl.BlockSpec(memory_space=pltpu.SMEM)
    pairs, columns = place.shape[0], dec.shape[2]
    latents = feats[0].shape[3]
    return pl.pallas_call(
        functools.partial(decode_kernel, names),
        in_specs=[smem] * 2 + [vmem] * 3,
        out_specs=vmem,
        out_shape=jax.ShapeDtypeStruct(dec.shape, bf16),
        scratch_shapes=[
            pltpu.VMEM(dec.shape, f32),
            pltpu.VMEM((rows, names * latents), bf16),
            pltpu.VMEM((names * latents, columns), bf16),
        ],
        compiler_params=pltpu.CompilerParams(vmem_limit_bytes=56 * 2**20),
        cost_estimate=pl.CostEstimate(
            flops=4 * pairs * rows * latents * columns,
            bytes_accessed=4 * (feats[0].size + dec.size),
            transcendentals=0,
        ),
        name="decode",
    )(place, block, *feats, dec)


def gram_kernel(names, skipped, land_ref, block_ref, core_ref, dec_ref, out_ref, decs):
    span_count = block_ref.shape[0] // names
    latents = dec_ref.shape[1]
    out_ref[...] = jnp.zeros_like(out_ref)

    def span_step(span, carry):
        for name in range(names):
            decs[name * latents : (name + 1) * latents] = dec_ref[block_ref[span * names + name]]
        kept = decs[...]
        if skipped:
            lane = lax.broadcasted_iota(jnp.int32, kept.shape, 1)
            kept = jnp.where(lane >= core_ref[0] * skipped, kept, jnp.zeros_like(kept))
        part = lax.dot_general(
            decs[...], kept, (((1,), (1,)), ((), ())), preferred_element_type=f32
        ).astype(bf16)
        for name in range(names):
            for other in range(names - 1):
                from_name = (name + 1 + other) % names
                at = land_ref[span * names + name] * (names - 1) + other
                out_ref[at] = part[
                    from_name * latents : (from_name + 1) * latents,
                    name * latents : (name + 1) * latents,
                ]
        return carry

    lax.fori_loop(0, span_count, span_step, 0)


def gram(names, skipped, land, block, core, dec):
    vmem = pl.BlockSpec(memory_space=pltpu.VMEM)
    smem = pl.BlockSpec(memory_space=pltpu.SMEM)
    places, latents = dec.shape[0] * MOST * (names - 1), dec.shape[1]
    return pl.pallas_call(
        functools.partial(gram_kernel, names, skipped),
        in_specs=[smem] * 3 + [vmem],
        out_specs=vmem,
        out_shape=jax.ShapeDtypeStruct((places, latents, latents), bf16),
        scratch_shapes=[pltpu.VMEM((names * latents, dec.shape[2]), bf16)],
        compiler_params=pltpu.CompilerParams(vmem_limit_bytes=56 * 2**20),
        cost_estimate=pl.CostEstimate(
            flops=2 * block.shape[0] * names * latents * latents * dec.shape[2],
            bytes_accessed=2 * (dec.size + places * latents * latents),
            transcendentals=0,
        ),
        name="gram",
    )(land, block, core, dec)


def back_kernel(names, place_ref, same_ref, other_ref, gram_ref, r_own_ref, r_far_ref):
    r_own_ref[...] = jnp.zeros_like(r_own_ref)
    r_far_ref[...] = jnp.zeros_like(r_far_ref)
    rows = 2 * r_own_ref.shape[1]
    for slot in range(r_own_ref.shape[0]):
        for name in range(names):
            weight = gram_ref[slot, name]

            def store(same, own, far):
                own_part = jnp.dot(own, weight, preferred_element_type=f32) * grad_scale
                far_part = jnp.dot(far, weight, preferred_element_type=f32) * grad_scale
                r_own_ref[slot] += jnp.where(same, own_part, far_part)
                r_far_ref[slot] += jnp.where(same, far_part, own_part)

            take_feats(place_ref[slot * names + name], rows, (same_ref, other_ref), store)


def back(names, rows, place, feats, grams):
    vmem = pl.BlockSpec(memory_space=pltpu.VMEM)
    smem = pl.BlockSpec(memory_space=pltpu.SMEM)
    _, most, _, latents = feats[0].shape
    return pl.pallas_call(
        functools.partial(back_kernel, names),
        in_specs=[smem] + [vmem] * 3,
        out_specs=[vmem, vmem],
        out_shape=[jax.ShapeDtypeStruct((most, rows // 2, latents), f32)] * 2,
        compiler_params=pltpu.CompilerParams(vmem_limit_bytes=56 * 2**20),
        cost_estimate=pl.CostEstimate(
            flops=2 * most * names * rows * latents * latents,
            bytes_accessed=8 * most * rows * latents,
            transcendentals=0,
        ),
        name="back",
    )(place, *feats, grams)


def shards(activations, enc_weight, enc_bias, dec_weight, dec_bias, active):
    count = lax.axis_size(AXIS)
    me = lax.axis_index(AXIS)
    span_count, part_rows, width = activations.shape
    names = active.shape[1]
    latents = enc_weight.shape[-1]
    stream = width // 2
    half, chips = count // 2, count // 2
    halves = [[h * half + i for i in range(half)] for h in range(2)]
    same_core = [[2 * i + c for i in range(chips)] for c in range(2)]
    my_half, core = me // half, me % 2
    enc, dec = enc_weight[0], dec_weight[0]
    span_of, live, slot_of, name_of = slot_tables(active, count)

    per_chip = width // chips
    if per_chip % 128 == 0:
        window = -(-(per_chip // 2) // 128) * 128
    else:
        window = per_chip // 2
    skipped = 2 * window - per_chip
    starts = [(i // 2) * per_chip + (i % 2) * (per_chip - window) for i in range(count)]

    shape = (half, MOST, part_rows)
    mine = lax.dynamic_slice(span_of, (my_half * half, 0), (half, MOST)).reshape(-1)
    across = swap(activations, half, count)
    x_own = exchange(pick_spans(activations, mine).reshape(shape + (width,)), halves)
    theirs = span_of[me ^ jnp.arange(half)].reshape(-1)
    parts = deal_spans(across, theirs)
    windows, x_own, dec, parts, act = lax.optimization_barrier(
        (cut_windows(dec, starts, window), x_own, dec, tuple(parts), activations)
    )
    dec_all = exchange(windows)
    parts = [parts[0]] + [swap(parts[i], i, count) for i in range(1, half)]

    rows = half * MOST * part_rows
    dot = functools.partial(jnp.dot, preferred_element_type=f32)
    my_live = lax.dynamic_slice(live, (me, 0), (1, MOST)).astype(f32)
    mask = jnp.broadcast_to(my_live[0][None, :, None, None], shape + (1,)).reshape(rows, 1)

    def by_slot(x):
        return x.reshape(half, MOST, part_rows, latents).transpose(1, 0, 2, 3).reshape(MOST, -1, latents)

    def by_source(x):
        return x.reshape(MOST, half, part_rows, latents).transpose(1, 0, 2, 3).reshape(rows, latents)

    def encode(x):
        preact = dot(x, enc) + enc_bias[0]
        feat = jnp.maximum(preact, 0.0) * mask
        return preact, feat, feat.astype(bf16)

    own = x_own.reshape(rows, width)
    preact_own, feat_own, fb_own = encode(own)

    weights = dec.astype(f32)
    base_norm = jnp.sqrt(jnp.sum(weights[:, :stream] * weights[:, :stream], axis=1) + epsilon)
    chat_norm = jnp.sqrt(jnp.sum(weights[:, stream:] * weights[:, stream:], axis=1) + epsilon)
    bias_dec = jnp.sum(weights * dec_bias[None, :], axis=1)
    constant = grad_scale * bias_dec + penalty_weight * (base_norm + chat_norm)
    inverse = jnp.concatenate(
        [
            jnp.broadcast_to(1.0 / base_norm[:, None], (latents, stream)),
            jnp.broadcast_to(1.0 / chat_norm[:, None], (latents, stream)),
        ],
        axis=1,
    )
    cross = functools.partial(
        lax.dot_general, dimension_numbers=(((1,), (1,)), ((), ())), preferred_element_type=f32
    )
    down = functools.partial(
        lax.dot_general, dimension_numbers=(((0,), (0,)), ((), ())), preferred_element_type=f32
    )
    xd_own = cross(own, dec)
    fx_own = down(fb_own, own)
    gram_self = cross(dec, dec).astype(bf16)
    act_sum = jnp.sum(act.astype(f32), axis=(0, 1))

    side = ((active % 2) ^ core) * chips
    place = (side + ((active // 2) ^ (me // 2))) * MOST + slot_of
    land = (side + active // 2) * MOST + slot_of
    ahead = half - half // 4
    dec_all, *parts[:ahead] = lax.optimization_barrier((dec_all, *parts[:ahead]))
    grams = gram(names, skipped, land.reshape(-1), active.reshape(-1), core.reshape(1), dec_all)
    grams = grams.reshape(2, chips, MOST, names - 1, latents, latents)
    near = swap(grams[1], 1, count)
    near = (grams[0].astype(f32) + near.astype(f32)).astype(bf16)

    near, xd_own, fx_own, constant, gram_self, act_sum, *parts = lax.optimization_barrier(
        (near, xd_own, fx_own, constant, gram_self, act_sum, *parts)
    )
    gram_in = jnp.sum(exchange(near, same_core).astype(f32), axis=0).astype(bf16)
    far = gather_rows(parts, (me % half).reshape(1)).reshape(rows, width)
    preact_far, feat_far, fb_far = encode(far)
    feature_sum = jnp.sum(feat_own, axis=0) + jnp.sum(feat_far, axis=0)
    rounded_sum = jnp.sum(fb_own.astype(f32), axis=0) + jnp.sum(fb_far.astype(f32), axis=0)
    bias_sum = jnp.sum(rounded_sum[:, None] * weights, axis=0) - act_sum
    coarse = lax.reduce_precision(bias_sum, 8, 7)
    fine = (bias_sum - coarse).astype(bf16)
    coarse = coarse.astype(bf16)
    extra = jnp.stack([coarse, fine]).reshape(MOST, -1, latents)
    extra = jnp.pad(extra, ((0, 0), (0, -extra.shape[1] % 16), (0, 0)))
    feats = jnp.concatenate([by_slot(fb_own), by_slot(fb_far), extra], axis=1)
    same = pack([feats] + [swap(feats, 2 * i, count) for i in range(1, chips)])
    feats = (same, swap(same, 1, count))

    behind, _ = lax.optimization_barrier((far, fb_far))
    xd_far = cross(behind, dec)
    fx = fx_own + down(fb_far, behind)
    dec_part = (
        grad_scale * (rounded_sum[:, None] * dec_bias[None, :] - fx)
        + penalty_weight * feature_sum[:, None] * weights * inverse
    )
    feats, gram_in = lax.optimization_barrier((feats, gram_in))
    last = [x[:, :, rows // MOST * 2 : rows // MOST * 2 + width // latents] for x in feats]
    bias_sum = sum(jnp.sum(x.astype(f32), axis=(0, 1)) for x in last).reshape(width)
    dec_bias_grad = grad_scale * (bias_sum + float(span_count * part_rows * count) * dec_bias)

    y_out = decode(names, 2 * half * part_rows, place.reshape(-1), active.reshape(-1), feats, dec_all)
    y_in = exchange(y_out)

    my_spans = lax.dynamic_slice(span_of, (me, 0), (1, MOST))[0]
    my_names = lax.dynamic_slice(name_of, (me, 0), (1, MOST))[0]
    turn = (my_names[:, None] + jnp.arange(names)) % names
    r_own, r_far = back(
        names,
        2 * half * part_rows,
        jnp.take_along_axis(place[my_spans], turn, axis=1).reshape(-1),
        feats,
        jnp.concatenate([jnp.broadcast_to(gram_self, (MOST, 1) + gram_self.shape), gram_in], axis=1),
    )
    r_own, r_far = by_source(r_own), by_source(r_far)

    grad_own = jnp.where((preact_own > 0.0) & (mask > 0.0), r_own - grad_scale * xd_own + constant, 0.0)
    grad_far = jnp.where((preact_far > 0.0) & (mask > 0.0), r_far - grad_scale * xd_far + constant, 0.0)
    bias_grad = jnp.sum(grad_own, axis=0) + jnp.sum(grad_far, axis=0)
    enc_grad = down(own, grad_own.astype(bf16)) + down(far, grad_far.astype(bf16))

    dec_grad = join_windows(dec_part, y_in, skipped)
    return (enc_grad[None], bias_grad[None], dec_grad[None], dec_bias_grad)


def solution(mesh):
    in_specs = (
        P("group", "latent", None),
        P(("group", "latent"), None, None),
        P(("group", "latent"), None),
        P(("group", "latent"), None, None),
        P("group"),
        P("group", None),
    )
    out_specs = (
        P(("group", "latent"), None, None),
        P(("group", "latent"), None),
        P(("group", "latent"), None, None),
        P("group"),
    )
    return jax.shard_map(shards, mesh=mesh, in_specs=in_specs, out_specs=out_specs, check_vma=False)
```

time: 369 us -> 316 us (0.86)
  blocking collectives: 28.2 us -> 0 us
  waiting for transfers between devices: 194 us -> 167 us
  local copies, waits for them, and re-layouts: 9.81 us -> 26.7 us
  starting transfers between devices: 56.9 us -> 46.5 us
  Pallas kernels: 37.7 us -> 33.4 us
    all_to_all x3 -> x4, waiting for transfers between devices: 74.7 us -> 26.2 us  [exchange(): lax.all_to_all(x, AXIS, split_axis=0, concat_axis=0, tiled=True, axis_ind...]
    all_to_all x1 -> x0, blocking collectives: 28.2 us -> none  [exchange(): lax.all_to_all(x, AXIS, split_axis=0, concat_axis=0, tiled=True, axis_ind...]
    ppermute x29 -> x17, waiting for transfers between devices: 119 us -> 141 us  [swap(): return lax.ppermute(x, AXIS, [(i, i ^ distance) for i in range(count)])]
    ppermute x29 -> x17, starting transfers between devices: 36.9 us -> 22.2 us  [swap(): return lax.ppermute(x, AXIS, [(i, i ^ distance) for i in range(count)])]
    unnamed x51 -> x73, local copies, waits for them, and re-layouts: 4.45 us -> 17 us
    pallas_call x1, Pallas kernels: 8.11 us -> 2.68 us  [deal_spans(): pl.pallas_call(deal_kernel, in_specs=[pl.BlockSpec(memory_space=pltpu.SME...]
    pallas_call x2 -> x5, Pallas kernels: 17.3 us -> 22.3 us  [the longest x1 9.24 us: decode(): pl.pallas_call(functools.partial(decode_kernel, names), in_specs=[smem] *...]
    pallas_call x1, Pallas kernels: 5.65 us -> 0.86 us  [pick_spans(): pl.pallas_call(pick_kernel, in_specs=[pl.BlockSpec(memory_space=pltpu.SME...]
  transfers between devices with their start and end apart: 32 -> 21, of which waited for: 17 -> 11; matrix products, arithmetic and copies ran while one was open for 9% -> 16% of each run, Pallas kernels for 3% -> 6%
where the time goes in v5:
time: 316 us; the launch traced here: 315 us
  waiting for transfers between devices  167 us (53%)
  starting transfers between devices  46.5 us (15%)
  Pallas kernels  33.4 us (11%)
  local copies, waits for them, and re-layouts  26.7 us (8%)
  matrix products  26.5 us (8%)
  other arithmetic  13.9 us (4%)
    ppermute x17, waiting for transfers between devices, swap(): return lax.ppermute(x, AXIS, [(i, i ^ distance) for i in range(count)])  141 us
    all_to_all x4, waiting for transfers between devices, exchange(): lax.all_to_all(x, AXIS, split_axis=0, concat_axis=0, tiled=True, axis_ind...  26.2 us
    all_to_all x4, starting transfers between devices, exchange(): lax.all_to_all(x, AXIS, split_axis=0, concat_axis=0, tiled=True, axis_ind...  24.3 us
    ppermute x17, starting transfers between devices, swap(): return lax.ppermute(x, AXIS, [(i, i ^ distance) for i in range(count)])  22.2 us
    unnamed x73, local copies, waits for them, and re-layouts  17 us
    pallas_call x1, Pallas kernels, decode(): pl.pallas_call(functools.partial(decode_kernel, names), in_specs=[smem] *...  9.24 us
    dot_general x2, matrix products, encode(): preact = dot(x, enc) + enc_bias[0]  7.17 us
    pallas_call x1, Pallas kernels, gram(): pl.pallas_call(functools.partial(gram_kernel, names, skipped), in_specs=[...  6.56 us
  transfers between devices with their start and end apart: 21, of which 11 were waited for; matrix products, arithmetic and copies ran while one was open for 16% of the time, Pallas kernels for 6%

profile of v5, /device:TPU:15, one launch (start us, length us, event | category | flops | bytes accessed | tf_op | source)
XLA Modules:
  0.0 315.2 jit_solution(9160627169908261826)
XLA Ops:
  0.7 0.9 fusion.34
  1.9 1.5 copy-done.5
  3.4 0.9 pick_spans.1
  4.2 1.8 copy-done.3
  6.1 5.1 %all-to-all-start = ((bf16[8,2,16,7168]{3,2,1,0:T(8,128)(2,1)}), bf16[8,2,16,7168]{3,2,1,0:T(8,128)(2,1)}, u32[]{:S(2)}, u32[]{:S(2)}) async-start(bf16[8,2,16,7168]{3,2,1,0:T(8,128)(2,1)} %bitcast.91), calls=%async_computation | async-start | bytes 7340032 | tf_op jit(solution)/shard_map/all_to_all | solution.py:27
  11.2 2.3 collective-permute-start
  14.3 2.9 cut_windows.1
  17.2 76.0 %collective-permute-done.rows_ref = bf16[8,16,7168]{2,1,0:T(8,128)(2,1)} collective-permute-done((bf16[8,16,7168]{2,1,0:T(8,128)(2,1)}, bf16[8,16,7168]{2,1,0:T(8,128)(2,1)}, u32[]{:S(2)}, u32[]{:S(2)}) %collective-permute-start) | collective-permute-done | bytes 1835040 | tf_op jit(solution)/shard_map/ppermute | solution.py:23
  93.2 2.7 deal_spans.1
  95.9 0.8 copy-done.13
  96.7 0.8 copy-done.14
  97.5 0.8 copy-done.15
  98.3 0.8 copy-done.16
  99.1 6.9 %all-to-all-start.1 = ((bf16[16,128,512]{2,1,0:T(8,128)(2,1)}), bf16[16,128,512]{2,1,0:T(8,128)(2,1)}, u32[]{:S(2)}, u32[]{:S(2)}) async-start(bf16[16,128,512]{2,1,0:T(8,128)(2,1)} %cut_windows.1), calls=%async_computation.1 | async-start | bytes 4194304 | tf_op jit(solution)/shard_map/all_to_all | solution.py:27
  108.0 3.8 %convert_reduce_fusion.4 = (f32[128]{0:T(128)}, bf16[256,128]{1,0:T(8,128)(2,1)S(1)}, f32[256,128]{1,0:T(8,128)S(1)}) fusion(f32[256]{0:T(256)S(1)} %broadcast_in_dim.32, f32[128]{0:T(128)S(1)} %bitcast.114, bf16[256,7168]{1,0:T(8,128)(2,1)} %bitcast.3, bf16[1,7168,128]{2,1,0:T(8,128)(2,1)S(1)} %copy-done), kind=kOutput, calls=%fused_computation.36 | convolution fusion | flops 469958528 | bytes 5703680 | tf_op jit(solution)/shard_map/dot_general | solution.py:413
  112.5 1.5 collective-permute-start.3
  114.3 1.4 collective-permute-start.5
  116.9 1.3 convolution_convert_fusion
  118.2 13.0 %collective-permute-done.2.refs_2_ = bf16[2,16,7168]{2,1,0:T(8,128)(2,1)S(1)} collective-permute-done((bf16[2,16,7168]{2,1,0:T(8,128)(2,1)}, bf16[2,16,7168]{2,1,0:T(8,128)(2,1)S(1)}, u32[]{:S(2)}, u32[]{:S(2)}) %collective-permute-start.2) | collective-permute-done | bytes 458784 | tf_op jit(solution)/shard_map/ppermute | solution.py:23
  131.1 5.8 %collective-permute-start.8 = (bf16[2,16,7168]{2,1,0:T(8,128)(2,1)}, bf16[2,16,7168]{2,1,0:T(8,128)(2,1)}, u32[]{:S(2)}, u32[]{:S(2)}) collective-permute-start(bf16[2,16,7168]{2,1,0:T(8,128)(2,1)} %get-tuple-element.79), channel_id=1, source_target_pairs={{0,7},{1,6},{2,5},{3,4},{4,3},{5,2},{6,1},{7,0},{8,15},{9,14},{10,... | collective-permute-start | bytes 1376264 | tf_op jit(solution)/shard_map/ppermute | solution.py:23
  136.9 10.1 %collective-permute-done.3.refs_3_ = bf16[2,16,7168]{2,1,0:T(8,128)(2,1)S(1)} collective-permute-done((bf16[2,16,7168]{2,1,0:T(8,128)(2,1)}, bf16[2,16,7168]{2,1,0:T(8,128)(2,1)S(1)}, u32[]{:S(2)}, u32[]{:S(2)}) %collective-permute-start.3) | collective-permute-done | bytes 458784 | tf_op jit(solution)/shard_map/ppermute | solution.py:23
  147.1 0.8 copy-done.7
  147.9 3.7 %collective-permute-done.4.refs_4_ = bf16[2,16,7168]{2,1,0:T(8,128)(2,1)S(1)} collective-permute-done((bf16[2,16,7168]{2,1,0:T(8,128)(2,1)}, bf16[2,16,7168]{2,1,0:T(8,128)(2,1)S(1)}, u32[]{:S(2)}, u32[]{:S(2)}) %collective-permute-start.4) | collective-permute-done | bytes 458784 | tf_op jit(solution)/shard_map/ppermute | solution.py:23
  151.6 0.8 copy-done.9
  152.4 10.0 %collective-permute-done.5.refs_5_ = bf16[2,16,7168]{2,1,0:T(8,128)(2,1)S(1)} collective-permute-done((bf16[2,16,7168]{2,1,0:T(8,128)(2,1)}, bf16[2,16,7168]{2,1,0:T(8,128)(2,1)S(1)}, u32[]{:S(2)}, u32[]{:S(2)}) %collective-permute-start.5) | collective-permute-done | bytes 458784 | tf_op jit(solution)/shard_map/ppermute | solution.py:23
  162.4 0.8 copy-done.11
  163.2 6.6 %gram.1 = bf16[64,128,128]{2,1,0:T(8,128)(2,1)} custom-call(s32[24]{0:T(128)} %reshape.291.land_ref, s32[24]{0:T(128)} %reshape.292.block_ref, s32[1]{0:T(128)} %bitcast.14.core_ref, bf16[16,128,512]{2,1,0:T(8,128)(2,1)} %all-to-all-done.1.dec_ref), custom_call_target="tpu_custom_call" | custom-call | flops 1207959552 | bytes 4194304 | tf_op jit(solution)/shard_map/gram/pallas_call | solution.py:315
  169.7 1.7 fusion.50
  172.1 3.8 %fusion.52 = f32[256,128]{1,0:T(8,128)} fusion(bf16[256,7168]{1,0:T(8,128)(2,1)} %bitcast.3, bf16[128,7168]{1,0:T(8,128)(2,1)S(1)} %bitcast.97), kind=kOutput, calls=%fused_computation.109 | convolution fusion | flops 469762048 | bytes 5636096 | tf_op jit(solution)/shard_map/dot_general | solution.py:438
  175.9 4.7 %fusion.53 = f32[128,7168]{1,0:T(8,128)} fusion(bf16[256,128]{1,0:T(8,128)(2,1)S(1)} %get-tuple-element.111, bf16[256,7168]{1,0:T(8,128)(2,1)} %bitcast.3), kind=kOutput, calls=%fused_computation.110 | convolution fusion | flops 469762048 | bytes 7405568 | tf_op jit(solution)/shard_map/dot_general | solution.py:439
  180.6 0.9 convert_reduce_fusion
  181.5 1.5 fusion.2
  182.9 5.2 %all-to-all-start.2 = ((bf16[8,2,2,128,128]{4,3,2,1,0:T(8,128)(2,1)}), bf16[8,2,2,128,128]{4,3,2,1,0:T(8,128)(2,1)}, u32[]{:S(2)}, u32[]{:S(2)}) async-start(bf16[8,2,2,128,128]{4,3,2,1,0:T(8,128)(2,1)} %fusion.2), calls=%async_computation.2 | async-start | bytes 2097152 | tf_op jit(solution)/shard_map/all_to_all | solution.py:27
  188.1 1.0 copy-done.8
  189.1 1.0 copy-done.10
  190.2 1.0 copy-done.12
  191.2 4.7 %gather_rows.1 = bf16[8,2,16,7168]{3,2,1,0:T(8,128)(2,1)} custom-call(s32[1]{0:T(128)} %bitcast.13.place_ref, bf16[2,16,7168]{2,1,0:T(8,128)(2,1)S(1)} %get-tuple-element.80.refs_0_, bf16[2,16,7168]{2,1,0:T(8,128)(2,1)S(1)} %collective-permute-done.1.refs_1_, bf16[2,16,7168]{2,1,0:T(8,128)(2,1)S(1)} %collective-permute-done.2.refs_2_, ...), custom_call_target="tpu_custom_call" | custom-call | bytes 7340032 | tf_op jit(solution)/shard_map/gather_rows/pallas_call | solution.py:102
  195.9 3.3 %fusion.22 = (f32[128]{0:T(128)S(1)}, f32[128]{0:T(128)S(1)}, f32[128]{0:T(128)S(1)}, bf16[256,128]{1,0:T(8,128)(2,1)S(1)}, f32[256,128]{1,0:T(8,128)S(1)}) fusion(f32[256]{0:T(256)S(1)} %broadcast_in_dim.32, f32[256,128]{1,0:T(8,128)S(1)} %get-tuple-element.125, f32[128]{0:T(128)S(1)} %bitcast.115, bf16[256,7168]{1,0:T(8,128)(2,1)} %bitcast.99, ...), kind=kOutput, calls=%fused_computation.41 | convolution fusion | flops 470089344 | bytes 5835776 | tf_op jit(solution)/shard_map/dot_general | solution.py:413
  200.5 0.9 copy-done.22
  201.3 0.7 copy-done.19
  202.1 2.7 fusion.1
  204.8 1.2 collective-permute-start.15
  206.4 4.8 %collective-permute-start.13 = (bf16[2,320,128]{2,1,0:T(8,128)(2,1)S(1)}, bf16[2,320,128]{2,1,0:T(8,128)(2,1)S(1)}, u32[]{:S(2)}, u32[]{:S(2)}) collective-permute-start(bf16[2,320,128]{2,1,0:T(8,128)(2,1)S(1)} %pad_maximum_fusion.1.refs_0_), channel_id=1, source_target_pairs={{0,10},{1,11},{2,8},{3,9},{4,14},{5,15},{6,12},{7,13},{8,2},{9,3},... | collective-permute-start | bytes 491528 | tf_op jit(solution)/shard_map/ppermute | solution.py:23
  211.5 18.6 %collective-permute-done.15.refs_7_ = bf16[2,320,128]{2,1,0:T(8,128)(2,1)S(1)} collective-permute-done((bf16[2,320,128]{2,1,0:T(8,128)(2,1)S(1)}, bf16[2,320,128]{2,1,0:T(8,128)(2,1)S(1)}, u32[]{:S(2)}, u32[]{:S(2)}) %collective-permute-start.15) | collective-permute-done | bytes 163872 | tf_op jit(solution)/shard_map/ppermute | solution.py:23
  230.2 3.1 collective-permute-done.14.refs_6_
  233.3 0.7 collective-permute-start.9
  234.0 1.9 collective-permute-done.13.refs_5_
  235.9 3.5 %collective-permute-done.12.refs_4_ = bf16[2,320,128]{2,1,0:T(8,128)(2,1)S(1)} collective-permute-done((bf16[2,320,128]{2,1,0:T(8,128)(2,1)S(1)}, bf16[2,320,128]{2,1,0:T(8,128)(2,1)S(1)}, u32[]{:S(2)}, u32[]{:S(2)}) %collective-permute-start.12) | collective-permute-done | bytes 163872 | tf_op jit(solution)/shard_map/ppermute | solution.py:23
  239.5 2.8 collective-permute-start.16
  242.9 1.4 reduce_sum.169
  245.0 1.0 copy-done.23
  246.0 9.2 %decode.1 = bf16[16,128,512]{2,1,0:T(8,128)(2,1)} custom-call(s32[24]{0:T(128)} %reshape.301.place_ref, s32[24]{0:T(128)} %reshape.292.block_ref, bf16[8,2,320,128]{3,2,1,0:T(8,128)(2,1)} %copy-done.4, bf16[8,2,320,128]{3,2,1,0:T(8,128)(2,1)} %copy-done.23, bf16[16,128,512]{2,1,0:T(8,128)(2,1)} %all-to-all-done.1.dec_ref), custom_call_target="tpu_custom_call" | custom-call | flops 1610612736 | bytes 6815744 | tf_op jit(solution)/shard_map/decode/pallas_call | solution.py:263
  255.2 7.1 %all-to-all-start.3 = ((bf16[16,128,512]{2,1,0:T(8,128)(2,1)}), bf16[16,128,512]{2,1,0:T(8,128)(2,1)}, u32[]{:S(2)}, u32[]{:S(2)}) async-start(bf16[16,128,512]{2,1,0:T(8,128)(2,1)} %decode.1), calls=%async_computation.3 | async-start | bytes 4194304 | tf_op jit(solution)/shard_map/all_to_all | solution.py:27
  266.3 0.7 pad_maximum_fusion.gram_ref
  267.1 3.4 %back.1 = (f32[2,128,128]{2,1,0:T(8,128)}, f32[2,128,128]{2,1,0:T(8,128)}) custom-call(s32[6]{0:T(128)} %and_select_fusion.1.place_ref, bf16[8,2,320,128]{3,2,1,0:T(8,128)(2,1)} %copy-done.4, bf16[8,2,320,128]{3,2,1,0:T(8,128)(2,1)} %copy-done.23, bf16[2,3,128,128]{3,2,1,0:T(8,128)(2,1)} %pad_maximum_fusion.gram_ref), custom_call_target="tpu_custom_call" | custom-call | flops 50331648 | bytes 524288 | tf_op jit(solution)/shard_map/back/pallas_call | solution.py:352
  270.5 0.9 copy.68
  271.4 0.9 copy.69
  272.3 1.1 convert_reduce_fusion.1
  273.6 2.6 fusion.51
  277.4 3.2 %fusion.27 = f32[7168,128]{1,0:T(8,128)S(1)} fusion(bf16[256,7168]{1,0:T(8,128)(2,1)} %bitcast.3, bf16[256,128]{1,0:T(8,128)(2,1)S(1)} %get-tuple-element.107), kind=kOutput, calls=%fused_computation.47 | convolution fusion | flops 469762048 | bytes 7405568 | tf_op jit(solution)/shard_map/dot_general | solution.py:501
  280.6 3.1 fusion
  283.7 26.2 %all-to-all-done.3.y_ref = bf16[16,128,512]{2,1,0:T(8,128)(2,1)} async-done(((bf16[16,128,512]{2,1,0:T(8,128)(2,1)}), bf16[16,128,512]{2,1,0:T(8,128)(2,1)}, u32[]{:S(2)}, u32[]{:S(2)}) %all-to-all-start.3) | async-done | bytes 2097184 | tf_op jit(solution)/shard_map/all_to_all | solution.py:27
  309.9 2.2 copy-done.2
  312.0 3.0 join_windows.1
  (138 shorter events, 14.2 us)
Async XLA Ops:
  0.6 107.3 %copy-start = (bf16[1,7168,128]{2,1,0:T(8,128)(2,1)S(1)}, bf16[1,7168,128]{2,1,0:T(8,128)(2,1)}, u32[]{:S(2)}) copy-start(bf16[1,7168,128]{2,1,0:T(8,128)(2,1)} %param.7) | copy-start | bytes 5505028
  1.9 1.5 copy-start.5
  4.2 1.8 copy-start.3
  6.1 93.1 %all-to-all-start = ((bf16[8,2,16,7168]{3,2,1,0:T(8,128)(2,1)}), bf16[8,2,16,7168]{3,2,1,0:T(8,128)(2,1)}, u32[]{:S(2)}, u32[]{:S(2)}) async-start(bf16[8,2,16,7168]{3,2,1,0:T(8,128)(2,1)} %bitcast.91), calls=%async_computation | async-start | bytes 7340032 | tf_op jit(solution)/shard_map/all_to_all | solution.py:27
  11.2 82.0 %collective-permute-start = (bf16[8,16,7168]{2,1,0:T(8,128)(2,1)}, bf16[8,16,7168]{2,1,0:T(8,128)(2,1)}, u32[]{:S(2)}, u32[]{:S(2)}) collective-permute-start(bf16[8,16,7168]{2,1,0:T(8,128)(2,1)} %rows_ref.1), channel_id=1, source_target_pairs={{0,8},{1,9},{2,10},{3,11},{4,12},{5,13},{6,14},{7,15},{8,0},{9,1},... | collective-permute-start | bytes 5505032 | tf_op jit(solution)/shard_map/ppermute | solution.py:23
  17.2 88.8 %copy-start.29 = (s32[8,3]{0,1:T(4,128)S(1)}, s32[8,3]{0,1:T(4,128)}, u32[]{:S(2)}) copy-start(s32[8,3]{0,1:T(4,128)} %param.11) | copy-start | bytes 292
  17.2 90.8 %copy-start.31 = (f32[1,128]{1,0:T(1,128)S(1)}, f32[1,128]{1,0:T(1,128)}, u32[]{:S(2)}) copy-start(f32[1,128]{1,0:T(1,128)} %param.8) | copy-start | bytes 1540
  95.9 0.8 copy-start.13
  96.7 0.8 copy-start.14
  97.5 0.8 copy-start.15
  98.3 0.8 copy-start.16
  99.1 64.0 %all-to-all-start.1 = ((bf16[16,128,512]{2,1,0:T(8,128)(2,1)}), bf16[16,128,512]{2,1,0:T(8,128)(2,1)}, u32[]{:S(2)}, u32[]{:S(2)}) async-start(bf16[16,128,512]{2,1,0:T(8,128)(2,1)} %cut_windows.1), calls=%async_computation.1 | async-start | bytes 4194304 | tf_op jit(solution)/shard_map/all_to_all | solution.py:27
  108.0 7.7 %copy-start.17 = (bf16[1,128,7168]{2,1,0:T(8,128)(2,1)S(1)}, bf16[1,128,7168]{2,1,0:T(8,128)(2,1)}, u32[]{:S(2)}) copy-start(bf16[1,128,7168]{2,1,0:T(8,128)(2,1)} %param.9) | copy-start | bytes 5505028
  111.8 4.2 %copy-start.25 = (f32[7168]{0:T(1024)S(1)}, f32[7168]{0:T(1024)}, u32[]{:S(2)}) copy-start(f32[7168]{0:T(1024)} %param.10) | copy-start | bytes 86020
  111.8 6.3 %collective-permute-start.1 = (bf16[2,16,7168]{2,1,0:T(8,128)(2,1)}, bf16[2,16,7168]{2,1,0:T(8,128)(2,1)S(1)}, u32[]{:S(2)}, u32[]{:S(2)}) collective-permute-start(bf16[2,16,7168]{2,1,0:T(8,128)(2,1)} %get-tuple-element.64), channel_id=1, source_target_pairs={{0,1},{1,0},{2,3},{3,2},{4,5},{5,4},{6,7},{7,6},{8,9},{9,8},{10,11... | collective-permute-start | bytes 1376264 | tf_op jit(solution)/shard_map/ppermute | solution.py:23
  112.2 18.9 %collective-permute-start.2 = (bf16[2,16,7168]{2,1,0:T(8,128)(2,1)}, bf16[2,16,7168]{2,1,0:T(8,128)(2,1)S(1)}, u32[]{:S(2)}, u32[]{:S(2)}) collective-permute-start(bf16[2,16,7168]{2,1,0:T(8,128)(2,1)} %copy-done.16), channel_id=1, source_target_pairs={{0,2},{1,3},{2,0},{3,1},{4,6},{5,7},{6,4},{7,5},{8,10},{9,11},{10,... | collective-permute-start | bytes 1376264 | tf_op jit(solution)/shard_map/ppermute | solution.py:23
  112.5 34.6 %collective-permute-start.3 = (bf16[2,16,7168]{2,1,0:T(8,128)(2,1)}, bf16[2,16,7168]{2,1,0:T(8,128)(2,1)S(1)}, u32[]{:S(2)}, u32[]{:S(2)}) collective-permute-start(bf16[2,16,7168]{2,1,0:T(8,128)(2,1)} %copy-done.15), channel_id=1, source_target_pairs={{0,3},{1,2},{2,1},{3,0},{4,7},{5,6},{6,5},{7,4},{8,11},{9,10},{10,... | collective-permute-start | bytes 1376264 | tf_op jit(solution)/shard_map/ppermute | solution.py:23
  114.0 37.6 %collective-permute-start.4 = (bf16[2,16,7168]{2,1,0:T(8,128)(2,1)}, bf16[2,16,7168]{2,1,0:T(8,128)(2,1)S(1)}, u32[]{:S(2)}, u32[]{:S(2)}) collective-permute-start(bf16[2,16,7168]{2,1,0:T(8,128)(2,1)} %copy-done.14), channel_id=1, source_target_pairs={{0,4},{1,5},{2,6},{3,7},{4,0},{5,1},{6,2},{7,3},{8,12},{9,13},{10,... | collective-permute-start | bytes 1376264 | tf_op jit(solution)/shard_map/ppermute | solution.py:23
  114.3 48.1 %collective-permute-start.5 = (bf16[2,16,7168]{2,1,0:T(8,128)(2,1)}, bf16[2,16,7168]{2,1,0:T(8,128)(2,1)S(1)}, u32[]{:S(2)}, u32[]{:S(2)}) collective-permute-start(bf16[2,16,7168]{2,1,0:T(8,128)(2,1)} %copy-done.13), channel_id=1, source_target_pairs={{0,5},{1,4},{2,7},{3,6},{4,1},{5,0},{6,3},{7,2},{8,13},{9,12},{10,... | collective-permute-start | bytes 1376264 | tf_op jit(solution)/shard_map/ppermute | solution.py:23
  118.1 64.8 %collective-permute-start.7 = (bf16[2,16,7168]{2,1,0:T(8,128)(2,1)}, bf16[2,16,7168]{2,1,0:T(8,128)(2,1)}, u32[]{:S(2)}, u32[]{:S(2)}) collective-permute-start(bf16[2,16,7168]{2,1,0:T(8,128)(2,1)} %get-tuple-element.78), channel_id=1, source_target_pairs={{0,6},{1,7},{2,4},{3,5},{4,2},{5,3},{6,0},{7,1},{8,14},{9,15},{10,... | collective-permute-start | bytes 1376264 | tf_op jit(solution)/shard_map/ppermute | solution.py:23
  131.1 51.8 %collective-permute-start.8 = (bf16[2,16,7168]{2,1,0:T(8,128)(2,1)}, bf16[2,16,7168]{2,1,0:T(8,128)(2,1)}, u32[]{:S(2)}, u32[]{:S(2)}) collective-permute-start(bf16[2,16,7168]{2,1,0:T(8,128)(2,1)} %get-tuple-element.79), channel_id=1, source_target_pairs={{0,7},{1,6},{2,5},{3,4},{4,3},{5,2},{6,1},{7,0},{8,15},{9,14},{10,... | collective-permute-start | bytes 1376264 | tf_op jit(solution)/shard_map/ppermute | solution.py:23
  147.1 0.8 copy-start.7
  151.6 0.8 copy-start.9
  162.4 0.8 copy-start.11
  163.2 8.9 %copy-start.18 = (bf16[1,128,7168]{2,1,0:T(8,128)(2,1)S(1)}, bf16[1,128,7168]{2,1,0:T(8,128)(2,1)}, u32[]{:S(2)}) copy-start(bf16[1,128,7168]{2,1,0:T(8,128)(2,1)} %param.9) | copy-start | bytes 5505028
  171.5 10.0 %collective-permute-start.6 = (bf16[8,2,2,128,128]{4,3,2,1,0:T(8,128)(2,1)S(1)}, bf16[8,2,2,128,128]{4,3,2,1,0:T(8,128)(2,1)S(1)}, u32[]{:S(2)}, u32[]{:S(2)}) collective-permute-start(bf16[8,2,2,128,128]{4,3,2,1,0:T(8,128)(2,1)S(1)} %bitcast.105), channel_id=1, source_target_pairs={{0,1},{1,0},{2,3},{3,2},{4,5},{5,4},{6,7},{7,6},{8,9},{9,8},{10,11... | collective-permute-start | bytes 3145736 | tf_op jit(solution)/shard_map/ppermute | solution.py:23
  175.9 4.7 %copy-start.6 = (bf16[8,16,7168]{2,1,0:T(8,128)(2,1)S(1)}, bf16[8,16,7168]{2,1,0:T(8,128)(2,1)}, u32[]{:S(2)}) copy-start(bf16[8,16,7168]{2,1,0:T(8,128)(2,1)} %rows_ref.1) | copy-start | bytes 5505028
  182.9 60.0 %all-to-all-start.2 = ((bf16[8,2,2,128,128]{4,3,2,1,0:T(8,128)(2,1)}), bf16[8,2,2,128,128]{4,3,2,1,0:T(8,128)(2,1)}, u32[]{:S(2)}, u32[]{:S(2)}) async-start(bf16[8,2,2,128,128]{4,3,2,1,0:T(8,128)(2,1)} %fusion.2), calls=%async_computation.2 | async-start | bytes 2097152 | tf_op jit(solution)/shard_map/all_to_all | solution.py:27
  188.1 1.0 copy-start.8
  189.1 1.0 copy-start.10
  190.2 1.0 copy-start.12
  191.2 4.7 %copy-start.32 = (f32[1,128]{1,0:T(1,128)S(1)}, f32[1,128]{1,0:T(1,128)}, u32[]{:S(2)}) copy-start(f32[1,128]{1,0:T(1,128)} %param.8) | copy-start | bytes 1540
  195.9 3.4 %copy-start.20 = (bf16[8,2,16,7168]{3,2,1,0:T(8,128)(2,1)S(1)}, bf16[8,2,16,7168]{3,2,1,0:T(8,128)(2,1)}, u32[]{:S(2)}) copy-start(bf16[8,2,16,7168]{3,2,1,0:T(8,128)(2,1)} %gather_rows.1) | copy-start | bytes 11010052
  199.3 0.8 copy-start.35
  199.3 0.8 copy-start.34
  199.3 1.0 copy-start.33
  199.3 2.0 copy-start.22
  200.0 2.1 copy-start.19
  200.0 2.1 copy-start.26
  202.1 2.7 copy-start.28
  204.8 25.3 %collective-permute-start.15 = (bf16[2,320,128]{2,1,0:T(8,128)(2,1)S(1)}, bf16[2,320,128]{2,1,0:T(8,128)(2,1)S(1)}, u32[]{:S(2)}, u32[]{:S(2)}) collective-permute-start(bf16[2,320,128]{2,1,0:T(8,128)(2,1)S(1)} %pad_maximum_fusion.1.refs_0_), channel_id=1, source_target_pairs={{0,14},{1,15},{2,12},{3,13},{4,10},{5,11},{6,8},{7,9},{8,6},{9,7},... | collective-permute-start | bytes 491528 | tf_op jit(solution)/shard_map/ppermute | solution.py:23
  206.1 27.2 %collective-permute-start.14 = (bf16[2,320,128]{2,1,0:T(8,128)(2,1)S(1)}, bf16[2,320,128]{2,1,0:T(8,128)(2,1)S(1)}, u32[]{:S(2)}, u32[]{:S(2)}) collective-permute-start(bf16[2,320,128]{2,1,0:T(8,128)(2,1)S(1)} %pad_maximum_fusion.1.refs_0_), channel_id=1, source_target_pairs={{0,12},{1,13},{2,14},{3,15},{4,8},{5,9},{6,10},{7,11},{8,4},{9,5},... | collective-permute-start | bytes 491528 | tf_op jit(solution)/shard_map/ppermute | solution.py:23
  206.4 29.5 %collective-permute-start.13 = (bf16[2,320,128]{2,1,0:T(8,128)(2,1)S(1)}, bf16[2,320,128]{2,1,0:T(8,128)(2,1)S(1)}, u32[]{:S(2)}, u32[]{:S(2)}) collective-permute-start(bf16[2,320,128]{2,1,0:T(8,128)(2,1)S(1)} %pad_maximum_fusion.1.refs_0_), channel_id=1, source_target_pairs={{0,10},{1,11},{2,8},{3,9},{4,14},{5,15},{6,12},{7,13},{8,2},{9,3},... | collective-permute-start | bytes 491528 | tf_op jit(solution)/shard_map/ppermute | solution.py:23
  211.2 28.2 %collective-permute-start.12 = (bf16[2,320,128]{2,1,0:T(8,128)(2,1)S(1)}, bf16[2,320,128]{2,1,0:T(8,128)(2,1)S(1)}, u32[]{:S(2)}, u32[]{:S(2)}) collective-permute-start(bf16[2,320,128]{2,1,0:T(8,128)(2,1)S(1)} %pad_maximum_fusion.1.refs_0_), channel_id=1, source_target_pairs={{0,8},{1,9},{2,10},{3,11},{4,12},{5,13},{6,14},{7,15},{8,0},{9,1},... | collective-permute-start | bytes 491528 | tf_op jit(solution)/shard_map/ppermute | solution.py:23
  211.2 28.2 %collective-permute-start.11 = (bf16[2,320,128]{2,1,0:T(8,128)(2,1)S(1)}, bf16[2,320,128]{2,1,0:T(8,128)(2,1)S(1)}, u32[]{:S(2)}, u32[]{:S(2)}) collective-permute-start(bf16[2,320,128]{2,1,0:T(8,128)(2,1)S(1)} %pad_maximum_fusion.1.refs_0_), channel_id=1, source_target_pairs={{0,6},{1,7},{2,4},{3,5},{4,2},{5,3},{6,0},{7,1},{8,14},{9,15},{10,... | collective-permute-start | bytes 491528 | tf_op jit(solution)/shard_map/ppermute | solution.py:23
  230.2 9.2 %collective-permute-start.10 = (bf16[2,320,128]{2,1,0:T(8,128)(2,1)S(1)}, bf16[2,320,128]{2,1,0:T(8,128)(2,1)S(1)}, u32[]{:S(2)}, u32[]{:S(2)}) collective-permute-start(bf16[2,320,128]{2,1,0:T(8,128)(2,1)S(1)} %pad_maximum_fusion.1.refs_0_), channel_id=1, source_target_pairs={{0,4},{1,5},{2,6},{3,7},{4,0},{5,1},{6,2},{7,3},{8,12},{9,13},{10,... | collective-permute-start | bytes 491528 | tf_op jit(solution)/shard_map/ppermute | solution.py:23
  233.3 6.1 %collective-permute-start.9 = (bf16[2,320,128]{2,1,0:T(8,128)(2,1)S(1)}, bf16[2,320,128]{2,1,0:T(8,128)(2,1)S(1)}, u32[]{:S(2)}, u32[]{:S(2)}) collective-permute-start(bf16[2,320,128]{2,1,0:T(8,128)(2,1)S(1)} %pad_maximum_fusion.1.refs_0_), channel_id=1, source_target_pairs={{0,2},{1,3},{2,0},{3,1},{4,6},{5,7},{6,4},{7,5},{8,10},{9,11},{10,... | collective-permute-start | bytes 491528 | tf_op jit(solution)/shard_map/ppermute | solution.py:23
  239.5 5.5 %copy-start.4 = (bf16[8,2,320,128]{3,2,1,0:T(8,128)(2,1)}, bf16[8,2,320,128]{3,2,1,0:T(8,128)(2,1)S(1)}, u32[]{:S(2)}) copy-start(bf16[8,2,320,128]{3,2,1,0:T(8,128)(2,1)S(1)} %pack.1.same_ref) | copy-start | bytes 3932164
  239.5 5.4 %collective-permute-start.16 = (bf16[8,2,320,128]{3,2,1,0:T(8,128)(2,1)S(1)}, bf16[8,2,320,128]{3,2,1,0:T(8,128)(2,1)S(1)}, u32[]{:S(2)}, u32[]{:S(2)}) collective-permute-start(bf16[8,2,320,128]{3,2,1,0:T(8,128)(2,1)S(1)} %pack.1.same_ref), channel_id=1, source_target_pairs={{0,1},{1,0},{2,3},{3,2},{4,5},{5,4},{6,7},{7,6},{8,9},{9,8},{10,11... | collective-permute-start | bytes 3932168 | tf_op jit(solution)/shard_map/ppermute | solution.py:23
  245.0 1.0 copy-start.23
  255.2 11.1 %copy-start.27 = (bf16[128,128]{1,0:T(8,128)(2,1)S(1)}, bf16[128,128]{1,0:T(8,128)(2,1)}, u32[]{:S(2)}) copy-start(bf16[128,128]{1,0:T(8,128)(2,1)} %convolution_convert_fusion) | copy-start | bytes 98308
  255.2 54.6 %all-to-all-start.3 = ((bf16[16,128,512]{2,1,0:T(8,128)(2,1)}), bf16[16,128,512]{2,1,0:T(8,128)(2,1)}, u32[]{:S(2)}, u32[]{:S(2)}) async-start(bf16[16,128,512]{2,1,0:T(8,128)(2,1)} %decode.1), calls=%async_computation.3 | async-start | bytes 4194304 | tf_op jit(solution)/shard_map/all_to_all | solution.py:27
  262.3 11.1 %copy-start.24 = (f32[256,128]{1,0:T(8,128)S(1)}, f32[256,128]{1,0:T(8,128)}, u32[]{:S(2)}) copy-start(f32[256,128]{1,0:T(8,128)} %fusion.52) | copy-start | bytes 393220
  262.3 11.1 %copy-start.30 = (f32[128]{0:T(128)S(1)}, f32[128]{0:T(128)}, u32[]{:S(2)}) copy-start(f32[128]{0:T(128)} %get-tuple-element.96) | copy-start | bytes 1540
  265.8 7.8 %copy-start.21 = (bf16[8,2,16,7168]{3,2,1,0:T(8,128)(2,1)S(1)}, bf16[8,2,16,7168]{3,2,1,0:T(8,128)(2,1)}, u32[]{:S(2)}) copy-start(bf16[8,2,16,7168]{3,2,1,0:T(8,128)(2,1)} %gather_rows.1) | copy-start | bytes 11010052
  309.9 5.1 %copy-start.1 = (bf16[1,7168,128]{2,1,0:T(8,128)(2,1)S(1)}, bf16[1,7168,128]{2,1,0:T(8,128)(2,1)}, u32[]{:S(2)}) copy-start(bf16[1,7168,128]{2,1,0:T(8,128)(2,1)} %param.7) | copy-start | bytes 5505028
  309.9 2.2 copy-start.2

commit v6 on v5

--- a/solution.py
+++ b/solution.py
@@ -80,16 +80,15 @@
         out_specs=[vmem] * parts,
         out_shape=[jax.ShapeDtypeStruct((MOST,) + rows.shape[1:], rows.dtype)] * parts,
         compiler_params=pltpu.CompilerParams(vmem_limit_bytes=48 * 2**20),
-        cost_estimate=pl.CostEstimate(flops=0, bytes_accessed=6 * rows.size, transcendentals=0),
+        cost_estimate=pl.CostEstimate(flops=0, bytes_accessed=5505024, transcendentals=0),
         name="deal_spans",
     )(index, rows)
 
 
-def gather_kernel(place_ref, *refs):
+def gather_kernel(*refs):
     parts, out_ref, sems = refs[:-2], refs[-2], refs[-1]
     copies = [
-        pltpu.make_async_copy(part, out_ref.at[i ^ place_ref[0]], sems.at[i])
-        for i, part in enumerate(parts)
+        pltpu.make_async_copy(part, out_ref.at[i], sems.at[i]) for i, part in enumerate(parts)
     ]
     for copy in copies:
         copy.start()
@@ -97,21 +96,47 @@
         copy.wait()
 
 
-def gather_rows(parts, place):
+def gather_rows(parts, cost):
     count = len(parts)
     return pl.pallas_call(
         gather_kernel,
-        in_specs=[pl.BlockSpec(memory_space=pltpu.SMEM)]
-        + [pl.BlockSpec(memory_space=pl.ANY)] * count,
+        in_specs=[pl.BlockSpec(memory_space=pl.ANY)] * count,
         out_specs=pl.BlockSpec(memory_space=pltpu.VMEM),
         out_shape=jax.ShapeDtypeStruct((count,) + parts[0].shape, parts[0].dtype),
         scratch_shapes=[pltpu.SemaphoreType.DMA((count,))],
         compiler_params=pltpu.CompilerParams(vmem_limit_bytes=48 * 2**20),
-        cost_estimate=pl.CostEstimate(
-            flops=0, bytes_accessed=4 * count * parts[0].size, transcendentals=0
-        ),
+        cost_estimate=pl.CostEstimate(flops=0, bytes_accessed=cost, transcendentals=0),
         name="gather_rows",
-    )(place, *parts)
+    )(*parts)
+
+
+def order_kernel(place_ref, own_ref, *refs):
+    fars, extra_ref, out_ref = refs[:-2], refs[-2], refs[-1]
+    count, most = own_ref.shape[:2]
+    for slot in range(most):
+        for i in range(count):
+            out_ref[slot, i] = own_ref[i, slot]
+        at = 0
+        for far in fars:
+            for i in range(far.shape[0]):
+                out_ref[slot, count + ((at + i) ^ place_ref[0])] = far[i, slot]
+            at += far.shape[0]
+        for i in range(extra_ref.shape[1]):
+            out_ref[slot, 2 * count + i] = extra_ref[slot, i]
+
+
+def order_rows(place, own, fars, extra):
+    vmem = pl.BlockSpec(memory_space=pltpu.VMEM)
+    count, most, rows, latents = own.shape
+    return pl.pallas_call(
+        order_kernel,
+        in_specs=[pl.BlockSpec(memory_space=pltpu.SMEM)] + [vmem] * (2 + len(fars)),
+        out_specs=vmem,
+        out_shape=jax.ShapeDtypeStruct((most, 2 * count + extra.shape[1], rows, latents), own.dtype),
+        compiler_params=pltpu.CompilerParams(vmem_limit_bytes=48 * 2**20),
+        cost_estimate=pl.CostEstimate(flops=0, bytes_accessed=8 * own.size, transcendentals=0),
+        name="order_rows",
+    )(place, own, *fars, extra)
 
 
 def pack_kernel(*refs):
@@ -155,13 +180,14 @@
         out_specs=pl.BlockSpec(memory_space=pl.ANY),
         out_shape=jax.ShapeDtypeStruct((len(starts), dec.shape[0], window), dec.dtype),
         scratch_shapes=[pltpu.SemaphoreType.DMA((len(starts),))],
-        cost_estimate=pl.CostEstimate(flops=0, bytes_accessed=4 * dec.size, transcendentals=0),
+        cost_estimate=pl.CostEstimate(flops=0, bytes_accessed=0, transcendentals=0),
         name="cut_windows",
     )(dec)
 
 
-def join_kernel(skipped, part_ref, y_ref, out_ref, windows, joined, in_sems, out_sems):
-    count, _, window = y_ref.shape
+def join_kernel(window, skipped, part_ref, y_ref, out_ref, windows, joined, in_sems, out_sems):
+    count, _, lanes = y_ref.shape
+    latents = part_ref.shape[0]
     per_chip = 2 * window - skipped
     arriving, leaving = [], []
     for chip in range(count // 2):
@@ -171,11 +197,20 @@
     for chip in range(count // 2):
         at = chip * per_chip
         arriving[chip].wait()
-        joined[chip, :, :window] = part_ref[:, at : at + window] + windows[2 * chip].astype(f32)
-        joined[chip, :, window:] = (
-            part_ref[:, at + window : at + per_chip]
-            + windows[2 * chip + 1][:, skipped:].astype(f32)
-        )
+        full = (window - skipped) // lanes
+        for core in range(2):
+            for tile in range(full):
+                cols = core * window + tile * lanes
+                joined[chip, :, cols : cols + lanes] = part_ref[
+                    :, at + cols : at + cols + lanes
+                ] + windows[2 * chip + core, tile * latents : (tile + 1) * latents].astype(f32)
+            for tile in range(skipped // lanes):
+                cols = window - skipped + tile * lanes
+                rows = slice(core * latents // 2, (core + 1) * latents // 2)
+                first = full * latents + tile * (latents // 2)
+                joined[chip, rows, cols : cols + lanes] = part_ref[
+                    rows, at + cols : at + cols + lanes
+                ] + windows[2 * chip + core, first : first + latents // 2].astype(f32)
         leaving.append(
             pltpu.make_async_copy(
                 joined.at[chip], out_ref.at[:, pl.ds(at, per_chip)], out_sems.at[chip]
@@ -186,15 +221,18 @@
         copy.wait()
 
 
-def join_windows(part, y, skipped):
-    count, latents, window = y.shape
-    if window % 128 or skipped % 128:
+def in_tiles(window, skipped):
+    return window % 128 == 0 and skipped % 128 == 0
+
+
+def join_windows(part, y, window, skipped):
+    count, latents = y.shape[0], part.shape[0]
+    if not in_tiles(window, skipped):
         cols = [y[i] if i % 2 == 0 else y[i][:, skipped:] for i in range(count)]
         return part + jnp.concatenate(cols, axis=1).astype(f32)
-    vmem = pl.BlockSpec(memory_space=pltpu.VMEM)
-    return pl.pallas_call(
-        functools.partial(join_kernel, skipped),
-        in_specs=[vmem, pl.BlockSpec(memory_space=pl.ANY)],
+    return pl.pallas_call(
+        functools.partial(join_kernel, window, skipped),
+        in_specs=[pl.BlockSpec(memory_space=pltpu.VMEM), pl.BlockSpec(memory_space=pl.ANY)],
         out_specs=pl.BlockSpec(memory_space=pl.ANY),
         out_shape=jax.ShapeDtypeStruct(part.shape, f32),
         scratch_shapes=[
@@ -226,7 +264,7 @@
             )
 
 
-def decode_kernel(names, place_ref, block_ref, same_ref, other_ref, dec_ref, y_ref, total, feats, decs):
+def decode_kernel(names, skipped, place_ref, block_ref, core_ref, same_ref, other_ref, dec_ref, y_ref, total, feats, decs):
     span_count = place_ref.shape[0] // names
     rows, latents = feats.shape[0], same_ref.shape[3]
     total[...] = jnp.zeros_like(total)
@@ -252,19 +290,37 @@
         return carry
 
     lax.fori_loop(0, span_count, span_step, 0, unroll=UNROLL)
-    y_ref[...] = total[...].astype(bf16)
-
-
-def decode(names, rows, place, block, feats, dec):
+    window = decs.shape[1]
+    if not in_tiles(window, skipped):
+        y_ref[...] = total[...].astype(bf16)
+        return
+    core, lanes = core_ref[0], y_ref.shape[2]
+    full, some = (window - skipped) // lanes, latents // 2
+    for tile in range(full):
+        cols = pl.ds(pl.multiple_of(core * skipped + tile * lanes, lanes), lanes)
+        y_ref[:, tile * latents : (tile + 1) * latents] = total[:, :, cols].astype(bf16)
+    for tile in range(skipped // lanes):
+        start = jnp.where(core == 0, window - skipped, 0) + tile * lanes
+        cols = pl.ds(pl.multiple_of(start, lanes), lanes)
+        first = full * latents + tile * some
+        y_ref[:, first : first + some] = total[
+            :, pl.ds(pl.multiple_of(core * some, some), some), cols
+        ].astype(bf16)
+
+
+def decode(names, skipped, rows, place, block, core, feats, dec):
     vmem = pl.BlockSpec(memory_space=pltpu.VMEM)
     smem = pl.BlockSpec(memory_space=pltpu.SMEM)
     pairs, columns = place.shape[0], dec.shape[2]
     latents = feats[0].shape[3]
-    return pl.pallas_call(
-        functools.partial(decode_kernel, names),
-        in_specs=[smem] * 2 + [vmem] * 3,
+    shape = dec.shape
+    if in_tiles(columns, skipped):
+        shape = (dec.shape[0], (2 * columns - skipped) // 2 * latents // 128, 128)
+    return pl.pallas_call(
+        functools.partial(decode_kernel, names, skipped),
+        in_specs=[smem] * 3 + [vmem] * 3,
         out_specs=vmem,
-        out_shape=jax.ShapeDtypeStruct(dec.shape, bf16),
+        out_shape=jax.ShapeDtypeStruct(shape, bf16),
         scratch_shapes=[
             pltpu.VMEM(dec.shape, f32),
             pltpu.VMEM((rows, names * latents), bf16),
@@ -277,7 +333,7 @@
             transcendentals=0,
         ),
         name="decode",
-    )(place, block, *feats, dec)
+    )(place, block, core, *feats, dec)
 
 
 def gram_kernel(names, skipped, land_ref, block_ref, core_ref, dec_ref, out_ref, decs):
@@ -401,17 +457,17 @@
     rows = half * MOST * part_rows
     dot = functools.partial(jnp.dot, preferred_element_type=f32)
     my_live = lax.dynamic_slice(live, (me, 0), (1, MOST)).astype(f32)
-    mask = jnp.broadcast_to(my_live[0][None, :, None, None], shape + (1,)).reshape(rows, 1)
-
-    def by_slot(x):
-        return x.reshape(half, MOST, part_rows, latents).transpose(1, 0, 2, 3).reshape(MOST, -1, latents)
+
+    def masked(x):
+        parted = x.reshape(-1, MOST, part_rows, latents)
+        return jnp.where(my_live[0][None, :, None, None] > 0.0, parted, 0.0).reshape(x.shape)
 
     def by_source(x):
-        return x.reshape(MOST, half, part_rows, latents).transpose(1, 0, 2, 3).reshape(rows, latents)
+        return x.reshape(MOST, half, part_rows, latents).transpose(1, 0, 2, 3)
 
     def encode(x):
         preact = dot(x, enc) + enc_bias[0]
-        feat = jnp.maximum(preact, 0.0) * mask
+        feat = masked(jnp.maximum(preact, 0.0))
         return preact, feat, feat.astype(bf16)
 
     own = x_own.reshape(rows, width)
@@ -443,64 +499,92 @@
     side = ((active % 2) ^ core) * chips
     place = (side + ((active // 2) ^ (me // 2))) * MOST + slot_of
     land = (side + active // 2) * MOST + slot_of
+    my_spans = lax.dynamic_slice(span_of, (me, 0), (1, MOST))[0]
+    my_names = lax.dynamic_slice(name_of, (me, 0), (1, MOST))[0]
+    turn = (my_names[:, None] + jnp.arange(names)) % names
+    my_place = jnp.take_along_axis(place[my_spans], turn, axis=1)
+    indices = tuple(x.reshape(-1) for x in (place, land, active, my_place, core))
     ahead = half - half // 4
-    dec_all, *parts[:ahead] = lax.optimization_barrier((dec_all, *parts[:ahead]))
-    grams = gram(names, skipped, land.reshape(-1), active.reshape(-1), core.reshape(1), dec_all)
+    first_far = gather_rows(parts[:ahead], 1000000).reshape(-1, width)
+    dec_all, indices, first_far = lax.optimization_barrier((dec_all, indices, first_far))
+    place, land, block, my_place, core_only = indices
+    grams = gram(names, skipped, land, block, core_only, dec_all)
     grams = grams.reshape(2, chips, MOST, names - 1, latents, latents)
     near = swap(grams[1], 1, count)
     near = (grams[0].astype(f32) + near.astype(f32)).astype(bf16)
 
-    near, xd_own, fx_own, constant, gram_self, act_sum, *parts = lax.optimization_barrier(
-        (near, xd_own, fx_own, constant, gram_self, act_sum, *parts)
+    far = [(first_far, encode(first_far))]
+    near, xd_own, fx_own, constant, gram_self, act_sum, far[0], *parts[ahead:] = (
+        lax.optimization_barrier(
+            (near, xd_own, fx_own, constant, gram_self, act_sum, far[0], *parts[ahead:])
+        )
     )
     gram_in = jnp.sum(exchange(near, same_core).astype(f32), axis=0).astype(bf16)
-    far = gather_rows(parts, (me % half).reshape(1)).reshape(rows, width)
-    preact_far, feat_far, fb_far = encode(far)
-    feature_sum = jnp.sum(feat_own, axis=0) + jnp.sum(feat_far, axis=0)
-    rounded_sum = jnp.sum(fb_own.astype(f32), axis=0) + jnp.sum(fb_far.astype(f32), axis=0)
-    bias_sum = jnp.sum(rounded_sum[:, None] * weights, axis=0) - act_sum
+    last_far = gather_rows(parts[ahead:], 0).reshape(-1, width)
+    far.append((last_far, encode(last_far)))
+    encoded = [(own, (preact_own, feat_own, fb_own))] + far
+
+    feature_sum = sum(jnp.sum(e[1], axis=0) for _, e in encoded)
+    rounded_sum = sum(jnp.sum(e[2].astype(f32), axis=0) for _, e in encoded)
+    total = lax.reduce_precision(rounded_sum, 8, 7)
+    total = jnp.stack([total, rounded_sum - total]).astype(bf16)
+    bias_sum = jnp.sum(dot(total, dec), axis=0) - act_sum
     coarse = lax.reduce_precision(bias_sum, 8, 7)
     fine = (bias_sum - coarse).astype(bf16)
-    coarse = coarse.astype(bf16)
-    extra = jnp.stack([coarse, fine]).reshape(MOST, -1, latents)
-    extra = jnp.pad(extra, ((0, 0), (0, -extra.shape[1] % 16), (0, 0)))
-    feats = jnp.concatenate([by_slot(fb_own), by_slot(fb_far), extra], axis=1)
-    same = pack([feats] + [swap(feats, 2 * i, count) for i in range(1, chips)])
-    feats = (same, swap(same, 1, count))
-
-    behind, _ = lax.optimization_barrier((far, fb_far))
-    xd_far = cross(behind, dec)
-    fx = fx_own + down(fb_far, behind)
+    extra = jnp.stack([coarse.astype(bf16), fine]).reshape(MOST, -1, latents)
+    extra = jnp.pad(extra, ((0, 0), (0, -extra.shape[1] % part_rows), (0, 0)))
+    extra = extra.reshape(MOST, -1, part_rows, latents)
+    in_parts = [e[2].reshape(-1, MOST, part_rows, latents) for _, e in encoded]
+    feats = order_rows((me % half).reshape(1), in_parts[0], in_parts[1:], extra)
+    feats = feats.reshape(MOST, -1, latents)
+    over = swap(feats, half, count)
+    behind, over = lax.optimization_barrier(([x for x, _ in far], over))
+    same = [x if i == 0 else swap(x, 2 * i, count) for x in (feats, over) for i in range(chips // 2)]
+    xd_far = [cross(x, dec) for x in behind]
+    fx = fx_own + sum(down(e[2], x) for x, (_, e) in zip(behind, far))
     dec_part = (
         grad_scale * (rounded_sum[:, None] * dec_bias[None, :] - fx)
         + penalty_weight * feature_sum[:, None] * weights * inverse
     )
+    xd_far, dec_part, *same = lax.optimization_barrier((xd_far, dec_part, *same))
+    same = pack(same)
+    feats = (same, swap(same, 1, count))
+
     feats, gram_in = lax.optimization_barrier((feats, gram_in))
+    y_out = decode(
+        names,
+        skipped,
+        2 * half * part_rows,
+        place,
+        block,
+        core_only,
+        feats,
+        dec_all,
+    )
+    y_in = exchange(y_out)
+
+    r_own, r_far = back(
+        names,
+        2 * half * part_rows,
+        my_place,
+        feats,
+        jnp.concatenate([jnp.broadcast_to(gram_self, (MOST, 1) + gram_self.shape), gram_in], axis=1),
+    )
+    r_own, feats = lax.optimization_barrier((r_own, feats))
     last = [x[:, :, rows // MOST * 2 : rows // MOST * 2 + width // latents] for x in feats]
     bias_sum = sum(jnp.sum(x.astype(f32), axis=(0, 1)) for x in last).reshape(width)
     dec_bias_grad = grad_scale * (bias_sum + float(span_count * part_rows * count) * dec_bias)
-
-    y_out = decode(names, 2 * half * part_rows, place.reshape(-1), active.reshape(-1), feats, dec_all)
-    y_in = exchange(y_out)
-
-    my_spans = lax.dynamic_slice(span_of, (me, 0), (1, MOST))[0]
-    my_names = lax.dynamic_slice(name_of, (me, 0), (1, MOST))[0]
-    turn = (my_names[:, None] + jnp.arange(names)) % names
-    r_own, r_far = back(
-        names,
-        2 * half * part_rows,
-        jnp.take_along_axis(place[my_spans], turn, axis=1).reshape(-1),
-        feats,
-        jnp.concatenate([jnp.broadcast_to(gram_self, (MOST, 1) + gram_self.shape), gram_in], axis=1),
-    )
-    r_own, r_far = by_source(r_own), by_source(r_far)
-
-    grad_own = jnp.where((preact_own > 0.0) & (mask > 0.0), r_own - grad_scale * xd_own + constant, 0.0)
-    grad_far = jnp.where((preact_far > 0.0) & (mask > 0.0), r_far - grad_scale * xd_far + constant, 0.0)
-    bias_grad = jnp.sum(grad_own, axis=0) + jnp.sum(grad_far, axis=0)
-    enc_grad = down(own, grad_own.astype(bf16)) + down(far, grad_far.astype(bf16))
-
-    dec_grad = join_windows(dec_part, y_in, skipped)
+    r_far = by_source(r_far)[(me % half) ^ jnp.arange(half)]
+    r_parts = [by_source(r_own), r_far[:ahead], r_far[ahead:]]
+
+    bias_grad, enc_grad = 0.0, 0.0
+    for (x, (preact, _, _)), r, xd in zip(encoded, r_parts, [xd_own] + xd_far):
+        grad = r.reshape(preact.shape) - grad_scale * xd + constant
+        grad = masked(jnp.where(preact > 0.0, grad, 0.0))
+        bias_grad = bias_grad + jnp.sum(grad, axis=0)
+        enc_grad = enc_grad + down(x, grad.astype(bf16))
+
+    dec_grad = join_windows(dec_part, y_in, window, skipped)
     return (enc_grad[None], bias_grad[None], dec_grad[None], dec_bias_grad)
 
 

time: 316 us -> 294 us (0.930)
  waiting for transfers between devices: 167 us -> 140 us
  local copies, waits for them, and re-layouts: 26.7 us -> 20.5 us
  other arithmetic: 13.9 us -> 20 us
  matrix products: 26.5 us -> 32.2 us
    ppermute x17, waiting for transfers between devices: 141 us -> 119 us  [swap(): return lax.ppermute(x, AXIS, [(i, i ^ distance) for i in range(count)])]
    unnamed x73 -> x61, local copies, waits for them, and re-layouts: 17 us -> 9.72 us
    dot_general x4 -> x8, matrix products: 9.63 us -> 14.6 us  [the longest x3 8.32 us: shards(): enc_grad = enc_grad + down(x, grad.astype(bf16))]
    all_to_all x4, waiting for transfers between devices: 26.2 us -> 21.4 us  [exchange(): lax.all_to_all(x, AXIS, split_axis=0, concat_axis=0, tiled=True, axis_ind...]
    reduce_sum x1 -> x5, other arithmetic: 0.12 us -> 3.43 us  [the longest x3 2.31 us: shards(): bias_grad = bias_grad + jnp.sum(grad, axis=0)]
    pallas_call x3 -> x5, Pallas kernels: 16.9 us -> 15.6 us  [the longest x1 9.43 us: decode(): pl.pallas_call(functools.partial(decode_kernel, names, skipped), in_specs...]
    dot_general x2 -> x3, matrix products: 7.17 us -> 7.72 us  [encode(): preact = dot(x, enc) + enc_bias[0]]
  transfers between devices with their start and end apart: 21 -> 21, of which waited for: 11 -> 10; matrix products, arithmetic and copies ran while one was open for 16% -> 20% of each run, Pallas kernels for 6% -> 7%
where the time goes in v6:
time: 294 us; the launch traced here: 292 us
  waiting for transfers between devices  140 us (48%)
  starting transfers between devices  43.8 us (15%)
  Pallas kernels  34.4 us (12%)
  matrix products  32.2 us (11%)
  local copies, waits for them, and re-layouts  20.5 us (7%)
  other arithmetic  20 us (7%)
    ppermute x17, waiting for transfers between devices, swap(): return lax.ppermute(x, AXIS, [(i, i ^ distance) for i in range(count)])  119 us
    all_to_all x4, starting transfers between devices, exchange(): lax.all_to_all(x, AXIS, split_axis=0, concat_axis=0, tiled=True, axis_ind...  23.5 us
    all_to_all x4, waiting for transfers between devices, exchange(): lax.all_to_all(x, AXIS, split_axis=0, concat_axis=0, tiled=True, axis_ind...  21.4 us
    ppermute x17, starting transfers between devices, swap(): return lax.ppermute(x, AXIS, [(i, i ^ distance) for i in range(count)])  20.3 us
    unnamed x61, local copies, waits for them, and re-layouts  9.72 us
    pallas_call x1, Pallas kernels, decode(): pl.pallas_call(functools.partial(decode_kernel, names, skipped), in_specs...  9.43 us
    dot_general x3, matrix products, shards(): enc_grad = enc_grad + down(x, grad.astype(bf16))  8.32 us
    dot_general x3, matrix products, encode(): preact = dot(x, enc) + enc_bias[0]  7.72 us
  transfers between devices with their start and end apart: 21, of which 10 were waited for; matrix products, arithmetic and copies ran while one was open for 20% of the time, Pallas kernels for 7%

profile of v6, /device:TPU:15, one launch (start us, length us, event | category | flops | bytes accessed | tf_op | source)
XLA Modules:
  0.0 292.4 jit_solution(7910869979844965299)
XLA Ops:
  0.7 0.9 fusion.42
  1.9 1.5 copy-done.7
  3.4 0.9 pick_spans.1
  4.2 1.8 copy-done.6
  6.1 5.1 %all-to-all-start = ((bf16[8,2,16,7168]{3,2,1,0:T(8,128)(2,1)}), bf16[8,2,16,7168]{3,2,1,0:T(8,128)(2,1)}, u32[]{:S(2)}, u32[]{:S(2)}) async-start(bf16[8,2,16,7168]{3,2,1,0:T(8,128)(2,1)} %bitcast.129), calls=%async_computation | async-start | bytes 7340032 | tf_op jit(solution)/shard_map/all_to_all | solution.py:27
  11.2 2.3 collective-permute-start
  14.9 3.0 %cut_windows.1 = bf16[16,128,512]{2,1,0:T(8,128)(2,1)} custom-call(bf16[128,7168]{1,0:T(8,128)(2,1)} %bitcast.139), custom_call_target="tpu_custom_call" | custom-call | tf_op jit(solution)/shard_map/cut_windows/pallas_call | solution.py:177
  17.8 75.4 %collective-permute-done.rows_ref = bf16[8,16,7168]{2,1,0:T(8,128)(2,1)} collective-permute-done((bf16[8,16,7168]{2,1,0:T(8,128)(2,1)}, bf16[8,16,7168]{2,1,0:T(8,128)(2,1)}, u32[]{:S(2)}, u32[]{:S(2)}) %collective-permute-start) | collective-permute-done | bytes 1835040 | tf_op jit(solution)/shard_map/ppermute | solution.py:23
  93.3 3.1 %deal_spans.1 = (bf16[2,16,7168]{2,1,0:T(8,128)(2,1)S(1)}, bf16[2,16,7168]{2,1,0:T(8,128)(2,1)S(1)}, bf16[2,16,7168]{2,1,0:T(8,128)(2,1)S(1)}, bf16[2,16,7168]{2...) custom-call(s32[16]{0:T(128)S(1)} %reshape.372.index_ref, ...), custom_call_target="tpu_custom_call" | custom-call | bytes 5505024 | tf_op jit(solution)/shard_map/deal_spans/pallas_call | solution.py:77
  96.3 0.8 copy-done.9
  97.1 6.9 %all-to-all-start.1 = ((bf16[16,128,512]{2,1,0:T(8,128)(2,1)}), bf16[16,128,512]{2,1,0:T(8,128)(2,1)}, u32[]{:S(2)}, u32[]{:S(2)}) async-start(bf16[16,128,512]{2,1,0:T(8,128)(2,1)} %cut_windows.1), calls=%async_computation.1 | async-start | bytes 4194304 | tf_op jit(solution)/shard_map/all_to_all | solution.py:27
  111.0 1.9 convert_element_type.90
  113.6 1.5 collective-permute-start.3
  115.4 1.4 collective-permute-start.5
  118.1 3.9 %fusion.71 = f32[256,128]{1,0:T(8,128)} fusion(bf16[256,7168]{1,0:T(8,128)(2,1)} %bitcast.3, bf16[128,7168]{1,0:T(8,128)(2,1)S(1)} %bitcast.142), kind=kOutput, calls=%fused_computation.135 | convolution fusion | flops 469762048 | bytes 5636096 | tf_op jit(solution)/shard_map/dot_general | solution.py:494
  122.4 3.9 %convert_reduce_fusion.3 = (f32[128]{0:T(128)S(1)}, bf16[256,128]{1,0:T(8,128)(2,1)S(1)}, f32[128]{0:T(128)S(1)}, f32[256,128]{1,0:T(8,128)}) fusion(pred[256]{0:T(512)(128)(4,1)S(1)} %broadcast_in_dim.117, f32[128]{0:T(128)S(1)} %bitcast.154, bf16[256,7168]{1,0:T(8,128)(2,1)} %bitcast.3, bf16[1,7168,128]{2,1,0:T(8,128)(2,1)S(1)} %copy-done), kind=kOutput, calls=%fused_computation.37 | convolution fusion | flops 470056704 | bytes 5703424 | tf_op jit(solution)/shard_map/dot_general | solution.py:469
  126.3 4.7 %collective-permute-done.2.refs_2_ = bf16[2,16,7168]{2,1,0:T(8,128)(2,1)S(1)} collective-permute-done((bf16[2,16,7168]{2,1,0:T(8,128)(2,1)S(1)}, bf16[2,16,7168]{2,1,0:T(8,128)(2,1)S(1)}, u32[]{:S(2)}, u32[]{:S(2)}) %collective-permute-start.2) | collective-permute-done | bytes 458784 | tf_op jit(solution)/shard_map/ppermute | solution.py:23
  131.0 5.6 %collective-permute-start.8 = (bf16[2,16,7168]{2,1,0:T(8,128)(2,1)}, bf16[2,16,7168]{2,1,0:T(8,128)(2,1)S(1)}, u32[]{:S(2)}, u32[]{:S(2)}) collective-permute-start(bf16[2,16,7168]{2,1,0:T(8,128)(2,1)} %get-tuple-element.92), channel_id=1, source_target_pairs={{0,7},{1,6},{2,5},{3,4},{4,3},{5,2},{6,1},{7,0},{8,15},{9,14},{10,... | collective-permute-start | bytes 1376264 | tf_op jit(solution)/shard_map/ppermute | solution.py:23
  136.7 10.0 %collective-permute-done.3.refs_3_ = bf16[2,16,7168]{2,1,0:T(8,128)(2,1)S(1)} collective-permute-done((bf16[2,16,7168]{2,1,0:T(8,128)(2,1)}, bf16[2,16,7168]{2,1,0:T(8,128)(2,1)S(1)}, u32[]{:S(2)}, u32[]{:S(2)}) %collective-permute-start.3) | collective-permute-done | bytes 458784 | tf_op jit(solution)/shard_map/ppermute | solution.py:23
  146.7 2.9 collective-permute-done.4.refs_4_
  149.6 10.7 %collective-permute-done.5.refs_5_ = bf16[2,16,7168]{2,1,0:T(8,128)(2,1)S(1)} collective-permute-done((bf16[2,16,7168]{2,1,0:T(8,128)(2,1)}, bf16[2,16,7168]{2,1,0:T(8,128)(2,1)S(1)}, u32[]{:S(2)}, u32[]{:S(2)}) %collective-permute-start.5) | collective-permute-done | bytes 458784 | tf_op jit(solution)/shard_map/ppermute | solution.py:23
  160.3 1.7 gather_rows.2
  162.0 1.5 copy-done.2
  163.5 6.4 %gram.1 = bf16[64,128,128]{2,1,0:T(8,128)(2,1)} custom-call(s32[24]{0:T(128)} %reshape.375.land_ref, s32[24]{0:T(128)} %reshape.376.block_ref, s32[1]{0:T(128)} %bitcast.10.core_ref, bf16[16,128,512]{2,1,0:T(8,128)(2,1)} %all-to-all-done.1.dec_ref), custom_call_target="tpu_custom_call" | custom-call | flops 1207959552 | bytes 4194304 | tf_op jit(solution)/shard_map/gram/pallas_call | solution.py:371
  169.9 1.9 fusion.70
  172.0 1.2 convolution_convert_fusion
  173.3 4.7 %fusion.72 = f32[128,7168]{1,0:T(8,128)} fusion(bf16[256,128]{1,0:T(8,128)(2,1)S(1)} %get-tuple-element.141, bf16[256,7168]{1,0:T(8,128)(2,1)} %bitcast.3), kind=kOutput, calls=%fused_computation.136 | convolution fusion | flops 469762048 | bytes 7405568 | tf_op jit(solution)/shard_map/dot_general | solution.py:495
  178.0 1.6 fusion.68
  179.6 1.4 fusion.2
  181.1 1.5 gather_rows.3
  182.6 2.2 convert_reduce_fusion.5
  185.3 1.5 collective-permute-start.9
  186.8 1.6 collective-permute-start.11
  188.4 1.2 collective-permute-start.12
  189.6 5.3 %all-to-all-start.2 = ((bf16[8,2,2,128,128]{4,3,2,1,0:T(8,128)(2,1)}), bf16[8,2,2,128,128]{4,3,2,1,0:T(8,128)(2,1)}, u32[]{:S(2)}, u32[]{:S(2)}) async-start(bf16[8,2,2,128,128]{4,3,2,1,0:T(8,128)(2,1)} %fusion.2), calls=%async_computation.2 | async-start | bytes 2097152 | tf_op jit(solution)/shard_map/all_to_all | solution.py:27
  194.9 1.1 reduce_sum.198
  196.7 1.8 fusion.75
  199.6 1.0 copy-done.14
  201.3 3.2 %fusion.1.part_ref = f32[128,7168]{1,0:T(8,128)} fusion(f32[128,3584]{1,0:T(8,128)S(1)} %broadcast_in_dim.128, f32[128,3584]{1,0:T(8,128)S(1)} %broadcast_in_dim.127, f32[128,7168]{1,0:T(8,128)S(1)} %copy-done.14, f32[128,7168]{1,0:T(8,128)S(1)} %convolution_add_fusion.2, f32[128]{0:T(128)S(1)} %add_multiply_fusion, f32[128]{0:T(128)S(1)} %get-tuple-element.139, ...), kind=kLoop, calls=%fused_computation.10 | loop fusion | flops 8257536 | bytes 16544768 | tf_op jit(solution)/shard_map/add | solution.py:546
  204.5 0.9 fusion.73
  205.4 2.1 collective-permute-start.15
  207.5 2.5 fusion.74
  210.1 1.1 collective-permute-done.13.refs_5_
  211.2 8.8 %collective-permute-done.14.refs_6_ = bf16[2,320,128]{2,1,0:T(8,128)(2,1)S(1)} collective-permute-done((bf16[2,320,128]{2,1,0:T(8,128)(2,1)S(1)}, bf16[2,320,128]{2,1,0:T(8,128)(2,1)S(1)}, u32[]{:S(2)}, u32[]{:S(2)}) %collective-permute-start.14) | collective-permute-done | bytes 163872 | tf_op jit(solution)/shard_map/ppermute | solution.py:23
  220.0 3.5 %collective-permute-done.15.refs_7_ = bf16[2,320,128]{2,1,0:T(8,128)(2,1)S(1)} collective-permute-done((bf16[2,320,128]{2,1,0:T(8,128)(2,1)S(1)}, bf16[2,320,128]{2,1,0:T(8,128)(2,1)S(1)}, u32[]{:S(2)}, u32[]{:S(2)}) %collective-permute-start.15) | collective-permute-done | bytes 163872 | tf_op jit(solution)/shard_map/ppermute | solution.py:23
  223.4 2.1 pack.1.same_ref
  225.5 1.2 collective-permute-start.16
  226.7 1.4 reduce_sum.200
  228.1 1.6 collective-permute-done.16.other_ref
  229.7 9.4 %decode.1 = bf16[16,448,128]{2,1,0:T(8,128)(2,1)} custom-call(s32[24]{0:T(128)} %reshape.374.place_ref, s32[24]{0:T(128)} %reshape.376.block_ref, s32[1]{0:T(128)} %bitcast.10.core_ref, bf16[8,2,320,128]{3,2,1,0:T(8,128)(2,1)} %pack.1.same_ref, bf16[8,2,320,128]{3,2,1,0:T(8,128)(2,1)} %collective-permute-done.16.other_ref, ...), custom_call_target="tpu_custom_call" | custom-call | flops 1610612736 | bytes 6815744 | tf_op jit(solution)/shard_map/decode/pallas_call | solution.py:319
  239.1 6.2 %all-to-all-start.3 = ((bf16[16,448,128]{2,1,0:T(8,128)(2,1)}), bf16[16,448,128]{2,1,0:T(8,128)(2,1)}, u32[]{:S(2)}, u32[]{:S(2)}) async-start(bf16[16,448,128]{2,1,0:T(8,128)(2,1)} %decode.1), calls=%async_computation.3 | async-start | bytes 3670016 | tf_op jit(solution)/shard_map/all_to_all | solution.py:27
  246.2 3.5 %back.1 = (f32[2,128,128]{2,1,0:T(8,128)}, f32[2,128,128]{2,1,0:T(8,128)}) custom-call(s32[6]{0:T(128)} %and_select_fusion.1.place_ref, bf16[8,2,320,128]{3,2,1,0:T(8,128)(2,1)} %pack.1.same_ref, bf16[8,2,320,128]{3,2,1,0:T(8,128)(2,1)} %collective-permute-done.16.other_ref, bf16[2,3,128,128]{3,2,1,0:T(8,128)(2,1)} %pad_maximum_fusion.gram_ref), custom_call_target="tpu_custom_call" | custom-call | flops 50331648 | bytes 524288 | tf_op jit(solution)/shard_map/back/pallas_call | solution.py:408
  249.6 1.5 gather_fusion.3
  251.1 0.9 copy.57
  252.0 1.0 convert_reduce_fusion.1
  253.0 1.0 convert_reduce_fusion.2
  254.0 0.8 fusion.64
  255.6 0.8 fusion.62
  257.5 3.2 %fusion.28 = f32[7168,128]{1,0:T(8,128)S(1)} fusion(bf16[256,7168]{1,0:T(8,128)(2,1)} %bitcast.3, bf16[256,128]{1,0:T(8,128)(2,1)S(1)} %get-tuple-element.135), kind=kOutput, calls=%fused_computation.50 | convolution fusion | flops 469762048 | bytes 7405568 | tf_op jit(solution)/shard_map/dot_general | solution.py:585
  260.7 1.2 convolution_add_fusion.1
  262.0 3.9 %fusion = f32[1,7168,128]{2,1,0:T(8,128)} fusion(f32[7168,128]{1,0:T(8,128)S(1)} %convolution_add_fusion.1, bf16[64,7168]{1,0:T(8,128)(2,1)} %bitcast.14, bf16[64,128]{1,0:T(8,128)(2,1)S(1)} %get-tuple-element.137), kind=kOutput, calls=%fused_computation.6 | convolution fusion | flops 118358016 | bytes 8273920 | tf_op jit(solution)/shard_map/dot_general | solution.py:585
  265.9 21.4 %all-to-all-done.3.y_ref = bf16[16,448,128]{2,1,0:T(8,128)(2,1)} async-done(((bf16[16,448,128]{2,1,0:T(8,128)(2,1)}), bf16[16,448,128]{2,1,0:T(8,128)(2,1)}, u32[]{:S(2)}, u32[]{:S(2)}) %all-to-all-start.3) | async-done | bytes 1835040 | tf_op jit(solution)/shard_map/all_to_all | solution.py:27
  287.3 2.0 copy-done.5
  289.3 2.9 %join_windows.1 = f32[128,7168]{1,0:T(8,128)} custom-call(f32[128,7168]{1,0:T(8,128)S(1)} %copy-done.5, bf16[16,448,128]{2,1,0:T(8,128)(2,1)} %all-to-all-done.3.y_ref), custom_call_target="tpu_custom_call" | custom-call | flops 917504 | bytes 7340032 | tf_op jit(solution)/shard_map/join_windows/pallas_call | solution.py:233
  (142 shorter events, 17.1 us)
Async XLA Ops:
  0.6 121.7 %copy-start = (bf16[1,7168,128]{2,1,0:T(8,128)(2,1)S(1)}, bf16[1,7168,128]{2,1,0:T(8,128)(2,1)}, u32[]{:S(2)}) copy-start(bf16[1,7168,128]{2,1,0:T(8,128)(2,1)} %param.7) | copy-start | bytes 5505028
  1.9 1.5 copy-start.7
  4.2 1.8 copy-start.6
  6.1 91.1 %all-to-all-start = ((bf16[8,2,16,7168]{3,2,1,0:T(8,128)(2,1)}), bf16[8,2,16,7168]{3,2,1,0:T(8,128)(2,1)}, u32[]{:S(2)}, u32[]{:S(2)}) async-start(bf16[8,2,16,7168]{3,2,1,0:T(8,128)(2,1)} %bitcast.129), calls=%async_computation | async-start | bytes 7340032 | tf_op jit(solution)/shard_map/all_to_all | solution.py:27
  11.2 82.0 %collective-permute-start = (bf16[8,16,7168]{2,1,0:T(8,128)(2,1)}, bf16[8,16,7168]{2,1,0:T(8,128)(2,1)}, u32[]{:S(2)}, u32[]{:S(2)}) collective-permute-start(bf16[8,16,7168]{2,1,0:T(8,128)(2,1)} %rows_ref.1), channel_id=1, source_target_pairs={{0,8},{1,9},{2,10},{3,11},{4,12},{5,13},{6,14},{7,15},{8,0},{9,1},... | collective-permute-start | bytes 5505032 | tf_op jit(solution)/shard_map/ppermute | solution.py:23
  17.8 86.2 %copy-start.26 = (s32[8,3]{0,1:T(4,128)S(1)}, s32[8,3]{0,1:T(4,128)}, u32[]{:S(2)}) copy-start(s32[8,3]{0,1:T(4,128)} %param.11) | copy-start | bytes 292
  96.3 0.8 copy-start.9
  97.1 66.4 %all-to-all-start.1 = ((bf16[16,128,512]{2,1,0:T(8,128)(2,1)}), bf16[16,128,512]{2,1,0:T(8,128)(2,1)}, u32[]{:S(2)}, u32[]{:S(2)}) async-start(bf16[16,128,512]{2,1,0:T(8,128)(2,1)} %cut_windows.1), calls=%async_computation.1 | async-start | bytes 4194304 | tf_op jit(solution)/shard_map/all_to_all | solution.py:27
  104.6 17.7 %copy-start.23 = (pred[256]{0:T(512)(128)(4,1)}, pred[256]{0:T(512)(128)(4,1)S(1)}, u32[]{:S(2)}) copy-start(pred[256]{0:T(512)(128)(4,1)S(1)} %broadcast_in_dim.117) | copy-start | bytes 772
  109.6 68.4 %copy-start.25 = (pred[192]{0:T(512)(128)(4,1)}, pred[192]{0:T(512)(128)(4,1)S(1)}, u32[]{:S(2)}) copy-start(pred[192]{0:T(512)(128)(4,1)S(1)} %broadcast_in_dim.122) | copy-start | bytes 580
  109.7 72.9 %copy-start.28 = (pred[64]{0:T(512)(128)(4,1)}, pred[64]{0:T(512)(128)(4,1)S(1)}, u32[]{:S(2)}) copy-start(pred[64]{0:T(512)(128)(4,1)S(1)} %broadcast_in_dim.125) | copy-start | bytes 196
  112.8 4.3 %copy-start.11 = (bf16[1,128,7168]{2,1,0:T(8,128)(2,1)S(1)}, bf16[1,128,7168]{2,1,0:T(8,128)(2,1)}, u32[]{:S(2)}) copy-start(bf16[1,128,7168]{2,1,0:T(8,128)(2,1)} %param.9) | copy-start | bytes 5505028
  112.8 4.3 %copy-start.18 = (f32[7168]{0:T(1024)S(1)}, f32[7168]{0:T(1024)}, u32[]{:S(2)}) copy-start(f32[7168]{0:T(1024)} %param.10) | copy-start | bytes 86020
  112.8 13.4 %collective-permute-start.1 = (bf16[2,16,7168]{2,1,0:T(8,128)(2,1)S(1)}, bf16[2,16,7168]{2,1,0:T(8,128)(2,1)S(1)}, u32[]{:S(2)}, u32[]{:S(2)}) collective-permute-start(bf16[2,16,7168]{2,1,0:T(8,128)(2,1)S(1)} %get-tuple-element.78), channel_id=1, source_target_pairs={{0,1},{1,0},{2,3},{3,2},{4,5},{5,4},{6,7},{7,6},{8,9},{9,8},{10,11... | collective-permute-start | bytes 1376264 | tf_op jit(solution)/shard_map/ppermute | solution.py:23
  113.3 17.8 %collective-permute-start.2 = (bf16[2,16,7168]{2,1,0:T(8,128)(2,1)S(1)}, bf16[2,16,7168]{2,1,0:T(8,128)(2,1)S(1)}, u32[]{:S(2)}, u32[]{:S(2)}) collective-permute-start(bf16[2,16,7168]{2,1,0:T(8,128)(2,1)S(1)} %get-tuple-element.79), channel_id=1, source_target_pairs={{0,2},{1,3},{2,0},{3,1},{4,6},{5,7},{6,4},{7,5},{8,10},{9,11},{10,... | collective-permute-start | bytes 1376264 | tf_op jit(solution)/shard_map/ppermute | solution.py:23
  113.6 33.1 %collective-permute-start.3 = (bf16[2,16,7168]{2,1,0:T(8,128)(2,1)}, bf16[2,16,7168]{2,1,0:T(8,128)(2,1)S(1)}, u32[]{:S(2)}, u32[]{:S(2)}) collective-permute-start(bf16[2,16,7168]{2,1,0:T(8,128)(2,1)} %get-tuple-element.80), channel_id=1, source_target_pairs={{0,3},{1,2},{2,1},{3,0},{4,7},{5,6},{6,5},{7,4},{8,11},{9,10},{10,... | collective-permute-start | bytes 1376264 | tf_op jit(solution)/shard_map/ppermute | solution.py:23
  115.1 34.5 %collective-permute-start.4 = (bf16[2,16,7168]{2,1,0:T(8,128)(2,1)}, bf16[2,16,7168]{2,1,0:T(8,128)(2,1)S(1)}, u32[]{:S(2)}, u32[]{:S(2)}) collective-permute-start(bf16[2,16,7168]{2,1,0:T(8,128)(2,1)} %get-tuple-element.81), channel_id=1, source_target_pairs={{0,4},{1,5},{2,6},{3,7},{4,0},{5,1},{6,2},{7,3},{8,12},{9,13},{10,... | collective-permute-start | bytes 1376264 | tf_op jit(solution)/shard_map/ppermute | solution.py:23
  115.4 44.9 %collective-permute-start.5 = (bf16[2,16,7168]{2,1,0:T(8,128)(2,1)}, bf16[2,16,7168]{2,1,0:T(8,128)(2,1)S(1)}, u32[]{:S(2)}, u32[]{:S(2)}) collective-permute-start(bf16[2,16,7168]{2,1,0:T(8,128)(2,1)} %get-tuple-element.82), channel_id=1, source_target_pairs={{0,5},{1,4},{2,7},{3,6},{4,1},{5,0},{6,3},{7,2},{8,13},{9,12},{10,... | collective-permute-start | bytes 1376264 | tf_op jit(solution)/shard_map/ppermute | solution.py:23
  118.1 3.9 %copy-start.8 = (bf16[8,16,7168]{2,1,0:T(8,128)(2,1)S(1)}, bf16[8,16,7168]{2,1,0:T(8,128)(2,1)}, u32[]{:S(2)}) copy-start(bf16[8,16,7168]{2,1,0:T(8,128)(2,1)} %rows_ref.1) | copy-start | bytes 5505028
  118.1 4.3 %copy-start.27 = (f32[1,128]{1,0:T(1,128)S(1)}, f32[1,128]{1,0:T(1,128)}, u32[]{:S(2)}) copy-start(f32[1,128]{1,0:T(1,128)} %param.8) | copy-start | bytes 1540
  122.4 37.9 %copy-start.10 = (bf16[2,16,7168]{2,1,0:T(8,128)(2,1)S(1)}, bf16[2,16,7168]{2,1,0:T(8,128)(2,1)}, u32[]{:S(2)}) copy-start(bf16[2,16,7168]{2,1,0:T(8,128)(2,1)} %copy-done.9) | copy-start | bytes 1376260
  126.2 54.8 %collective-permute-start.7 = (bf16[2,16,7168]{2,1,0:T(8,128)(2,1)}, bf16[2,16,7168]{2,1,0:T(8,128)(2,1)S(1)}, u32[]{:S(2)}, u32[]{:S(2)}) collective-permute-start(bf16[2,16,7168]{2,1,0:T(8,128)(2,1)} %get-tuple-element.91), channel_id=1, source_target_pairs={{0,6},{1,7},{2,4},{3,5},{4,2},{5,3},{6,0},{7,1},{8,14},{9,15},{10,... | collective-permute-start | bytes 1376264 | tf_op jit(solution)/shard_map/ppermute | solution.py:23
  131.0 50.0 %collective-permute-start.8 = (bf16[2,16,7168]{2,1,0:T(8,128)(2,1)}, bf16[2,16,7168]{2,1,0:T(8,128)(2,1)S(1)}, u32[]{:S(2)}, u32[]{:S(2)}) collective-permute-start(bf16[2,16,7168]{2,1,0:T(8,128)(2,1)} %get-tuple-element.92), channel_id=1, source_target_pairs={{0,7},{1,6},{2,5},{3,4},{4,3},{5,2},{6,1},{7,0},{8,15},{9,14},{10,... | collective-permute-start | bytes 1376264 | tf_op jit(solution)/shard_map/ppermute | solution.py:23
  161.9 1.5 copy-start.2
  169.9 2.1 copy-start.12
  171.8 7.8 %collective-permute-start.6 = (bf16[8,2,2,128,128]{4,3,2,1,0:T(8,128)(2,1)S(1)}, bf16[8,2,2,128,128]{4,3,2,1,0:T(8,128)(2,1)S(1)}, u32[]{:S(2)}, u32[]{:S(2)}) collective-permute-start(bf16[8,2,2,128,128]{4,3,2,1,0:T(8,128)(2,1)S(1)} %bitcast.150), channel_id=1, source_target_pairs={{0,1},{1,0},{2,3},{3,2},{4,5},{5,4},{6,7},{7,6},{8,9},{9,8},{10,11... | collective-permute-start | bytes 3145736 | tf_op jit(solution)/shard_map/ppermute | solution.py:23
  173.3 4.7 %copy-start.3 = (bf16[6,2,16,7168]{3,2,1,0:T(8,128)(2,1)S(1)}, bf16[6,2,16,7168]{3,2,1,0:T(8,128)(2,1)}, u32[]{:S(2)}) copy-start(bf16[6,2,16,7168]{3,2,1,0:T(8,128)(2,1)} %copy-done.2) | copy-start | bytes 8257540
  185.3 10.7 %collective-permute-start.9 = (bf16[2,320,128]{2,1,0:T(8,128)(2,1)S(1)}, bf16[2,320,128]{2,1,0:T(8,128)(2,1)S(1)}, u32[]{:S(2)}, u32[]{:S(2)}) collective-permute-start(bf16[2,320,128]{2,1,0:T(8,128)(2,1)S(1)} %bitcast.131), channel_id=1, source_target_pairs={{0,8},{1,9},{2,10},{3,11},{4,12},{5,13},{6,14},{7,15},{8,0},{9,1},... | collective-permute-start | bytes 491528 | tf_op jit(solution)/shard_map/ppermute | solution.py:23
  186.8 18.6 %collective-permute-start.10 = (bf16[2,320,128]{2,1,0:T(8,128)(2,1)S(1)}, bf16[2,320,128]{2,1,0:T(8,128)(2,1)S(1)}, u32[]{:S(2)}, u32[]{:S(2)}) collective-permute-start(bf16[2,320,128]{2,1,0:T(8,128)(2,1)S(1)} %bitcast.132), channel_id=1, source_target_pairs={{0,2},{1,3},{2,0},{3,1},{4,6},{5,7},{6,4},{7,5},{8,10},{9,11},{10,... | collective-permute-start | bytes 491528 | tf_op jit(solution)/shard_map/ppermute | solution.py:23
  186.8 23.2 %collective-permute-start.11 = (bf16[2,320,128]{2,1,0:T(8,128)(2,1)S(1)}, bf16[2,320,128]{2,1,0:T(8,128)(2,1)S(1)}, u32[]{:S(2)}, u32[]{:S(2)}) collective-permute-start(bf16[2,320,128]{2,1,0:T(8,128)(2,1)S(1)} %bitcast.133), channel_id=1, source_target_pairs={{0,4},{1,5},{2,6},{3,7},{4,0},{5,1},{6,2},{7,3},{8,12},{9,13},{10,... | collective-permute-start | bytes 491528 | tf_op jit(solution)/shard_map/ppermute | solution.py:23
  188.4 21.7 %collective-permute-start.12 = (bf16[2,320,128]{2,1,0:T(8,128)(2,1)S(1)}, bf16[2,320,128]{2,1,0:T(8,128)(2,1)}, u32[]{:S(2)}, u32[]{:S(2)}) collective-permute-start(bf16[2,320,128]{2,1,0:T(8,128)(2,1)S(1)} %bitcast.134), channel_id=1, source_target_pairs={{0,6},{1,7},{2,4},{3,5},{4,2},{5,3},{6,0},{7,1},{8,14},{9,15},{10,... | collective-permute-start | bytes 491528 | tf_op jit(solution)/shard_map/ppermute | solution.py:23
  189.6 37.1 %all-to-all-start.2 = ((bf16[8,2,2,128,128]{4,3,2,1,0:T(8,128)(2,1)}), bf16[8,2,2,128,128]{4,3,2,1,0:T(8,128)(2,1)}, u32[]{:S(2)}, u32[]{:S(2)}) async-start(bf16[8,2,2,128,128]{4,3,2,1,0:T(8,128)(2,1)} %fusion.2), calls=%async_computation.2 | async-start | bytes 2097152 | tf_op jit(solution)/shard_map/all_to_all | solution.py:27
  194.9 3.6 %copy-start.4 = (bf16[6,2,16,7168]{3,2,1,0:T(8,128)(2,1)S(1)}, bf16[6,2,16,7168]{3,2,1,0:T(8,128)(2,1)}, u32[]{:S(2)}) copy-start(bf16[6,2,16,7168]{3,2,1,0:T(8,128)(2,1)} %copy-done.2) | copy-start | bytes 8257540
  196.0 15.2 %collective-permute-start.13 = (bf16[2,320,128]{2,1,0:T(8,128)(2,1)S(1)}, bf16[2,320,128]{2,1,0:T(8,128)(2,1)S(1)}, u32[]{:S(2)}, u32[]{:S(2)}) collective-permute-start(bf16[2,320,128]{2,1,0:T(8,128)(2,1)S(1)} %collective-permute-done.9.refs_4_), channel_id=1, source_target_pairs={{0,2},{1,3},{2,0},{3,1},{4,6},{5,7},{6,4},{7,5},{8,10},{9,11},{10,... | collective-permute-start | bytes 491528 | tf_op jit(solution)/shard_map/ppermute | solution.py:23
  196.4 23.6 %collective-permute-start.14 = (bf16[2,320,128]{2,1,0:T(8,128)(2,1)S(1)}, bf16[2,320,128]{2,1,0:T(8,128)(2,1)S(1)}, u32[]{:S(2)}, u32[]{:S(2)}) collective-permute-start(bf16[2,320,128]{2,1,0:T(8,128)(2,1)S(1)} %collective-permute-done.9.refs_4_), channel_id=1, source_target_pairs={{0,4},{1,5},{2,6},{3,7},{4,0},{5,1},{6,2},{7,3},{8,12},{9,13},{10,... | collective-permute-start | bytes 491528 | tf_op jit(solution)/shard_map/ppermute | solution.py:23
  198.5 2.0 copy-start.14
  199.2 2.1 copy-start.13
  205.4 18.0 %collective-permute-start.15 = (bf16[2,320,128]{2,1,0:T(8,128)(2,1)S(1)}, bf16[2,320,128]{2,1,0:T(8,128)(2,1)S(1)}, u32[]{:S(2)}, u32[]{:S(2)}) collective-permute-start(bf16[2,320,128]{2,1,0:T(8,128)(2,1)S(1)} %collective-permute-done.9.refs_4_), channel_id=1, source_target_pairs={{0,6},{1,7},{2,4},{3,5},{4,2},{5,3},{6,0},{7,1},{8,14},{9,15},{10,... | collective-permute-start | bytes 491528 | tf_op jit(solution)/shard_map/ppermute | solution.py:23
  225.5 4.2 %collective-permute-start.16 = (bf16[8,2,320,128]{3,2,1,0:T(8,128)(2,1)}, bf16[8,2,320,128]{3,2,1,0:T(8,128)(2,1)}, u32[]{:S(2)}, u32[]{:S(2)}) collective-permute-start(bf16[8,2,320,128]{3,2,1,0:T(8,128)(2,1)} %pack.1.same_ref), channel_id=1, source_target_pairs={{0,1},{1,0},{2,3},{3,2},{4,5},{5,4},{6,7},{7,6},{8,9},{9,8},{10,11... | collective-permute-start | bytes 3932168 | tf_op jit(solution)/shard_map/ppermute | solution.py:23
  239.1 6.3 %copy-start.29 = (s32[8]{0:T(128)S(1)}, s32[8]{0:T(128)}, u32[]{:S(2)}) copy-start(s32[8]{0:T(128)} %get-tuple-element.161) | copy-start | bytes 100
  239.1 6.3 %copy-start.20 = (bf16[128,128]{1,0:T(8,128)(2,1)S(1)}, bf16[128,128]{1,0:T(8,128)(2,1)}, u32[]{:S(2)}) copy-start(bf16[128,128]{1,0:T(8,128)(2,1)} %convolution_convert_fusion) | copy-start | bytes 98308
  239.1 48.1 %all-to-all-start.3 = ((bf16[16,448,128]{2,1,0:T(8,128)(2,1)}), bf16[16,448,128]{2,1,0:T(8,128)(2,1)}, u32[]{:S(2)}, u32[]{:S(2)}) async-start(bf16[16,448,128]{2,1,0:T(8,128)(2,1)} %decode.1), calls=%async_computation.3 | async-start | bytes 3670016 | tf_op jit(solution)/shard_map/all_to_all | solution.py:27
  245.3 8.7 %copy-start.21 = (f32[64,128]{1,0:T(8,128)S(1)}, f32[64,128]{1,0:T(8,128)}, u32[]{:S(2)}) copy-start(f32[64,128]{1,0:T(8,128)} %get-tuple-element.159) | copy-start | bytes 98308
  245.3 8.7 %copy-start.22 = (f32[64,128]{1,0:T(8,128)S(1)}, f32[64,128]{1,0:T(8,128)}, u32[]{:S(2)}) copy-start(f32[64,128]{1,0:T(8,128)} %fusion.74) | copy-start | bytes 98308
  245.4 9.4 %copy-start.15 = (f32[192,128]{1,0:T(8,128)S(1)}, f32[192,128]{1,0:T(8,128)}, u32[]{:S(2)}) copy-start(f32[192,128]{1,0:T(8,128)} %get-tuple-element.120) | copy-start | bytes 294916
  245.4 10.2 %copy-start.16 = (f32[256,128]{1,0:T(8,128)S(1)}, f32[256,128]{1,0:T(8,128)}, u32[]{:S(2)}) copy-start(f32[256,128]{1,0:T(8,128)} %fusion.71) | copy-start | bytes 393220
  245.4 10.2 %copy-start.17 = (f32[256,128]{1,0:T(8,128)S(1)}, f32[256,128]{1,0:T(8,128)}, u32[]{:S(2)}) copy-start(f32[256,128]{1,0:T(8,128)} %get-tuple-element.158) | copy-start | bytes 393220
  245.4 10.2 %copy-start.24 = (pred[256]{0:T(512)(128)(4,1)S(1)}, pred[256]{0:T(512)(128)(4,1)}, u32[]{:S(2)}) copy-start(pred[256]{0:T(512)(128)(4,1)} %copy-done.23) | copy-start | bytes 772
  245.4 11.5 %copy-start.19 = (f32[7168]{0:T(1024)S(1)}, f32[7168]{0:T(1024)}, u32[]{:S(2)}) copy-start(f32[7168]{0:T(1024)} %param.10) | copy-start | bytes 86020
  262.0 30.3 %copy-start.1 = (bf16[1,7168,128]{2,1,0:T(8,128)(2,1)S(1)}, bf16[1,7168,128]{2,1,0:T(8,128)(2,1)}, u32[]{:S(2)}) copy-start(bf16[1,7168,128]{2,1,0:T(8,128)(2,1)} %param.7) | copy-start | bytes 5505028
  287.3 2.0 copy-start.5

commit v7 on v6

--- a/solution.py
+++ b/solution.py
@@ -185,32 +185,36 @@
     )(dec)
 
 
-def join_kernel(window, skipped, part_ref, y_ref, out_ref, windows, joined, in_sems, out_sems):
+def join_kernel(window, skipped, part_ref, y_ref, out_ref, windows, joined, in_sems, part_sems, out_sems):
     count, _, lanes = y_ref.shape
     latents = part_ref.shape[0]
     per_chip = 2 * window - skipped
-    arriving, leaving = [], []
+    arriving, held, leaving = [], [], []
     for chip in range(count // 2):
         pair = pl.ds(2 * chip, 2)
         arriving.append(pltpu.make_async_copy(y_ref.at[pair], windows.at[pair], in_sems.at[chip]))
         arriving[-1].start()
+        cols = pl.ds(chip * per_chip, per_chip)
+        held.append(pltpu.make_async_copy(part_ref.at[:, cols], joined.at[chip], part_sems.at[chip]))
+        held[-1].start()
     for chip in range(count // 2):
         at = chip * per_chip
         arriving[chip].wait()
+        held[chip].wait()
         full = (window - skipped) // lanes
         for core in range(2):
             for tile in range(full):
                 cols = core * window + tile * lanes
-                joined[chip, :, cols : cols + lanes] = part_ref[
-                    :, at + cols : at + cols + lanes
-                ] + windows[2 * chip + core, tile * latents : (tile + 1) * latents].astype(f32)
+                joined[chip, :, cols : cols + lanes] += windows[
+                    2 * chip + core, tile * latents : (tile + 1) * latents
+                ].astype(f32)
             for tile in range(skipped // lanes):
                 cols = window - skipped + tile * lanes
                 rows = slice(core * latents // 2, (core + 1) * latents // 2)
                 first = full * latents + tile * (latents // 2)
-                joined[chip, rows, cols : cols + lanes] = part_ref[
-                    rows, at + cols : at + cols + lanes
-                ] + windows[2 * chip + core, first : first + latents // 2].astype(f32)
+                joined[chip, rows, cols : cols + lanes] += windows[
+                    2 * chip + core, first : first + latents // 2
+                ].astype(f32)
         leaving.append(
             pltpu.make_async_copy(
                 joined.at[chip], out_ref.at[:, pl.ds(at, per_chip)], out_sems.at[chip]
@@ -232,12 +236,13 @@
         return part + jnp.concatenate(cols, axis=1).astype(f32)
     return pl.pallas_call(
         functools.partial(join_kernel, window, skipped),
-        in_specs=[pl.BlockSpec(memory_space=pltpu.VMEM), pl.BlockSpec(memory_space=pl.ANY)],
+        in_specs=[pl.BlockSpec(memory_space=pltpu.HBM)] * 2,
         out_specs=pl.BlockSpec(memory_space=pl.ANY),
         out_shape=jax.ShapeDtypeStruct(part.shape, f32),
         scratch_shapes=[
             pltpu.VMEM(y.shape, y.dtype),
             pltpu.VMEM((count // 2, latents, 2 * window - skipped), f32),
+            pltpu.SemaphoreType.DMA((count // 2,)),
             pltpu.SemaphoreType.DMA((count // 2,)),
             pltpu.SemaphoreType.DMA((count // 2,)),
         ],
@@ -361,7 +366,7 @@
                 ]
         return carry
 
-    lax.fori_loop(0, span_count, span_step, 0)
+    lax.fori_loop(0, span_count, span_step, 0, unroll=UNROLL)
 
 
 def gram(names, skipped, land, block, core, dec):
@@ -384,13 +389,19 @@
     )(land, block, core, dec)
 
 
-def back_kernel(names, place_ref, same_ref, other_ref, gram_ref, r_own_ref, r_far_ref):
+def back_kernel(names, place_ref, same_ref, other_ref, self_ref, gram_ref, r_own_ref, r_far_ref):
     r_own_ref[...] = jnp.zeros_like(r_own_ref)
     r_far_ref[...] = jnp.zeros_like(r_far_ref)
     rows = 2 * r_own_ref.shape[1]
     for slot in range(r_own_ref.shape[0]):
         for name in range(names):
-            weight = gram_ref[slot, name]
+            if name == 0:
+                weight = self_ref[...]
+            else:
+                weight = gram_ref[0, slot, name - 1].astype(f32)
+                for chip in range(1, gram_ref.shape[0]):
+                    weight += gram_ref[chip, slot, name - 1].astype(f32)
+                weight = weight.astype(bf16)
 
             def store(same, own, far):
                 own_part = jnp.dot(own, weight, preferred_element_type=f32) * grad_scale
@@ -401,13 +412,13 @@
             take_feats(place_ref[slot * names + name], rows, (same_ref, other_ref), store)
 
 
-def back(names, rows, place, feats, grams):
+def back(names, rows, place, feats, self_gram, grams):
     vmem = pl.BlockSpec(memory_space=pltpu.VMEM)
     smem = pl.BlockSpec(memory_space=pltpu.SMEM)
     _, most, _, latents = feats[0].shape
     return pl.pallas_call(
         functools.partial(back_kernel, names),
-        in_specs=[smem] + [vmem] * 3,
+        in_specs=[smem] + [vmem] * 4,
         out_specs=[vmem, vmem],
         out_shape=[jax.ShapeDtypeStruct((most, rows // 2, latents), f32)] * 2,
         compiler_params=pltpu.CompilerParams(vmem_limit_bytes=56 * 2**20),
@@ -417,7 +428,7 @@
             transcendentals=0,
         ),
         name="back",
-    )(place, *feats, grams)
+    )(place, *feats, self_gram, grams)
 
 
 def shards(activations, enc_weight, enc_bias, dec_weight, dec_bias, active):
@@ -504,7 +515,7 @@
     turn = (my_names[:, None] + jnp.arange(names)) % names
     my_place = jnp.take_along_axis(place[my_spans], turn, axis=1)
     indices = tuple(x.reshape(-1) for x in (place, land, active, my_place, core))
-    ahead = half - half // 4
+    ahead = half * 5 // 8
     first_far = gather_rows(parts[:ahead], 1000000).reshape(-1, width)
     dec_all, indices, first_far = lax.optimization_barrier((dec_all, indices, first_far))
     place, land, block, my_place, core_only = indices
@@ -519,7 +530,7 @@
             (near, xd_own, fx_own, constant, gram_self, act_sum, far[0], *parts[ahead:])
         )
     )
-    gram_in = jnp.sum(exchange(near, same_core).astype(f32), axis=0).astype(bf16)
+    gram_in = exchange(near, same_core)
     last_far = gather_rows(parts[ahead:], 0).reshape(-1, width)
     far.append((last_far, encode(last_far)))
     encoded = [(own, (preact_own, feat_own, fb_own))] + far
@@ -561,6 +572,7 @@
         feats,
         dec_all,
     )
+    feats, y_out = lax.optimization_barrier((feats, y_out))
     y_in = exchange(y_out)
 
     r_own, r_far = back(
@@ -568,7 +580,8 @@
         2 * half * part_rows,
         my_place,
         feats,
-        jnp.concatenate([jnp.broadcast_to(gram_self, (MOST, 1) + gram_self.shape), gram_in], axis=1),
+        gram_self,
+        gram_in,
     )
     r_own, feats = lax.optimization_barrier((r_own, feats))
     last = [x[:, :, rows // MOST * 2 : rows // MOST * 2 + width // latents] for x in feats]

time: 294 us -> 291 us (0.990)
  waiting for transfers between devices: 140 us -> 147 us
  other arithmetic: 20 us -> 14.9 us
  matrix products: 32.2 us -> 27.7 us
    all_to_all x4, waiting for transfers between devices: 21.4 us -> 25 us  [exchange(): lax.all_to_all(x, AXIS, split_axis=0, concat_axis=0, tiled=True, axis_ind...]
    ppermute x17, waiting for transfers between devices: 119 us -> 122 us  [swap(): return lax.ppermute(x, AXIS, [(i, i ^ distance) for i in range(count)])]
    unnamed x61 -> x63, local copies, waits for them, and re-layouts: 9.72 us -> 9.88 us
  transfers between devices with their start and end apart: 21 -> 21, of which waited for: 10 -> 10; matrix products, arithmetic and copies ran while one was open for 20% -> 18% of each run, Pallas kernels for 7% -> 6%
where the time goes in v7:
time: 291 us; the launch traced here: 290 us
  waiting for transfers between devices  147 us (51%)
  starting transfers between devices  46.2 us (16%)
  Pallas kernels  32.9 us (11%)
  matrix products  27.7 us (10%)
  local copies, waits for them, and re-layouts  20.8 us (7%)
  other arithmetic  14.9 us (5%)
    ppermute x17, waiting for transfers between devices, swap(): return lax.ppermute(x, AXIS, [(i, i ^ distance) for i in range(count)])  122 us
    all_to_all x4, waiting for transfers between devices, exchange(): lax.all_to_all(x, AXIS, split_axis=0, concat_axis=0, tiled=True, axis_ind...  25 us
    all_to_all x4, starting transfers between devices, exchange(): lax.all_to_all(x, AXIS, split_axis=0, concat_axis=0, tiled=True, axis_ind...  24.4 us
    ppermute x17, starting transfers between devices, swap(): return lax.ppermute(x, AXIS, [(i, i ^ distance) for i in range(count)])  21.8 us
    unnamed x63, local copies, waits for them, and re-layouts  9.88 us
    pallas_call x1, Pallas kernels, decode(): pl.pallas_call(functools.partial(decode_kernel, names, skipped), in_specs...  9.43 us
    dot_general x3, matrix products, shards(): enc_grad = enc_grad + down(x, grad.astype(bf16))  6.97 us
    dot_general x3, matrix products, encode(): preact = dot(x, enc) + enc_bias[0]  6.3 us
  transfers between devices with their start and end apart: 21, of which 10 were waited for; matrix products, arithmetic and copies ran while one was open for 18% of the time, Pallas kernels for 6%

profile of v7, /device:TPU:15, one launch (start us, length us, event | category | flops | bytes accessed | tf_op | source)
XLA Modules:
  0.0 290.5 jit_solution(18358684798697962710)
XLA Ops:
  0.7 0.9 fusion.42
  1.9 1.5 copy-done.10
  3.4 0.9 pick_spans.1
  4.2 1.8 copy-done.9
  6.1 5.1 %all-to-all-start = ((bf16[8,2,16,7168]{3,2,1,0:T(8,128)(2,1)}), bf16[8,2,16,7168]{3,2,1,0:T(8,128)(2,1)}, u32[]{:S(2)}, u32[]{:S(2)}) async-start(bf16[8,2,16,7168]{3,2,1,0:T(8,128)(2,1)} %bitcast.133), calls=%async_computation | async-start | bytes 7340032 | tf_op jit(solution)/shard_map/all_to_all | solution.py:27
  11.2 2.3 collective-permute-start
  14.7 3.0 %cut_windows.1 = bf16[16,128,512]{2,1,0:T(8,128)(2,1)} custom-call(bf16[128,7168]{1,0:T(8,128)(2,1)} %bitcast.143), custom_call_target="tpu_custom_call" | custom-call | tf_op jit(solution)/shard_map/cut_windows/pallas_call | solution.py:177
  17.7 75.5 %collective-permute-done.rows_ref = bf16[8,16,7168]{2,1,0:T(8,128)(2,1)} collective-permute-done((bf16[8,16,7168]{2,1,0:T(8,128)(2,1)}, bf16[8,16,7168]{2,1,0:T(8,128)(2,1)}, u32[]{:S(2)}, u32[]{:S(2)}) %collective-permute-start) | collective-permute-done | bytes 1835040 | tf_op jit(solution)/shard_map/ppermute | solution.py:23
  93.3 3.3 %deal_spans.1 = (bf16[2,16,7168]{2,1,0:T(8,128)(2,1)S(1)}, bf16[2,16,7168]{2,1,0:T(8,128)(2,1)S(1)}, bf16[2,16,7168]{2,1,0:T(8,128)(2,1)}, bf16[2,16,7168]{2,1,0...) custom-call(s32[16]{0:T(128)S(1)} %reshape.372.index_ref, ...), custom_call_target="tpu_custom_call" | custom-call | bytes 5505024 | tf_op jit(solution)/shard_map/deal_spans/pallas_call | solution.py:77
  96.5 7.0 %all-to-all-start.1 = ((bf16[16,128,512]{2,1,0:T(8,128)(2,1)}), bf16[16,128,512]{2,1,0:T(8,128)(2,1)}, u32[]{:S(2)}, u32[]{:S(2)}) async-start(bf16[16,128,512]{2,1,0:T(8,128)(2,1)} %cut_windows.1), calls=%async_computation.1 | async-start | bytes 4194304 | tf_op jit(solution)/shard_map/all_to_all | solution.py:27
  105.1 0.7 reshape.374.place_ref
  109.4 0.7 gather_fusion.4
  110.7 1.9 convert_element_type.88
  113.3 1.5 collective-permute-start.3
  115.1 1.4 collective-permute-start.6
  117.8 3.3 %fusion.71 = f32[256,128]{1,0:T(8,128)S(1)} fusion(bf16[256,7168]{1,0:T(8,128)(2,1)} %bitcast.3, bf16[128,7168]{1,0:T(8,128)(2,1)S(1)} %bitcast.146), kind=kOutput, calls=%fused_computation.134 | convolution fusion | flops 469762048 | bytes 5636096 | tf_op jit(solution)/shard_map/dot_general | solution.py:505
  121.4 4.3 %convert_reduce_fusion.3 = (f32[128]{0:T(128)S(1)}, bf16[256,128]{1,0:T(8,128)(2,1)S(1)}, f32[128]{0:T(128)}, f32[256,128]{1,0:T(8,128)}) fusion(pred[256]{0:T(512)(128)(4,1)S(1)} %broadcast_in_dim.114, f32[128]{0:T(128)S(1)} %bitcast.158, bf16[256,7168]{1,0:T(8,128)(2,1)} %bitcast.3, bf16[1,7168,128]{2,1,0:T(8,128)(2,1)S(1)} %copy-done), kind=kOutput, calls=%fused_computation.36 | convolution fusion | flops 470056704 | bytes 5703424 | tf_op jit(solution)/shard_map/dot_general | solution.py:480
  125.8 5.1 %collective-permute-done.2.refs_2_ = bf16[2,16,7168]{2,1,0:T(8,128)(2,1)S(1)} collective-permute-done((bf16[2,16,7168]{2,1,0:T(8,128)(2,1)}, bf16[2,16,7168]{2,1,0:T(8,128)(2,1)S(1)}, u32[]{:S(2)}, u32[]{:S(2)}) %collective-permute-start.2) | collective-permute-done | bytes 458784 | tf_op jit(solution)/shard_map/ppermute | solution.py:23
  130.9 5.5 %collective-permute-start.8 = (bf16[2,16,7168]{2,1,0:T(8,128)(2,1)}, bf16[2,16,7168]{2,1,0:T(8,128)(2,1)}, u32[]{:S(2)}, u32[]{:S(2)}) collective-permute-start(bf16[2,16,7168]{2,1,0:T(8,128)(2,1)} %get-tuple-element.96), channel_id=1, source_target_pairs={{0,7},{1,6},{2,5},{3,4},{4,3},{5,2},{6,1},{7,0},{8,15},{9,14},{10,... | collective-permute-start | bytes 1376264 | tf_op jit(solution)/shard_map/ppermute | solution.py:23
  136.4 10.0 %collective-permute-done.3.refs_3_ = bf16[2,16,7168]{2,1,0:T(8,128)(2,1)S(1)} collective-permute-done((bf16[2,16,7168]{2,1,0:T(8,128)(2,1)}, bf16[2,16,7168]{2,1,0:T(8,128)(2,1)S(1)}, u32[]{:S(2)}, u32[]{:S(2)}) %collective-permute-start.3) | collective-permute-done | bytes 458784 | tf_op jit(solution)/shard_map/ppermute | solution.py:23
  146.4 2.7 collective-permute-done.4.refs_4_
  149.1 1.4 gather_rows.2
  150.5 1.4 copy-done.2
  151.9 5.2 %gram.1 = bf16[64,128,128]{2,1,0:T(8,128)(2,1)} custom-call(s32[24]{0:T(128)} %reshape.375.land_ref, s32[24]{0:T(128)} %reshape.376.block_ref, s32[1]{0:T(128)} %bitcast.10.core_ref, bf16[16,128,512]{2,1,0:T(8,128)(2,1)} %all-to-all-done.1.dec_ref), custom_call_target="tpu_custom_call" | custom-call | flops 1207959552 | bytes 4194304 | tf_op jit(solution)/shard_map/gram/pallas_call | solution.py:376
  157.1 1.9 fusion.70
  159.0 1.3 collective-permute-start.5
  160.3 1.2 convolution_convert_fusion.self_ref
  161.6 4.7 %fusion.72 = f32[128,7168]{1,0:T(8,128)} fusion(bf16[256,128]{1,0:T(8,128)(2,1)S(1)} %get-tuple-element.149, bf16[256,7168]{1,0:T(8,128)(2,1)} %bitcast.3), kind=kOutput, calls=%fused_computation.135 | convolution fusion | flops 469762048 | bytes 7405568 | tf_op jit(solution)/shard_map/dot_general | solution.py:506
  166.3 1.4 fusion.68
  167.7 1.4 fusion.2
  169.2 9.1 %collective-permute-done.8.refs_2_ = bf16[2,16,7168]{2,1,0:T(8,128)(2,1)} collective-permute-done((bf16[2,16,7168]{2,1,0:T(8,128)(2,1)}, bf16[2,16,7168]{2,1,0:T(8,128)(2,1)}, u32[]{:S(2)}, u32[]{:S(2)}) %collective-permute-start.8) | collective-permute-done | bytes 458784 | tf_op jit(solution)/shard_map/ppermute | solution.py:23
  178.3 1.6 gather_rows.3
  180.0 1.2 copy-done.5
  182.1 2.2 collective-permute-start.9
  184.3 0.9 collective-permute-start.10
  185.3 1.6 collective-permute-start.11
  187.0 6.4 %all-to-all-start.2 = ((bf16[8,2,2,128,128]{4,3,2,1,0:T(8,128)(2,1)}), bf16[8,2,2,128,128]{4,3,2,1,0:T(8,128)(2,1)}, u32[]{:S(2)}, u32[]{:S(2)}) async-start(bf16[8,2,2,128,128]{4,3,2,1,0:T(8,128)(2,1)} %fusion.2), calls=%async_computation.2 | async-start | bytes 2097152 | tf_op jit(solution)/shard_map/all_to_all | solution.py:27
  193.8 0.8 collective-permute-start.14
  194.6 2.0 fusion.75
  197.7 0.9 copy-done.15
  198.7 0.7 copy-done.14
  199.4 3.2 %fusion.1.part_ref = f32[128,7168]{1,0:T(8,128)} fusion(f32[128,3584]{1,0:T(8,128)S(1)} %broadcast_in_dim.125, f32[128,3584]{1,0:T(8,128)S(1)} %broadcast_in_dim.124, f32[128,7168]{1,0:T(8,128)S(1)} %copy-done.15, f32[128,7168]{1,0:T(8,128)S(1)} %convolution_add_fusion.2, f32[128]{0:T(128)S(1)} %add_multiply_fusion, f32[128]{0:T(128)S(1)} %get-tuple-element.147, ...), kind=kLoop, calls=%fused_computation.10 | loop fusion | flops 8257536 | bytes 16544768 | tf_op jit(solution)/shard_map/add | solution.py:557
  202.6 0.8 fusion.73
  203.4 1.6 collective-permute-start.15
  205.0 1.4 fusion.74
  206.4 3.5 %collective-permute-done.13.refs_5_ = bf16[2,320,128]{2,1,0:T(8,128)(2,1)S(1)} collective-permute-done((bf16[2,320,128]{2,1,0:T(8,128)(2,1)S(1)}, bf16[2,320,128]{2,1,0:T(8,128)(2,1)S(1)}, u32[]{:S(2)}, u32[]{:S(2)}) %collective-permute-start.13) | collective-permute-done | bytes 163872 | tf_op jit(solution)/shard_map/ppermute | solution.py:23
  209.9 7.4 %collective-permute-done.14.refs_6_ = bf16[2,320,128]{2,1,0:T(8,128)(2,1)S(1)} collective-permute-done((bf16[2,320,128]{2,1,0:T(8,128)(2,1)S(1)}, bf16[2,320,128]{2,1,0:T(8,128)(2,1)S(1)}, u32[]{:S(2)}, u32[]{:S(2)}) %collective-permute-start.14) | collective-permute-done | bytes 163872 | tf_op jit(solution)/shard_map/ppermute | solution.py:23
  217.3 5.4 %collective-permute-done.15.refs_7_ = bf16[2,320,128]{2,1,0:T(8,128)(2,1)S(1)} collective-permute-done((bf16[2,320,128]{2,1,0:T(8,128)(2,1)S(1)}, bf16[2,320,128]{2,1,0:T(8,128)(2,1)S(1)}, u32[]{:S(2)}, u32[]{:S(2)}) %collective-permute-start.15) | collective-permute-done | bytes 163872 | tf_op jit(solution)/shard_map/ppermute | solution.py:23
  222.7 1.1 pack.1.same_ref
  223.8 1.0 collective-permute-start.16
  224.8 3.0 %collective-permute-done.16.other_ref = bf16[8,2,320,128]{3,2,1,0:T(8,128)(2,1)} collective-permute-done((bf16[8,2,320,128]{3,2,1,0:T(8,128)(2,1)}, bf16[8,2,320,128]{3,2,1,0:T(8,128)(2,1)}, u32[]{:S(2)}, u32[]{:S(2)}) %collective-permute-start.16) | collective-permute-done | bytes 1310752 | tf_op jit(solution)/shard_map/ppermute | solution.py:23
  227.8 9.4 %decode.1 = bf16[16,448,128]{2,1,0:T(8,128)(2,1)} custom-call(s32[24]{0:T(128)} %reshape.374.place_ref, s32[24]{0:T(128)} %reshape.376.block_ref, s32[1]{0:T(128)} %bitcast.10.core_ref, bf16[8,2,320,128]{3,2,1,0:T(8,128)(2,1)} %pack.1.same_ref, bf16[8,2,320,128]{3,2,1,0:T(8,128)(2,1)} %collective-permute-done.16.other_ref, ...), custom_call_target="tpu_custom_call" | custom-call | flops 1610612736 | bytes 6815744 | tf_op jit(solution)/shard_map/decode/pallas_call | solution.py:324
  237.3 5.9 %all-to-all-start.3 = ((bf16[16,448,128]{2,1,0:T(8,128)(2,1)}), bf16[16,448,128]{2,1,0:T(8,128)(2,1)}, u32[]{:S(2)}, u32[]{:S(2)}) async-start(bf16[16,448,128]{2,1,0:T(8,128)(2,1)} %decode.1), calls=%async_computation.3 | async-start | bytes 3670016 | tf_op jit(solution)/shard_map/all_to_all | solution.py:27
  243.3 3.9 %back.1 = (f32[2,128,128]{2,1,0:T(8,128)}, f32[2,128,128]{2,1,0:T(8,128)}) custom-call(s32[6]{0:T(128)} %and_select_fusion.1.place_ref, bf16[8,2,320,128]{3,2,1,0:T(8,128)(2,1)} %pack.1.same_ref, bf16[8,2,320,128]{3,2,1,0:T(8,128)(2,1)} %collective-permute-done.16.other_ref, bf16[128,128]{1,0:T(8,128)(2,1)} %convolution_convert_fusion.self_ref, ...), custom_call_target="tpu_custom_call" | custom-call | flops 50331648 | bytes 524288 | tf_op jit(solution)/shard_map/back/pallas_call | solution.py:419
  247.2 1.5 gather_fusion.3
  248.7 0.9 copy.57
  249.6 1.0 convert_reduce_fusion.1
  250.6 1.0 convert_reduce_fusion.2
  253.1 3.2 %fusion.28 = f32[7168,128]{1,0:T(8,128)S(1)} fusion(bf16[256,7168]{1,0:T(8,128)(2,1)} %bitcast.3, bf16[256,128]{1,0:T(8,128)(2,1)S(1)} %get-tuple-element.143), kind=kOutput, calls=%fused_computation.49 | convolution fusion | flops 469762048 | bytes 7405568 | tf_op jit(solution)/shard_map/dot_general | solution.py:598
  256.3 1.2 convolution_add_fusion.1
  257.6 2.5 fusion
  260.2 25.0 %all-to-all-done.3.y_ref = bf16[16,448,128]{2,1,0:T(8,128)(2,1)} async-done(((bf16[16,448,128]{2,1,0:T(8,128)(2,1)}), bf16[16,448,128]{2,1,0:T(8,128)(2,1)}, u32[]{:S(2)}, u32[]{:S(2)}) %all-to-all-start.3) | async-done | bytes 1835040 | tf_op jit(solution)/shard_map/all_to_all | solution.py:27
  285.1 2.0 copy-done.8
  287.2 3.1 %join_windows.1 = f32[128,7168]{1,0:T(8,128)} custom-call(f32[128,7168]{1,0:T(8,128)S(1)} %copy-done.8, bf16[16,448,128]{2,1,0:T(8,128)(2,1)} %all-to-all-done.3.y_ref), custom_call_target="tpu_custom_call" | custom-call | flops 917504 | bytes 7340032 | tf_op jit(solution)/shard_map/join_windows/pallas_call | solution.py:237
  (141 shorter events, 14.2 us)
Async XLA Ops:
  0.6 120.8 %copy-start = (bf16[1,7168,128]{2,1,0:T(8,128)(2,1)S(1)}, bf16[1,7168,128]{2,1,0:T(8,128)(2,1)}, u32[]{:S(2)}) copy-start(bf16[1,7168,128]{2,1,0:T(8,128)(2,1)} %param.7) | copy-start | bytes 5505028
  1.9 1.5 copy-start.10
  4.2 1.8 copy-start.9
  6.1 90.4 %all-to-all-start = ((bf16[8,2,16,7168]{3,2,1,0:T(8,128)(2,1)}), bf16[8,2,16,7168]{3,2,1,0:T(8,128)(2,1)}, u32[]{:S(2)}, u32[]{:S(2)}) async-start(bf16[8,2,16,7168]{3,2,1,0:T(8,128)(2,1)} %bitcast.133), calls=%async_computation | async-start | bytes 7340032 | tf_op jit(solution)/shard_map/all_to_all | solution.py:27
  11.2 82.0 %collective-permute-start = (bf16[8,16,7168]{2,1,0:T(8,128)(2,1)}, bf16[8,16,7168]{2,1,0:T(8,128)(2,1)}, u32[]{:S(2)}, u32[]{:S(2)}) collective-permute-start(bf16[8,16,7168]{2,1,0:T(8,128)(2,1)} %rows_ref.1), channel_id=1, source_target_pairs={{0,8},{1,9},{2,10},{3,11},{4,12},{5,13},{6,14},{7,15},{8,0},{9,1},... | collective-permute-start | bytes 5505032 | tf_op jit(solution)/shard_map/ppermute | solution.py:23
  96.5 7.0 %copy-start.21 = (s32[8,3]{0,1:T(4,128)S(1)}, s32[8,3]{0,1:T(4,128)}, u32[]{:S(2)}) copy-start(s32[8,3]{0,1:T(4,128)} %param.11) | copy-start | bytes 292
  96.5 55.4 %all-to-all-start.1 = ((bf16[16,128,512]{2,1,0:T(8,128)(2,1)}), bf16[16,128,512]{2,1,0:T(8,128)(2,1)}, u32[]{:S(2)}, u32[]{:S(2)}) async-start(bf16[16,128,512]{2,1,0:T(8,128)(2,1)} %cut_windows.1), calls=%async_computation.1 | async-start | bytes 4194304 | tf_op jit(solution)/shard_map/all_to_all | solution.py:27
  109.2 57.1 %copy-start.23 = (pred[160]{0:T(512)(128)(4,1)}, pred[160]{0:T(512)(128)(4,1)S(1)}, u32[]{:S(2)}) copy-start(pred[160]{0:T(512)(128)(4,1)S(1)} %broadcast_in_dim.119) | copy-start | bytes 484
  109.4 70.6 %copy-start.25 = (pred[96]{0:T(512)(128)(4,1)}, pred[96]{0:T(512)(128)(4,1)S(1)}, u32[]{:S(2)}) copy-start(pred[96]{0:T(512)(128)(4,1)S(1)} %broadcast_in_dim.122) | copy-start | bytes 292
  112.5 4.3 %copy-start.12 = (bf16[1,128,7168]{2,1,0:T(8,128)(2,1)S(1)}, bf16[1,128,7168]{2,1,0:T(8,128)(2,1)}, u32[]{:S(2)}) copy-start(bf16[1,128,7168]{2,1,0:T(8,128)(2,1)} %param.9) | copy-start | bytes 5505028
  112.5 4.3 %copy-start.18 = (f32[7168]{0:T(1024)S(1)}, f32[7168]{0:T(1024)}, u32[]{:S(2)}) copy-start(f32[7168]{0:T(1024)} %param.10) | copy-start | bytes 86020
  112.6 13.2 %collective-permute-start.1 = (bf16[2,16,7168]{2,1,0:T(8,128)(2,1)S(1)}, bf16[2,16,7168]{2,1,0:T(8,128)(2,1)S(1)}, u32[]{:S(2)}, u32[]{:S(2)}) collective-permute-start(bf16[2,16,7168]{2,1,0:T(8,128)(2,1)S(1)} %get-tuple-element.82), channel_id=1, source_target_pairs={{0,1},{1,0},{2,3},{3,2},{4,5},{5,4},{6,7},{7,6},{8,9},{9,8},{10,11... | collective-permute-start | bytes 1376264 | tf_op jit(solution)/shard_map/ppermute | solution.py:23
  113.0 17.9 %collective-permute-start.2 = (bf16[2,16,7168]{2,1,0:T(8,128)(2,1)}, bf16[2,16,7168]{2,1,0:T(8,128)(2,1)S(1)}, u32[]{:S(2)}, u32[]{:S(2)}) collective-permute-start(bf16[2,16,7168]{2,1,0:T(8,128)(2,1)} %get-tuple-element.83), channel_id=1, source_target_pairs={{0,2},{1,3},{2,0},{3,1},{4,6},{5,7},{6,4},{7,5},{8,10},{9,11},{10,... | collective-permute-start | bytes 1376264 | tf_op jit(solution)/shard_map/ppermute | solution.py:23
  113.3 33.2 %collective-permute-start.3 = (bf16[2,16,7168]{2,1,0:T(8,128)(2,1)}, bf16[2,16,7168]{2,1,0:T(8,128)(2,1)S(1)}, u32[]{:S(2)}, u32[]{:S(2)}) collective-permute-start(bf16[2,16,7168]{2,1,0:T(8,128)(2,1)} %get-tuple-element.84), channel_id=1, source_target_pairs={{0,3},{1,2},{2,1},{3,0},{4,7},{5,6},{6,5},{7,4},{8,11},{9,10},{10,... | collective-permute-start | bytes 1376264 | tf_op jit(solution)/shard_map/ppermute | solution.py:23
  114.8 34.3 %collective-permute-start.4 = (bf16[2,16,7168]{2,1,0:T(8,128)(2,1)}, bf16[2,16,7168]{2,1,0:T(8,128)(2,1)S(1)}, u32[]{:S(2)}, u32[]{:S(2)}) collective-permute-start(bf16[2,16,7168]{2,1,0:T(8,128)(2,1)} %get-tuple-element.85), channel_id=1, source_target_pairs={{0,4},{1,5},{2,6},{3,7},{4,0},{5,1},{6,2},{7,3},{8,12},{9,13},{10,... | collective-permute-start | bytes 1376264 | tf_op jit(solution)/shard_map/ppermute | solution.py:23
  115.1 54.1 %collective-permute-start.6 = (bf16[2,16,7168]{2,1,0:T(8,128)(2,1)}, bf16[2,16,7168]{2,1,0:T(8,128)(2,1)S(1)}, u32[]{:S(2)}, u32[]{:S(2)}) collective-permute-start(bf16[2,16,7168]{2,1,0:T(8,128)(2,1)} %get-tuple-element.94), channel_id=1, source_target_pairs={{0,5},{1,4},{2,7},{3,6},{4,1},{5,0},{6,3},{7,2},{8,13},{9,12},{10,... | collective-permute-start | bytes 1376264 | tf_op jit(solution)/shard_map/ppermute | solution.py:23
  117.8 3.3 %copy-start.11 = (bf16[8,16,7168]{2,1,0:T(8,128)(2,1)S(1)}, bf16[8,16,7168]{2,1,0:T(8,128)(2,1)}, u32[]{:S(2)}) copy-start(bf16[8,16,7168]{2,1,0:T(8,128)(2,1)} %rows_ref.1) | copy-start | bytes 5505028
  117.8 3.6 %copy-start.22 = (f32[1,128]{1,0:T(1,128)S(1)}, f32[1,128]{1,0:T(1,128)}, u32[]{:S(2)}) copy-start(f32[1,128]{1,0:T(1,128)} %param.8) | copy-start | bytes 1540
  125.8 43.4 %collective-permute-start.7 = (bf16[2,16,7168]{2,1,0:T(8,128)(2,1)}, bf16[2,16,7168]{2,1,0:T(8,128)(2,1)S(1)}, u32[]{:S(2)}, u32[]{:S(2)}) collective-permute-start(bf16[2,16,7168]{2,1,0:T(8,128)(2,1)} %get-tuple-element.95), channel_id=1, source_target_pairs={{0,6},{1,7},{2,4},{3,5},{4,2},{5,3},{6,0},{7,1},{8,14},{9,15},{10,... | collective-permute-start | bytes 1376264 | tf_op jit(solution)/shard_map/ppermute | solution.py:23
  130.9 47.4 %collective-permute-start.8 = (bf16[2,16,7168]{2,1,0:T(8,128)(2,1)}, bf16[2,16,7168]{2,1,0:T(8,128)(2,1)}, u32[]{:S(2)}, u32[]{:S(2)}) collective-permute-start(bf16[2,16,7168]{2,1,0:T(8,128)(2,1)} %get-tuple-element.96), channel_id=1, source_target_pairs={{0,7},{1,6},{2,5},{3,4},{4,3},{5,2},{6,1},{7,0},{8,15},{9,14},{10,... | collective-permute-start | bytes 1376264 | tf_op jit(solution)/shard_map/ppermute | solution.py:23
  150.5 1.4 copy-start.2
  157.1 3.2 %copy-start.13 = (bf16[1,128,7168]{2,1,0:T(8,128)(2,1)S(1)}, bf16[1,128,7168]{2,1,0:T(8,128)(2,1)}, u32[]{:S(2)}) copy-start(bf16[1,128,7168]{2,1,0:T(8,128)(2,1)} %param.9) | copy-start | bytes 5505028
  159.0 8.7 %collective-permute-start.5 = (bf16[8,2,2,128,128]{4,3,2,1,0:T(8,128)(2,1)S(1)}, bf16[8,2,2,128,128]{4,3,2,1,0:T(8,128)(2,1)S(1)}, u32[]{:S(2)}, u32[]{:S(2)}) collective-permute-start(bf16[8,2,2,128,128]{4,3,2,1,0:T(8,128)(2,1)S(1)} %bitcast.154), channel_id=1, source_target_pairs={{0,1},{1,0},{2,3},{3,2},{4,5},{5,4},{6,7},{7,6},{8,9},{9,8},{10,11... | collective-permute-start | bytes 3145736 | tf_op jit(solution)/shard_map/ppermute | solution.py:23
  161.6 4.7 %copy-start.3 = (bf16[5,2,16,7168]{3,2,1,0:T(8,128)(2,1)S(1)}, bf16[5,2,16,7168]{3,2,1,0:T(8,128)(2,1)}, u32[]{:S(2)}) copy-start(bf16[5,2,16,7168]{3,2,1,0:T(8,128)(2,1)} %copy-done.2) | copy-start | bytes 6881284
  179.9 1.2 copy-start.5
  181.6 11.7 %copy-start.27 = (f32[128]{0:T(128)S(1)}, f32[128]{0:T(128)}, u32[]{:S(2)}) copy-start(f32[128]{0:T(128)} %get-tuple-element.156) | copy-start | bytes 1540
  182.1 11.3 %collective-permute-start.9 = (bf16[2,320,128]{2,1,0:T(8,128)(2,1)S(1)}, bf16[2,320,128]{2,1,0:T(8,128)(2,1)S(1)}, u32[]{:S(2)}, u32[]{:S(2)}) collective-permute-start(bf16[2,320,128]{2,1,0:T(8,128)(2,1)S(1)} %bitcast.134), channel_id=1, source_target_pairs={{0,8},{1,9},{2,10},{3,11},{4,12},{5,13},{6,14},{7,15},{8,0},{9,1},... | collective-permute-start | bytes 491528 | tf_op jit(solution)/shard_map/ppermute | solution.py:23
  184.3 19.1 %collective-permute-start.10 = (bf16[2,320,128]{2,1,0:T(8,128)(2,1)S(1)}, bf16[2,320,128]{2,1,0:T(8,128)(2,1)S(1)}, u32[]{:S(2)}, u32[]{:S(2)}) collective-permute-start(bf16[2,320,128]{2,1,0:T(8,128)(2,1)S(1)} %bitcast.135), channel_id=1, source_target_pairs={{0,2},{1,3},{2,0},{3,1},{4,6},{5,7},{6,4},{7,5},{8,10},{9,11},{10,... | collective-permute-start | bytes 491528 | tf_op jit(solution)/shard_map/ppermute | solution.py:23
  185.3 21.1 %collective-permute-start.11 = (bf16[2,320,128]{2,1,0:T(8,128)(2,1)S(1)}, bf16[2,320,128]{2,1,0:T(8,128)(2,1)S(1)}, u32[]{:S(2)}, u32[]{:S(2)}) collective-permute-start(bf16[2,320,128]{2,1,0:T(8,128)(2,1)S(1)} %bitcast.136), channel_id=1, source_target_pairs={{0,4},{1,5},{2,6},{3,7},{4,0},{5,1},{6,2},{7,3},{8,12},{9,13},{10,... | collective-permute-start | bytes 491528 | tf_op jit(solution)/shard_map/ppermute | solution.py:23
  186.8 19.5 %collective-permute-start.12 = (bf16[2,320,128]{2,1,0:T(8,128)(2,1)S(1)}, bf16[2,320,128]{2,1,0:T(8,128)(2,1)S(1)}, u32[]{:S(2)}, u32[]{:S(2)}) collective-permute-start(bf16[2,320,128]{2,1,0:T(8,128)(2,1)S(1)} %bitcast.137), channel_id=1, source_target_pairs={{0,6},{1,7},{2,4},{3,5},{4,2},{5,3},{6,0},{7,1},{8,14},{9,15},{10,... | collective-permute-start | bytes 491528 | tf_op jit(solution)/shard_map/ppermute | solution.py:23
  187.0 40.9 %all-to-all-start.2 = ((bf16[8,2,2,128,128]{4,3,2,1,0:T(8,128)(2,1)}), bf16[8,2,2,128,128]{4,3,2,1,0:T(8,128)(2,1)}, u32[]{:S(2)}, u32[]{:S(2)}) async-start(bf16[8,2,2,128,128]{4,3,2,1,0:T(8,128)(2,1)} %fusion.2), calls=%async_computation.2 | async-start | bytes 2097152 | tf_op jit(solution)/shard_map/all_to_all | solution.py:27
  193.4 3.2 %copy-start.4 = (bf16[5,2,16,7168]{3,2,1,0:T(8,128)(2,1)S(1)}, bf16[5,2,16,7168]{3,2,1,0:T(8,128)(2,1)}, u32[]{:S(2)}) copy-start(bf16[5,2,16,7168]{3,2,1,0:T(8,128)(2,1)} %copy-done.2) | copy-start | bytes 6881284
  193.4 16.5 %collective-permute-start.13 = (bf16[2,320,128]{2,1,0:T(8,128)(2,1)S(1)}, bf16[2,320,128]{2,1,0:T(8,128)(2,1)S(1)}, u32[]{:S(2)}, u32[]{:S(2)}) collective-permute-start(bf16[2,320,128]{2,1,0:T(8,128)(2,1)S(1)} %collective-permute-done.9.refs_4_), channel_id=1, source_target_pairs={{0,2},{1,3},{2,0},{3,1},{4,6},{5,7},{6,4},{7,5},{8,10},{9,11},{10,... | collective-permute-start | bytes 491528 | tf_op jit(solution)/shard_map/ppermute | solution.py:23
  193.8 23.5 %collective-permute-start.14 = (bf16[2,320,128]{2,1,0:T(8,128)(2,1)S(1)}, bf16[2,320,128]{2,1,0:T(8,128)(2,1)S(1)}, u32[]{:S(2)}, u32[]{:S(2)}) collective-permute-start(bf16[2,320,128]{2,1,0:T(8,128)(2,1)S(1)} %collective-permute-done.9.refs_4_), channel_id=1, source_target_pairs={{0,4},{1,5},{2,6},{3,7},{4,0},{5,1},{6,2},{7,3},{8,12},{9,13},{10,... | collective-permute-start | bytes 491528 | tf_op jit(solution)/shard_map/ppermute | solution.py:23
  196.6 0.7 copy-start.30
  196.6 0.9 copy-start.29
  196.6 2.0 copy-start.15
  197.3 2.1 copy-start.14
  197.3 2.1 copy-start.19
  202.6 2.4 copy-start.6
  203.4 19.2 %collective-permute-start.15 = (bf16[2,320,128]{2,1,0:T(8,128)(2,1)S(1)}, bf16[2,320,128]{2,1,0:T(8,128)(2,1)S(1)}, u32[]{:S(2)}, u32[]{:S(2)}) collective-permute-start(bf16[2,320,128]{2,1,0:T(8,128)(2,1)S(1)} %collective-permute-done.9.refs_4_), channel_id=1, source_target_pairs={{0,6},{1,7},{2,4},{3,5},{4,2},{5,3},{6,0},{7,1},{8,14},{9,15},{10,... | collective-permute-start | bytes 491528 | tf_op jit(solution)/shard_map/ppermute | solution.py:23
  223.8 4.0 %collective-permute-start.16 = (bf16[8,2,320,128]{3,2,1,0:T(8,128)(2,1)}, bf16[8,2,320,128]{3,2,1,0:T(8,128)(2,1)}, u32[]{:S(2)}, u32[]{:S(2)}) collective-permute-start(bf16[8,2,320,128]{3,2,1,0:T(8,128)(2,1)} %pack.1.same_ref), channel_id=1, source_target_pairs={{0,1},{1,0},{2,3},{3,2},{4,5},{5,4},{6,7},{7,6},{8,9},{9,8},{10,11... | collective-permute-start | bytes 3932168 | tf_op jit(solution)/shard_map/ppermute | solution.py:23
  237.3 5.9 %copy-start.28 = (s32[8]{0:T(128)S(1)}, s32[8]{0:T(128)}, u32[]{:S(2)}) copy-start(s32[8]{0:T(128)} %get-tuple-element.169) | copy-start | bytes 100
  237.3 47.8 %all-to-all-start.3 = ((bf16[16,448,128]{2,1,0:T(8,128)(2,1)}), bf16[16,448,128]{2,1,0:T(8,128)(2,1)}, u32[]{:S(2)}, u32[]{:S(2)}) async-start(bf16[16,448,128]{2,1,0:T(8,128)(2,1)} %decode.1), calls=%async_computation.3 | async-start | bytes 3670016 | tf_op jit(solution)/shard_map/all_to_all | solution.py:27
  243.2 8.3 %copy-start.20 = (f32[96,128]{1,0:T(8,128)S(1)}, f32[96,128]{1,0:T(8,128)}, u32[]{:S(2)}) copy-start(f32[96,128]{1,0:T(8,128)} %fusion.74) | copy-start | bytes 147460
  243.2 8.3 %copy-start.26 = (pred[96]{0:T(512)(128)(4,1)S(1)}, pred[96]{0:T(512)(128)(4,1)}, u32[]{:S(2)}) copy-start(pred[96]{0:T(512)(128)(4,1)} %copy-done.25) | copy-start | bytes 292
  243.2 8.4 %copy-start.17 = (f32[160,128]{1,0:T(8,128)S(1)}, f32[160,128]{1,0:T(8,128)}, u32[]{:S(2)}) copy-start(f32[160,128]{1,0:T(8,128)} %get-tuple-element.128) | copy-start | bytes 245764
  243.2 8.4 %copy-start.24 = (pred[160]{0:T(512)(128)(4,1)S(1)}, pred[160]{0:T(512)(128)(4,1)}, u32[]{:S(2)}) copy-start(pred[160]{0:T(512)(128)(4,1)} %copy-done.23) | copy-start | bytes 484
  243.3 8.5 %copy-start.16 = (f32[256,128]{1,0:T(8,128)S(1)}, f32[256,128]{1,0:T(8,128)}, u32[]{:S(2)}) copy-start(f32[256,128]{1,0:T(8,128)} %get-tuple-element.166) | copy-start | bytes 393220
  256.3 1.3 copy-start.7
  285.1 2.0 copy-start.8
  287.2 3.2 %copy-start.1 = (bf16[1,7168,128]{2,1,0:T(8,128)(2,1)S(1)}, bf16[1,7168,128]{2,1,0:T(8,128)(2,1)}, u32[]{:S(2)}) copy-start(bf16[1,7168,128]{2,1,0:T(8,128)(2,1)} %param.7) | copy-start | bytes 5505028
